TPU v7x, 32 devices: a whole 2x2x4 slice. The times are simulated.
32 devices in a mesh: strip: 4 (over y, x), req: 8 (over z, core).
Axes of the slice: x: 2, y: 2, z: 4, core: 2. Of those that a mesh axis runs over, the one named last changes fastest.
Arguments:
- hidden_states: bfloat16 [2, 16, 16, 2, 14, 640], P(None, 'req', 'strip'), may hold values from -20 to 20
- gate: int32 [16], P('req'), may hold values from 0 to 1, as said below
- context_slot: int32 [16], replicated, may hold values from 0 to 15, as said below
- context_pages: bfloat16 [2, 16, 77, 640], P(None, 'req'), may hold values from -800 to 800
- conv_weight: bfloat16 [3, 3, 640, 640], replicated, may hold values from -0.078125 to 0.078125
- conv_bias: float32 [640], replicated, may hold values from -4 to 4
- conv_gain: float32 [640], replicated, may hold values from 0.25 to 1.75
- temporal_gain: float32 [640], replicated, may hold values from 0.25 to 1.75
- temporal_query: bfloat16 [640, 640], replicated, may hold values from -18 to 18
- temporal_key: bfloat16 [640, 640], replicated, may hold values from -0.25 to 0.25
- temporal_value: bfloat16 [640, 640], replicated, may hold values from -0.25 to 0.25
- temporal_out: bfloat16 [640, 640], replicated, may hold values from -0.25 to 0.25
- cross_gain: float32 [640], replicated, may hold values from 0.25 to 1.75
- cross_query: bfloat16 [640, 640], replicated, may hold values from -0.25 to 0.25
- cross_out: bfloat16 [640, 640], replicated, may hold values from -0.25 to 0.25
Outputs:
- guided: bfloat16 [16, 16, 2, 14, 640], P('req', 'strip')
Inputs may be any that keep to these rules, and one draw needn't show every extreme that they name: Requests 2 * i to 2 * i + 1 lie on req device i. Devices i and i + 4 form a pair, and of the 4 requests of a pair exactly 2 have gate 1. `context_slot`: A permutation of the 16 pages; page p lies on req device p // 2, and the page of a request lies on the request's own device or on the other device of its pair.
All inputs are finite; a program needn't handle non-finite values.
Results may differ from a plain program's by a relative error of at most 0.012.
Values may be sent and summed in bfloat16 or wider, within the bound.
No kernel may reach another device: no remote copies, remote signals or barrier semaphores. Data moves between devices by JAX's collectives and lax.ppermute only.
A program may use at most 64 MiB of HBM per device.

v0:
```python
import jax
import jax.numpy as jnp
from jax import lax
from jax.sharding import PartitionSpec as P

HEAD_DIM = 64
REQ_DEV = 2


EPSILON = 1e-06


def padded_2(block, sides, width):
    for axis, dim in sides:
        count = lax.axis_size(axis)
        forward = [(i, i + 1) for i in range(count - 1)]
        backward = [(target, source) for source, target in forward]
        low = lax.ppermute(
            lax.slice_in_dim(block, block.shape[dim] - width, None, axis=dim), axis, forward
        )
        high = lax.ppermute(lax.slice_in_dim(block, 0, width, axis=dim), axis, backward)
        block = jnp.concatenate([low, block, high], axis=dim)
    return block


def partner(value, axis, bit):
    mask = 2**bit
    pairs = [(source, source ^ mask) for source in range(lax.axis_size(axis))]
    return lax.ppermute(value, axis, pairs)


def rms_norm(field, scale_gain):
    field = field.astype(jnp.float32)
    return field * lax.rsqrt(jnp.mean(field * field, axis=-1, keepdims=True) + EPSILON) * scale_gain


def project(field, weight):
    return jnp.dot(field, weight, preferred_element_type=jnp.float32)


def cross_attend(queries, key_page, value_page):
    count, positions, width = queries.shape
    heads = width // HEAD_DIM
    query_heads = queries.reshape(count, positions, heads, HEAD_DIM)
    key_heads = key_page.reshape(count, key_page.shape[1], heads, HEAD_DIM)
    value_heads = value_page.reshape(count, value_page.shape[1], heads, HEAD_DIM)
    scores = (
        jnp.einsum("rphd,rchd->rhpc", query_heads, key_heads, preferred_element_type=jnp.float32)
        * 0.125
    )
    attn_weights = jax.nn.softmax(scores, axis=-1).astype(jnp.bfloat16)
    attended = jnp.einsum(
        "rhpc,rchd->rphd", attn_weights, value_heads, preferred_element_type=jnp.float32
    )
    return attended.astype(jnp.bfloat16).reshape(count, positions, width)


def pick_pages(pages, page_ids, wanted):
    selector = (wanted[:, None] == page_ids[None, :]).astype(jnp.bfloat16)
    chosen = jnp.einsum("rk,vkcd->vrcd", selector, pages, preferred_element_type=jnp.float32)
    return chosen.astype(jnp.bfloat16)


def block(states, weights, cross_mixer):
    (
        conv_weight,
        conv_bias,
        conv_gain,
        temporal_gain,
        temporal_query,
        temporal_key,
        temporal_value,
        temporal_out,
        cross_gain,
        cross_query,
        cross_out,
    ) = weights
    slots, rows, cols, frames, width = states.shape
    heads = width // HEAD_DIM
    activated = jax.nn.silu(rms_norm(states, conv_gain)).astype(jnp.bfloat16)
    with_rows = padded_2(activated, (("strip", 1),), 1)
    padded = jnp.pad(with_rows, ((0, 0), (0, 0), (1, 1), (0, 0), (0, 0)))
    conv_sum = jnp.zeros(states.shape, jnp.float32) + conv_bias
    for row_step in range(3):
        for col_step in range(3):
            window = padded[:, row_step : row_step + rows, col_step : col_step + cols]
            conv_sum = conv_sum + project(window, conv_weight[row_step, col_step])
    after_conv = states.astype(jnp.float32) + conv_sum
    normed = rms_norm(after_conv, temporal_gain).astype(jnp.bfloat16)
    head_shape = (slots, rows, cols, frames, heads, HEAD_DIM)
    time_query = project(normed, temporal_query).astype(jnp.bfloat16).reshape(head_shape)
    time_key = project(normed, temporal_key).astype(jnp.bfloat16).reshape(head_shape)
    time_value = project(normed, temporal_value).astype(jnp.bfloat16).reshape(head_shape)
    scores = (
        jnp.einsum(
            "srwfhd,srwghd->srwhfg", time_query, time_key, preferred_element_type=jnp.float32
        )
        * 0.125
    )
    time_weights = jax.nn.softmax(scores, axis=-1).astype(jnp.bfloat16)
    time_mixed = jnp.einsum(
        "srwhfg,srwghd->srwfhd", time_weights, time_value, preferred_element_type=jnp.float32
    )
    time_mixed = time_mixed.astype(jnp.bfloat16).reshape(states.shape)
    after_time = after_conv + project(time_mixed, temporal_out)
    normed_cross = rms_norm(after_time[:REQ_DEV], cross_gain).astype(jnp.bfloat16)
    queries = (
        project(normed_cross, cross_query)
        .astype(jnp.bfloat16)
        .reshape(REQ_DEV, rows * cols * frames, width)
    )
    cross_mixed = cross_mixer(queries).reshape((REQ_DEV, rows, cols, frames, width))
    after_cross = after_time[:REQ_DEV] + project(cross_mixed, cross_out)
    return jnp.concatenate([after_cross, after_time[REQ_DEV:]], axis=0).astype(jnp.bfloat16)


def on_device(
    hidden_states,
    gate,
    context_slot,
    context_pages,
    conv_weight,
    conv_bias,
    conv_gain,
    temporal_gain,
    temporal_query,
    temporal_key,
    temporal_value,
    temporal_out,
    cross_gain,
    cross_query,
    cross_out,
):
    weights = (
        conv_weight,
        conv_bias,
        conv_gain,
        temporal_gain,
        temporal_query,
        temporal_key,
        temporal_value,
        temporal_out,
        cross_gain,
        cross_query,
        cross_out,
    )
    top_bit = lax.axis_size("req").bit_length() - 2
    device_index = lax.axis_index("req")
    partner_index = jnp.bitwise_xor(device_index, lax.axis_size("req") // 2)
    own_ids = device_index * REQ_DEV + jnp.arange(REQ_DEV, dtype=jnp.int32)
    wanted = lax.dynamic_slice_in_dim(context_slot, device_index * REQ_DEV, REQ_DEV)

    def cross_mixer(queries):
        far_pages = partner(context_pages, "req", top_bit)
        candidates = jnp.concatenate([context_pages, far_pages], axis=1)
        partner_ids = partner_index * REQ_DEV + jnp.arange(REQ_DEV, dtype=jnp.int32)
        page_ids = jnp.concatenate([own_ids, partner_ids])
        chosen = pick_pages(candidates, page_ids, wanted)
        return cross_attend(queries, chosen[0], chosen[1])

    outputs = block(
        hidden_states.reshape((2 * REQ_DEV,) + hidden_states.shape[2:]), weights, cross_mixer
    )
    unconditioned = outputs[REQ_DEV:]
    conditioned = outputs[:REQ_DEV]
    frames = hidden_states.shape[4]
    frame_scale = (1.0 + 2.0 * jnp.arange(frames, dtype=jnp.float32) / (frames - 1)).reshape(
        1, 1, 1, frames, 1
    )
    cond_wide = conditioned.astype(jnp.float32)
    uncond_wide = unconditioned.astype(jnp.float32)
    mixed_out = uncond_wide + frame_scale * (cond_wide - uncond_wide)
    guided = jnp.where((gate == 1)[:, None, None, None, None], mixed_out, cond_wide)
    return guided.astype(jnp.bfloat16)


def solution(mesh):
    return jax.shard_map(
        on_device,
        mesh=mesh,
        in_specs=(
            P(None, "req", "strip", None, None, None),
            P("req"),
            P(),
            P(None, "req", None, None),
            P(),
            P(),
            P(),
            P(),
            P(),
            P(),
            P(),
            P(),
            P(),
            P(),
            P(),
        ),
        out_specs=P("req", "strip", None, None, None),
        check_vma=False,
    )
```

profile of v0, /device:TPU:0, one launch (start us, length us, event | category | flops | bytes accessed | tf_op | source)
XLA Modules:
  0.0 86.6 jit_solution(3794621560146206105)
XLA Ops:
  4.4 4.9 %collective-permute-start = (bf16[4,1,2,14,640]{4,1,3,2,0:T(2,128)(2,1)}, bf16[4,1,2,14,640]{4,1,3,2,0:T(2,128)(2,1)S(1)}, u32[]{:S(2)}, u32[]{:S(2)}) collective-permute-start(bf16[4,1,2,14,640]{4,1,3,2,0:T(2,128)(2,1)} %get-tuple-element.13), channel_id=1, source_target_pairs={{0,8},{8,16},{16,24},{1,9},{9,17},{17,25},{2,10},{10,18},{18,26},{... | collective-permute-start | bytes 430088 | tf_op jit(solution)/shard_map/ppermute | solution.py:18
  9.2 1.5 %collective-permute-start.1 = (bf16[4,1,2,14,640]{4,1,3,2,0:T(2,128)(2,1)}, bf16[4,1,2,14,640]{4,1,3,2,0:T(2,128)(2,1)}, u32[]{:S(2)}, u32[]{:S(2)}) collective-permute-start(bf16[4,1,2,14,640]{4,1,3,2,0:T(2,128)(2,1)} %get-tuple-element.14), channel_id=1, source_target_pairs={{8,0},{16,8},{24,16},{9,1},{17,9},{25,17},{10,2},{18,10},{26,18},{... | collective-permute-start | bytes 430088 | tf_op jit(solution)/shard_map/ppermute | solution.py:21
  10.7 2.7 %collective-permute-start.2 = (bf16[2,2,77,640]{3,1,2,0:T(2,128)(2,1)}, bf16[2,2,77,640]{3,1,2,0:T(2,128)(2,1)}, u32[]{:S(2)}, u32[]{:S(2)}) collective-permute-start(bf16[2,2,77,640]{3,1,2,0:T(2,128)(2,1)} %param.18), channel_id=1, source_target_pairs={{0,4},{1,5},{2,6},{3,7},{4,0},{5,1},{6,2},{7,3},{8,12},{9,13},{10,... | collective-permute-start | bytes 1182728 | tf_op jit(solution)/shard_map/ppermute | solution.py:29
  13.4 2.2 %fusion.24 = bf16[2,2,4,2,14,640]{5,3,4,2,1,0:T(2,128)(2,1)} fusion(bf16[2,2,4,2,14,640]{5,3,4,2,1,0:T(2,128)(2,1)S(1)} %copy-done.1, f32[640]{0:T(1024)S(1)} %copy-done.7, f32[2,2,4,2,14]{3,4,2,1,0:T(8,128)S(1)} %add_rsqrt_fusion), kind=kLoop, calls=%fused_computation.52 | loop fusion | flops 2293760 | bytes 1151232 | tf_op jit(solution)/shard_map/convert_element_type | solution.py:80
  15.6 3.1 %fusion.41 = f32[4,4,2,14,640]{4,3,2,1,0:T(8,128)} fusion(bf16[3,3,640,640]{3,2,1,0:T(8,128)(2,1)} %param.19, bf16[4,4,2,14,640]{4,2,3,1,0:T(2,128)(2,1)} %bitcast.124), kind=kOutput, calls=%fused_computation.69 | convolution fusion | flops 367001600 | bytes 2539520 | tf_op jit(solution)/shard_map/dot_general | solution.py:38
  18.9 4.8 %collective-permute-done.1 = bf16[4,1,2,14,640]{4,1,3,2,0:T(2,128)(2,1)} collective-permute-done((bf16[4,1,2,14,640]{4,1,3,2,0:T(2,128)(2,1)}, bf16[4,1,2,14,640]{4,1,3,2,0:T(2,128)(2,1)}, u32[]{:S(2)}, u32[]{:S(2)}) %collective-permute-start.1) | collective-permute-done | bytes 143392 | tf_op jit(solution)/shard_map/ppermute | solution.py:21
  23.7 2.1 %fusion.10 = bf16[4,6,4,14,640]{4,1,3,2,0:T(8,128)(2,1)S(1)} fusion(bf16[4,1,2,14,640]{4,1,3,2,0:T(2,128)(2,1)} %collective-permute-done.1, bf16[4,4,2,14,640]{4,1,3,2,0:T(4,128)(2,1)S(1)} %fusion.23, bf16[4,1,2,14,640]{4,1,3,2,0:T(2,128)(2,1)S(1)} %collective-permute-done), kind=kLoop, calls=%fused_computation.13 | loop fusion | flops 10321920 | bytes 2580480 | tf_op jit(solution)/shard_map/concatenate | solution.py:22
  27.0 1.9 %fusion.33 = f32[4,4,2,14,640]{4,3,2,1,0:T(8,128)S(1)} fusion(bf16[3,3,640,640]{3,2,1,0:T(8,128)(2,1)} %param.19, bf16[4,4,2,14,640]{4,1,3,2,0:T(4,128)(2,1)S(1)} %get-tuple-element.10), kind=kOutput, calls=%fused_computation.61 | convolution fusion | flops 367001600 | bytes 2539520 | tf_op jit(solution)/shard_map/dot_general | solution.py:38
  28.9 1.9 %fusion.37 = f32[4,4,2,14,640]{4,3,2,1,0:T(8,128)S(1)} fusion(bf16[3,3,640,640]{3,2,1,0:T(8,128)(2,1)} %param.19, bf16[4,4,2,14,640]{4,1,3,2,0:T(4,128)(2,1)S(1)} %get-tuple-element.6), kind=kOutput, calls=%fused_computation.65 | convolution fusion | flops 367001600 | bytes 2539520 | tf_op jit(solution)/shard_map/dot_general | solution.py:38
  33.9 2.2 %pad_maximum_fusion.3 = (bf16[4,4,2,14,640]{4,1,3,2,0:T(4,128)(2,1)S(1)}, bf16[4,4,2,14,640]{4,1,3,2,0:T(4,128)(2,1)S(1)}) fusion(bf16[4,4,2,14,640]{4,1,3,2,0:T(4,128)(2,1)S(1)} %fusion.23, bf16[4,1,2,14,640]{4,1,3,2,0:T(2,128)(2,1)S(1)} %collective-permute-done, bf16[4,1,2,14,640]{4,1,3,2,0:T(2,128)(2,1)} %collective-permute-done.1), kind=kLoop, calls=%fused_computation.110 | loop fusion | flops 2293760 | bytes 2007040 | tf_op jit(solution)/shard_map/concatenate | solution.py:22
  38.2 6.6 %bitcast_add_fusion = f32[4,4,2,14,640]{4,1,3,2,0:T(4,128)S(1)} fusion(f32[2,2,4,2,14,640]{5,2,4,3,1,0:T(4,128)S(1)} %copy.90, f32[4,4,2,14,640]{4,3,2,1,0:T(8,128)S(1)} %fusion.33, f32[4,4,2,14,640]{4,3,2,1,0:T(8,128)S(1)} %fusion.35, f32[4,4,2,14,640]{4,3,2,1,0:T(8,128)S(1)} %fusion.37, f32[4,4,2,14,640]{4,3,2,1,0:T(8,128)S(1)} %fusion.39, ...), kind=kLoop, calls=%fused_computation.35 | loop fusion | flops 2867200 | bytes 12618240 | tf_op jit(solution)/shard_map/add | solution.py:88
  47.4 2.0 %reshape.89 = bf16[4,4,2,14,10,64]{5,4,3,2,1,0:T(8,128)(2,1)} reshape(bf16[4,4,2,14,640]{4,3,2,1,0:T(8,128)(2,1)S(1)} %convolution_convert_fusion.2) | data formatting | bytes 1146880 | tf_op jit(solution)/shard_map/reshape | solution.py:91
  49.4 2.1 %convolution_convert_fusion.1 = bf16[4,4,2,14,640]{4,3,2,1,0:T(8,128)(2,1)S(1)} fusion(bf16[640,640]{1,0:T(8,128)(2,1)} %param.24, bf16[4,4,2,14,640]{4,1,3,2,0:T(4,128)(2,1)} %copy-done.5), kind=kOutput, calls=%fused_computation.17 | convolution fusion | flops 367288320 | bytes 1966080 | tf_op jit(solution)/shard_map/dot_general | solution.py:38
  51.5 2.0 %reshape.90 = bf16[4,4,2,14,10,64]{5,4,3,2,1,0:T(8,128)(2,1)} reshape(bf16[4,4,2,14,640]{4,3,2,1,0:T(8,128)(2,1)S(1)} %convolution_convert_fusion.1) | data formatting | bytes 1146880 | tf_op jit(solution)/shard_map/reshape | solution.py:92
  53.5 2.9 %fusion.13 = f32[4,4,2,10,14,14]{4,5,3,2,1,0:T(8,128)S(1)} fusion(bf16[4,4,2,14,10,64]{5,4,3,2,1,0:T(8,128)(2,1)} %reshape.90, bf16[4,4,2,14,10,64]{5,4,3,2,1,0:T(8,128)(2,1)} %reshape.89), kind=kOutput, calls=%fused_computation.20 | convolution fusion | flops 8028160 | bytes 1397760 | tf_op jit(solution)/shard_map/srwfhd,srwghd->srwhfg/dot_general | solution.py:95
  56.4 2.5 %fusion.89 = (f32[4,4,2,10,14]{4,3,2,1,0:T(8,128)S(1)}, f32[4,4,2,10,14,14]{4,5,3,2,1,0:T(8,128)}) fusion(f32[4,4,2,10,14,14]{4,5,3,2,1,0:T(8,128)S(1)} %fusion.13), kind=kOutput, calls=%fused_computation.136 | output fusion | flops 250893 | bytes 519680 | tf_op jit(solution)/shard_map/sub | solution.py:100
  59.7 2.0 %reshape.88 = bf16[4,4,2,14,10,64]{5,4,3,2,1,0:T(8,128)(2,1)} reshape(bf16[4,4,2,14,640]{4,3,2,1,0:T(8,128)(2,1)S(1)} %convolution_convert_fusion.3) | data formatting | bytes 1146880 | tf_op jit(solution)/shard_map/reshape | solution.py:93
  61.7 3.0 %fusion.11 = bf16[4,4,2,14,10,64]{5,3,4,2,1,0:T(8,128)(2,1)S(1)} fusion(f32[4,4,2,10,14,14]{4,5,3,2,1,0:T(8,128)} %get-tuple-element.18, bf16[4,4,2,14,10,64]{5,4,3,2,1,0:T(8,128)(2,1)} %reshape.88, f32[4,4,2,10,14]{4,3,2,1,0:T(8,128)S(1)} %get-tuple-element.17), kind=kOutput, calls=%fused_computation.15 | convolution fusion | flops 8440320 | bytes 1415680 | tf_op jit(solution)/shard_map/srwhfg,srwghd->srwfhd/dot_general | solution.py:101
  64.7 1.7 %copy.157 = bf16[4,4,2,14,10,64]{5,4,3,2,1,0:T(8,128)(2,1)} copy(bf16[4,4,2,14,10,64]{5,3,4,2,1,0:T(8,128)(2,1)S(1)} %fusion.11) | data formatting | bytes 1146880 | tf_op jit(solution)/shard_map/reshape | solution.py:104
  66.4 3.0 %reshape.91 = bf16[4,4,2,14,640]{4,3,2,1,0:T(8,128)(2,1)S(1)} reshape(bf16[4,4,2,14,10,64]{5,4,3,2,1,0:T(8,128)(2,1)} %copy.157) | data formatting | bytes 1146880 | tf_op jit(solution)/shard_map/reshape | solution.py:104
  69.4 1.9 %fusion.28 = f32[4,4,2,14,640]{4,3,2,1,0:T(8,128)S(1)} fusion(bf16[4,4,2,14,640]{4,3,2,1,0:T(8,128)(2,1)S(1)} %reshape.91, bf16[640,640]{1,0:T(8,128)(2,1)} %param.26), kind=kOutput, calls=%fused_computation.56 | convolution fusion | flops 367001600 | bytes 2539520 | tf_op jit(solution)/shard_map/dot_general | solution.py:38
  74.4 2.1 %fusion.20 = bf16[2,2,77,640]{3,1,2,0:T(2,128)(2,1)S(1)} fusion(bf16[2,2,77,640]{3,1,2,0:T(2,128)(2,1)} %collective-permute-done.2, bf16[2,2,77,640]{3,1,2,0:T(2,128)(2,1)} %param.18, s32[4]{0:T(128)S(1)} %pad_add_fusion, s32[2]{0:T(128)S(1)} %dynamic_slice.3), kind=kOutput, calls=%fused_computation.31 | convolution fusion | flops 3351048 | bytes 1182744 | tf_op jit(solution)/shard_map/rk,vkcd->vrcd/dot_general | solution.py:60
  80.5 1.7 %fusion.21 = bf16[2,112,10,64]{1,3,2,0:T(8,128)(2,1)S(1)} fusion(bf16[2,77,10,64]{1,3,2,0:T(8,128)(2,1)S(1)} %bitcast.125, f32[2,10,112]{2,1,0:T(8,128)S(1)} %fusion.90, f32[2,10,112,77]{2,3,1,0:T(8,128)} %copy-done.4), kind=kOutput, calls=%fused_computation.32 | convolution fusion | flops 22740556 | bytes 1182720 | tf_op jit(solution)/shard_map/rhpc,rchd->rphd/dot_general | solution.py:52
  83.5 1.6 %fusion.25 = f32[2,4,2,14,640]{4,3,2,1,0:T(8,128)S(1)} fusion(bf16[2,4,2,14,640]{4,3,2,1,0:T(8,128)(2,1)S(1)} %reshape.93, bf16[640,640]{1,0:T(8,128)(2,1)} %param.29), kind=kOutput, calls=%fused_computation.53 | convolution fusion | flops 183500800 | bytes 1679360 | tf_op jit(solution)/shard_map/dot_general | solution.py:38
  (74 shorter events, 23.9 us)
Async XLA Ops:
  0.0 46.6 %copy-start = (bf16[640,640]{1,0:T(8,128)(2,1)S(1)}, bf16[640,640]{1,0:T(8,128)(2,1)}, u32[]{:S(2)}) copy-start(bf16[640,640]{1,0:T(8,128)(2,1)} %param.23) | copy-start | bytes 2457604
  0.0 1.4 %copy-start.1 = (bf16[2,2,4,2,14,640]{5,3,4,2,1,0:T(2,128)(2,1)S(1)}, bf16[2,2,4,2,14,640]{5,3,4,2,1,0:T(2,128)(2,1)}, u32[]{:S(2)}) copy-start(bf16[2,2,4,2,14,640]{5,3,4,2,1,0:T(2,128)(2,1)} %param.15) | copy-start | bytes 1720324
  0.0 2.4 %copy-start.7 = (f32[640]{0:T(1024)S(1)}, f32[640]{0:T(1024)}, u32[]{:S(2)}) copy-start(f32[640]{0:T(1024)} %param.21) | copy-start | bytes 7684
  3.1 12.4 %copy-start.12 = (s32[2]{0:T(128)S(1)}, s32[2]{0:T(128)}, u32[]{:S(2)}) copy-start(s32[2]{0:T(128)} %param.16) | copy-start | bytes 28
  4.4 14.5 %collective-permute-start = (bf16[4,1,2,14,640]{4,1,3,2,0:T(2,128)(2,1)}, bf16[4,1,2,14,640]{4,1,3,2,0:T(2,128)(2,1)S(1)}, u32[]{:S(2)}, u32[]{:S(2)}) collective-permute-start(bf16[4,1,2,14,640]{4,1,3,2,0:T(2,128)(2,1)} %get-tuple-element.13), channel_id=1, source_target_pairs={{0,8},{8,16},{16,24},{1,9},{9,17},{17,25},{2,10},{10,18},{18,26},{... | collective-permute-start | bytes 430088 | tf_op jit(solution)/shard_map/ppermute | solution.py:18
  9.2 14.5 %collective-permute-start.1 = (bf16[4,1,2,14,640]{4,1,3,2,0:T(2,128)(2,1)}, bf16[4,1,2,14,640]{4,1,3,2,0:T(2,128)(2,1)}, u32[]{:S(2)}, u32[]{:S(2)}) collective-permute-start(bf16[4,1,2,14,640]{4,1,3,2,0:T(2,128)(2,1)} %get-tuple-element.14), channel_id=1, source_target_pairs={{8,0},{16,8},{24,16},{9,1},{17,9},{25,17},{10,2},{18,10},{26,18},{... | collective-permute-start | bytes 430088 | tf_op jit(solution)/shard_map/ppermute | solution.py:21
  10.7 63.7 %collective-permute-start.2 = (bf16[2,2,77,640]{3,1,2,0:T(2,128)(2,1)}, bf16[2,2,77,640]{3,1,2,0:T(2,128)(2,1)}, u32[]{:S(2)}, u32[]{:S(2)}) collective-permute-start(bf16[2,2,77,640]{3,1,2,0:T(2,128)(2,1)} %param.18), channel_id=1, source_target_pairs={{0,4},{1,5},{2,6},{3,7},{4,0},{5,1},{6,2},{7,3},{8,12},{9,13},{10,... | collective-permute-start | bytes 1182728 | tf_op jit(solution)/shard_map/ppermute | solution.py:29
  15.6 3.2 %copy-start.13 = (s32[16]{0:T(128)S(1)}, s32[16]{0:T(128)}, u32[]{:S(2)}) copy-start(s32[16]{0:T(128)} %param.17) | copy-start | bytes 196
  23.7 7.2 %slice-start = ((s8[7372800]{0:T(1024)(128)(4,1)}), s8[4194304]{0:T(1024)(128)(4,1)S(1)}, s32[]{:S(2)}) async-start(s8[7372800]{0:T(1024)(128)(4,1)} %bitcast.127), calls=%async_computation | async-start | bytes 8388608
  25.8 5.0 %slice-start.1 = ((s8[7372800]{0:T(1024)(128)(4,1)}), s8[3178496]{0:T(1024)(128)(4,1)S(1)}, s32[]{:S(2)}) async-start(s8[7372800]{0:T(1024)(128)(4,1)} %bitcast.127), calls=%async_computation.1 | async-start | bytes 6356992
  36.9 1.3 %copy-start.2 = (f32[4,4,2,14,640]{4,3,2,1,0:T(8,128)S(1)}, f32[4,4,2,14,640]{4,3,2,1,0:T(8,128)}, u32[]{:S(2)}) copy-start(f32[4,4,2,14,640]{4,3,2,1,0:T(8,128)} %fusion.41) | copy-start | bytes 3440644
  36.9 1.3 %copy-start.10 = (f32[640]{0:T(1024)S(1)}, f32[640]{0:T(1024)}, u32[]{:S(2)}) copy-start(f32[640]{0:T(1024)} %param.20) | copy-start | bytes 7684
  44.8 0.7 copy-start.8
  45.8 0.8 copy-start.5
  56.3 2.6 %copy-start.6 = (bf16[4,4,2,14,640]{4,1,3,2,0:T(4,128)(2,1)S(1)}, bf16[4,4,2,14,640]{4,1,3,2,0:T(4,128)(2,1)}, u32[]{:S(2)}) copy-start(bf16[4,4,2,14,640]{4,1,3,2,0:T(4,128)(2,1)} %copy-done.5) | copy-start | bytes 1720324
  56.3 2.6 %copy-start.11 = (bf16[640,640]{1,0:T(8,128)(2,1)S(1)}, bf16[640,640]{1,0:T(8,128)(2,1)}, u32[]{:S(2)}) copy-start(bf16[640,640]{1,0:T(8,128)(2,1)} %param.25) | copy-start | bytes 2457604
  71.3 1.2 %copy-start.9 = (f32[640]{0:T(1024)S(1)}, f32[640]{0:T(1024)}, u32[]{:S(2)}) copy-start(f32[640]{0:T(1024)} %param.27) | copy-start | bytes 7684
  72.3 1.1 %copy-start.3 = (bf16[640,640]{1,0:T(8,128)(2,1)S(1)}, bf16[640,640]{1,0:T(8,128)(2,1)}, u32[]{:S(2)}) copy-start(bf16[640,640]{1,0:T(8,128)(2,1)} %param.28) | copy-start | bytes 2457604
  79.1 0.9 %copy-start.4 = (f32[2,10,112,77]{2,3,1,0:T(8,128)}, f32[2,10,112,77]{2,3,1,0:T(8,128)S(1)}, u32[]{:S(2)}) copy-start(f32[2,10,112,77]{2,3,1,0:T(8,128)S(1)} %convolution_multiply_fusion) | copy-start | bytes 2069764
where the time goes:
time: 87.3 us; the launch traced here: 86.6 us
  matrix products  29.2 us (33%)
  local copies, waits for them, and re-layouts  23.4 us (27%)
  other arithmetic  19.8 us (23%)
  starting transfers between devices  8.98 us (10%)
  waiting for transfers between devices  4.79 us (5%)
    dot_general x15, matrix products, project(): return jnp.dot(field, weight, preferred_element_type=jnp.float32)  19 us
    add x1, other arithmetic, block(): after_conv = states.astype(jnp.float32) + conv_sum  6.56 us
    ppermute x1, starting transfers between devices, padded_2(): lax.ppermute(lax.slice_in_dim(block, block.shape[dim] - width, None, axis...  4.85 us
    ppermute x1, waiting for transfers between devices, padded_2(): lax.ppermute(lax.slice_in_dim(block, 0, width, axis=dim), axis, backward)  4.79 us
    reshape x2, local copies, waits for them, and re-layouts, block(): time_mixed = time_mixed.astype(jnp.bfloat16).reshape(states.shape)  4.76 us
    concatenate x2, other arithmetic, padded_2(): block = jnp.concatenate([low, block, high], axis=dim)  4.34 us
    unnamed x33, local copies, waits for them, and re-layouts  3.56 us
    dot_general x1, matrix products, block(): jnp.einsum('srwhfg,srwghd->srwfhd', time_weights, time_value, preferred_e...  2.99 us
  transfers between devices with their start and end apart: 3, of which 1 were waited for; matrix products, arithmetic and copies ran while one was open for 62% of the time, Pallas kernels for 0%

commit v1 on v0

v1 whole, which is shorter than its diff:
```python
import functools
import jax
import jax.numpy as jnp
from jax import lax
from jax.experimental import pallas as pl
from jax.experimental.pallas import tpu as pltpu
from jax.sharding import PartitionSpec as P

HEAD_DIM = 64
REQ_DEV = 2
PAD = 16
EPSILON = 1e-06
LOG2E = 1.4426950408889634
F32 = jnp.float32
BF16 = jnp.bfloat16
NEG = -1e30


def rms(x, gain):
    return x * lax.rsqrt(jnp.mean(x * x, axis=-1, keepdims=True) + EPSILON) * gain


def silu(y):
    return y * (0.5 * jnp.tanh(0.5 * y) + 0.5)


def dot(a, b):
    return jnp.dot(a, b, preferred_element_type=F32)


def dot_t(a, b):
    return lax.dot_general(a, b, (((1,), (1,)), ((), ())), preferred_element_type=F32)


def conv_kernel(x_ref, w_ref, bias_ref, gain_ref, out_ref, act):
    slots, rows, _, wide = x_ref.shape
    width = wide // 2
    for c in range(2):
        x = x_ref[:, :, :, c * width : (c + 1) * width].astype(F32)
        act[:, :, :, c * width : (c + 1) * width] = silu(rms(x, gain_ref[...])).astype(BF16)
    for c in range(2):
        lo, hi = 1 - c, 3 - c

        def taps(dr):
            return w_ref[dr, lo:hi].reshape(wide, width)

        mid = dot(act[...].reshape(-1, wide), taps(1)).reshape(slots, rows, PAD, width)
        out_ref[c] = x_ref[:, :, :, c * width : (c + 1) * width].astype(F32) + bias_ref[...] + mid
        up = dot(act[:, : rows - 1].reshape(-1, wide), taps(0))
        out_ref[c, :, 1:] += up.reshape(slots, rows - 1, PAD, width)
        down = dot(act[:, 1:].reshape(-1, wide), taps(2))
        out_ref[c, :, : rows - 1] += down.reshape(slots, rows - 1, PAD, width)


def two_heads(q, k, v, mask, frames_scale):
    m = q.shape[0]
    n = k.shape[0]
    lane = lax.broadcasted_iota(jnp.int32, (m, 2 * HEAD_DIM), 1)
    first = lane < HEAD_DIM
    zero = jnp.zeros_like(q)
    stacked = jnp.concatenate([jnp.where(first, q, zero), jnp.where(first, zero, q)], axis=0)
    s = dot_t(stacked, k)
    if mask is not None:
        s = s + mask
    top = jnp.max(s, axis=-1, keepdims=True)
    p = jnp.exp2((s - top) * frames_scale).astype(BF16)
    both = dot(p, jnp.concatenate([v, jnp.ones((n, 2 * HEAD_DIM), BF16)], axis=1))
    d = 2 * HEAD_DIM
    num = jnp.where(first, both[:m, :d], both[m:, :d])
    den = jnp.where(first, both[:m, d:], both[m:, d:])
    return (num / den).astype(BF16)


def time_kernel(
    frames, part_ref, low_ref, high_ref, w_ref, cgain_ref, tgain_ref, wq_ref, wk_ref, wv_ref, wo_ref,
    xgain_ref, xq_ref, after_ref, query_ref, normed, tq, tk, tv, mixed, mask
):
    cols, slots, rows, _, width = part_ref.shape
    wide = 2 * width
    half = slots // 2
    total = cols * slots * rows * PAD
    block = half * rows * PAD
    low = jnp.concatenate(
        [silu(rms(low_ref[:, :, c * width : (c + 1) * width].astype(F32), cgain_ref[...])).astype(BF16) for c in range(2)],
        axis=-1,
    ).reshape(-1, wide)
    high = jnp.concatenate(
        [silu(rms(high_ref[:, :, c * width : (c + 1) * width].astype(F32), cgain_ref[...])).astype(BF16) for c in range(2)],
        axis=-1,
    ).reshape(-1, wide)
    for c in range(2):
        lo, hi = 1 - c, 3 - c
        after_ref[c] = part_ref[c]
        after_ref[c, :, 0] += dot(low, w_ref[0, lo:hi].reshape(wide, width)).reshape(slots, PAD, width)
        after_ref[c, :, rows - 1] += dot(high, w_ref[2, lo:hi].reshape(wide, width)).reshape(slots, PAD, width)
    normed[...] = rms(after_ref[...].reshape(total, width), tgain_ref[...]).astype(BF16)
    tq[...] = dot(normed[...], wq_ref[...]).astype(BF16)
    tk[...] = dot(normed[...], wk_ref[...]).astype(BF16)
    tv[...] = dot(normed[...], wv_ref[...]).astype(BF16)
    row = lax.broadcasted_iota(jnp.int32, (2 * block, block), 0) % block
    col = lax.broadcasted_iota(jnp.int32, (2 * block, block), 1)
    mask[...] = jnp.where((row // PAD == col // PAD) & (col % PAD < frames), 0.0, NEG).astype(F32)
    for b in range(total // block):
        rs = slice(b * block, (b + 1) * block)
        for j in range(width // 128):
            ls = slice(j * 128, (j + 1) * 128)
            mixed[rs, ls] = two_heads(tq[rs, ls], tk[rs, ls], tv[rs, ls], mask[...], 0.125 * LOG2E)
    after_ref[...] += dot(mixed[...], wo_ref[...]).reshape(after_ref.shape)
    for c in range(2):
        nc = rms(after_ref[c, :half].reshape(block, width), xgain_ref[...]).astype(BF16)
        query_ref[c] = dot(nc, xq_ref[...]).astype(BF16).reshape(half, rows, PAD, width)


def cross_kernel(
    frames, slot_ref, gate_ref, after_ref, query_ref, own_ref, far_ref, xo_ref, out_ref, mixed
):
    cols, slots, rows, _, width = after_ref.shape
    half = slots // 2
    for r in range(half):
        index = slot_ref[r]
        mine = index < REQ_DEV
        i = lax.rem(index, REQ_DEV)
        k = jnp.where(mine, own_ref[0, i], far_ref[0, i])
        v = jnp.where(mine, own_ref[1, i], far_ref[1, i])
        q = query_ref[:, r].reshape(cols * rows * PAD, width)
        for j in range(width // 128):
            ls = slice(j * 128, (j + 1) * 128)
            out = two_heads(q[:, ls], k[:, ls], v[:, ls], None, 0.125 * LOG2E)
            mixed[:, r, :, :, ls] = out.reshape(cols, rows, PAD, 128)
    frame = lax.broadcasted_iota(jnp.int32, (rows, PAD, width), 1).astype(F32)
    scale = 1.0 + 2.0 * frame / (frames - 1)
    for c in range(cols):
        add = dot(mixed[c].reshape(-1, width), xo_ref[...]).reshape(half, rows, PAD, width)
        for r in range(half):
            cond = (after_ref[c, r] + add[r]).astype(BF16).astype(F32)
            uncond = after_ref[c, half + r].astype(BF16).astype(F32)
            guided = jnp.where(gate_ref[r] == 1, uncond + scale * (cond - uncond), cond)
            out_ref[r, :, :, c * width : (c + 1) * width] = guided.astype(BF16)


def on_device(
    hidden_states, gate, context_slot, context_pages, conv_weight, conv_bias, conv_gain, temporal_gain,
    temporal_query, temporal_key, temporal_value, temporal_out, cross_gain, cross_query, cross_out,
):
    _, _, rows, cols, frames, width = hidden_states.shape
    slots = 2 * REQ_DEV
    count = lax.axis_size("req")
    device_index = lax.axis_index("req")
    partner_pairs = [(i, i ^ (count // 2)) for i in range(count)]
    strips = lax.axis_size("strip")
    forward = [(i, i + 1) for i in range(strips - 1)]
    backward = [(i + 1, i) for i in range(strips - 1)]
    wanted = lax.dynamic_slice_in_dim(context_slot, device_index * REQ_DEV, REQ_DEV)
    local = wanted - device_index * REQ_DEV
    index = jnp.where((local >= 0) & (local < REQ_DEV), local, REQ_DEV + lax.rem(wanted, REQ_DEV))

    far_pages = lax.ppermute(context_pages, "req", partner_pairs)
    x = hidden_states.reshape((slots, rows, cols, frames, width)).transpose(0, 1, 3, 2, 4)
    x = x.reshape(slots, rows, frames, cols * width)
    x = jnp.pad(x, ((0, 0), (0, 0), (0, PAD - frames), (0, 0)))
    low = lax.ppermute(x[:, rows - 1], "strip", forward)
    high = lax.ppermute(x[:, 0], "strip", backward)

    vec = lambda g: g.reshape(1, width)
    vm = pl.BlockSpec(memory_space=pltpu.VMEM)
    sm = pl.BlockSpec(memory_space=pltpu.SMEM)
    any_ = pl.BlockSpec(memory_space=pl.ANY)
    total = cols * slots * rows * PAD
    part = pl.pallas_call(
        conv_kernel,
        out_shape=jax.ShapeDtypeStruct((cols, slots, rows, PAD, width), F32),
        in_specs=[vm] * 4,
        out_specs=vm,
        scratch_shapes=[pltpu.VMEM((slots, rows, PAD, cols * width), BF16)],
        compiler_params=pltpu.CompilerParams(vmem_limit_bytes=24 << 20),
        cost_estimate=pl.CostEstimate(flops=2 * 256 * 3840 * 640 * 2, bytes_accessed=9 << 20, transcendentals=0),
        name="conv_own",
    )(x, conv_weight, vec(conv_bias), vec(conv_gain))
    after, query = pl.pallas_call(
        functools.partial(time_kernel, frames),
        out_shape=(
            jax.ShapeDtypeStruct((cols, slots, rows, PAD, width), F32),
            jax.ShapeDtypeStruct((cols, REQ_DEV, rows, PAD, width), BF16),
        ),
        in_specs=[vm] * 12,
        out_specs=(vm, vm),
        scratch_shapes=[pltpu.VMEM((total, width), BF16)] * 5
        + [pltpu.VMEM((slots * rows * PAD, slots * rows * PAD // 2), F32)],
        compiler_params=pltpu.CompilerParams(vmem_limit_bytes=32 << 20),
        cost_estimate=pl.CostEstimate(flops=2 * 512 * 640 * 640 * 5, bytes_accessed=9 << 20, transcendentals=0),
        name="time_mix",
    )(
        part, low, high, conv_weight, vec(conv_gain), vec(temporal_gain), temporal_query, temporal_key,
        temporal_value, temporal_out, vec(cross_gain), cross_query,
    )
    out = pl.pallas_call(
        functools.partial(cross_kernel, frames),
        out_shape=jax.ShapeDtypeStruct((REQ_DEV, rows, PAD, cols * width), BF16),
        in_specs=[sm, sm] + [vm] * 5,
        out_specs=vm,
        scratch_shapes=[pltpu.VMEM((cols, REQ_DEV, rows, PAD, width), BF16)],
        compiler_params=pltpu.CompilerParams(vmem_limit_bytes=24 << 20),
        cost_estimate=pl.CostEstimate(flops=2 * 256 * 640 * 640, bytes_accessed=4 << 20, transcendentals=0),
        name="cross_mix",
    )(index, gate, after, query, context_pages, far_pages, cross_out)
    out = out[:, :, :frames].reshape(REQ_DEV, rows, frames, cols, width)
    return out.transpose(0, 1, 3, 2, 4)


def solution(mesh):
    return jax.shard_map(
        on_device,
        mesh=mesh,
        in_specs=(
            P(None, "req", "strip", None, None, None),
            P("req"),
            P(),
            P(None, "req", None, None),
        )
        + (P(),) * 11,
        out_specs=P("req", "strip", None, None, None),
        check_vma=False,
    )
```

time: 87.3 us -> 38.5 us (0.44)
  matrix products: 29.2 us -> 0 us
  other arithmetic: 19.8 us -> 0.09 us
  Pallas kernels: 0 us -> 13.8 us
  local copies, waits for them, and re-layouts: 23.4 us -> 14.5 us
  waiting for transfers between devices: 4.79 us -> 0.01 us
    dot_general x20 -> x0, matrix products: 29.2 us -> none  [the longest x15 19 us: project(): return jnp.dot(field, weight, preferred_element_type=jnp.float32)]
    pallas_call x0 -> x3, Pallas kernels: none -> 13.8 us  [the longest x1 8.25 us: on_device(): pl.pallas_call(functools.partial(time_kernel, frames), out_shape=(jax.Sha...]
    reshape x5 -> x7, local copies, waits for them, and re-layouts: 10.8 us -> 1.27 us  [the longest x1 0.82 us: on_device(): out = out[:, :, :frames].reshape(REQ_DEV, rows, frames, cols, width)]
    unnamed x33 -> x34, local copies, waits for them, and re-layouts: 3.56 us -> 11.9 us
    add x4 -> x0, other arithmetic: 7.49 us -> none  [the longest x1 6.56 us: block(): after_conv = states.astype(jnp.float32) + conv_sum]
    slice x5 -> x0, local copies, waits for them, and re-layouts: 4.8 us -> none  [the longest x3 2.41 us: cross_mixer(): return cross_attend(queries, chosen[0], chosen[1])]
    ppermute x3, waiting for transfers between devices: 4.79 us -> 0.01 us  [the longest x1 0.01 us: on_device(): far_pages = lax.ppermute(context_pages, 'req', partner_pairs)]
    concatenate x3 -> x0, other arithmetic: 4.42 us -> none  [the longest x2 4.34 us: padded_2(): block = jnp.concatenate([low, block, high], axis=dim)]
  transfers between devices with their start and end apart: 3 -> 3, of which waited for: 1 -> 0; matrix products, arithmetic and copies ran while one was open for 62% -> 1% of each run, Pallas kernels for 0% -> 29%
where the time goes in v1:
time: 38.5 us; the launch traced here: 38 us
  local copies, waits for them, and re-layouts  14.5 us (38%)
  Pallas kernels  13.8 us (36%)
  starting transfers between devices  9.44 us (25%)
    unnamed x34, local copies, waits for them, and re-layouts  11.9 us
    pallas_call x1, Pallas kernels, on_device(): pl.pallas_call(functools.partial(time_kernel, frames), out_shape=(jax.Sha...  8.25 us
    ppermute x1, starting transfers between devices, on_device(): low = lax.ppermute(x[:, rows - 1], 'strip', forward)  5.51 us
    pallas_call x1, Pallas kernels, on_device(): pl.pallas_call(conv_kernel, out_shape=jax.ShapeDtypeStruct((cols, slots,...  2.95 us
    ppermute x1, starting transfers between devices, on_device(): far_pages = lax.ppermute(context_pages, 'req', partner_pairs)  2.65 us
    pallas_call x1, Pallas kernels, on_device(): pl.pallas_call(functools.partial(cross_kernel, frames), out_shape=jax.Sha...  2.57 us
    ppermute x1, starting transfers between devices, on_device(): high = lax.ppermute(x[:, 0], 'strip', backward)  1.28 us
    reshape x1, local copies, waits for them, and re-layouts, on_device(): out = out[:, :, :frames].reshape(REQ_DEV, rows, frames, cols, width)  0.82 us
  transfers between devices with their start and end apart: 3, of which 0 were waited for; matrix products, arithmetic and copies ran while one was open for 1% of the time, Pallas kernels for 29%

profile of v1, /device:TPU:0, one launch (start us, length us, event | category | flops | bytes accessed | tf_op | source)
XLA Modules:
  0.0 38.0 jit_solution(4637584184006430971)
XLA Ops:
  0.0 1.1 %copy-done = bf16[2,2,4,2,14,640]{5,3,4,2,1,0:T(2,128)(2,1)S(1)} copy-done((bf16[2,2,4,2,14,640]{5,3,4,2,1,0:T(2,128)(2,1)S(1)}, bf16[2,2,4,2,14,640]{5,3,4,2,1,0:T(2,128)(2,1)}, u32[]{:S(2)}) %copy-start) | copy-done | bytes 573464
  1.1 0.5 %copy_bitcast_fusion = bf16[4,4,14,2,640]{4,3,1,2,0:T(2,128)(2,1)S(1)} fusion(bf16[2,2,4,2,14,640]{5,3,4,2,1,0:T(2,128)(2,1)S(1)} %copy-done), kind=kLoop, calls=%fused_computation | loop fusion | bytes 1146880 | tf_op jit(solution)/shard_map/transpose | solution.py:158
  1.5 0.4 reshape.23
  1.9 0.0 copy-start.10
  1.9 0.1 copy.21
  2.0 0.0 copy-start.11
  2.0 0.0 copy-start.12
  2.0 0.7 %slice_bitcast_fusion = (bf16[4,16,1280]{2,1,0:T(8,128)(2,1)}, bf16[4,16,1280]{2,1,0:T(8,128)(2,1)}) fusion(bf16[4,4,14,1280]{3,2,0,1:T(8,128)(2,1)S(1)} %copy.21), kind=kLoop, calls=%fused_computation.1 | loop fusion | bytes 901120 | tf_op jit(solution)/shard_map/squeeze | solution.py:162
  2.8 5.5 %collective-permute-start = (bf16[4,16,1280]{2,1,0:T(8,128)(2,1)}, bf16[4,16,1280]{2,1,0:T(8,128)(2,1)}, u32[]{:S(2)}, u32[]{:S(2)}) collective-permute-start(bf16[4,16,1280]{2,1,0:T(8,128)(2,1)} %get-tuple-element.10), channel_id=1, source_target_pairs={{0,8},{8,16},{16,24},{1,9},{9,17},{17,25},{2,10},{10,18},{18,26},{... | collective-permute-start | bytes 491528 | tf_op jit(solution)/shard_map/ppermute | solution.py:161
  8.3 1.3 %collective-permute-start.1 = (bf16[4,16,1280]{2,1,0:T(8,128)(2,1)}, bf16[4,16,1280]{2,1,0:T(8,128)(2,1)}, u32[]{:S(2)}, u32[]{:S(2)}) collective-permute-start(bf16[4,16,1280]{2,1,0:T(8,128)(2,1)} %get-tuple-element.9), channel_id=1, source_target_pairs={{8,0},{16,8},{24,16},{9,1},{17,9},{25,17},{10,2},{18,10},{26,18},{... | collective-permute-start | bytes 491528 | tf_op jit(solution)/shard_map/ppermute | solution.py:162
  9.6 2.7 %collective-permute-start.2 = (bf16[2,2,77,640]{3,2,1,0:T(8,128)(2,1)S(1)}, bf16[2,2,77,640]{3,2,1,0:T(8,128)(2,1)S(1)}, u32[]{:S(2)}, u32[]{:S(2)}) collective-permute-start(bf16[2,2,77,640]{3,2,1,0:T(8,128)(2,1)S(1)} %copy.24.own_ref), channel_id=1, source_target_pairs={{0,4},{1,5},{2,6},{3,7},{4,0},{5,1},{6,2},{7,3},{8,12},{9,13},{10,... | collective-permute-start | bytes 1182728 | tf_op jit(solution)/shard_map/ppermute | solution.py:157
  12.4 0.1 pad.4.clone.x_ref
  12.5 3.1 %copy-done.1 = bf16[3,3,640,640]{3,2,1,0:T(8,128)(2,1)S(1)} copy-done((bf16[3,3,640,640]{3,2,1,0:T(8,128)(2,1)S(1)}, bf16[3,3,640,640]{3,2,1,0:T(8,128)(2,1)}, u32[]{:S(2)}) %copy-start.1) | copy-done | bytes 7372824
  15.6 2.9 %conv_own.1.part_ref = f32[2,4,4,16,640]{4,3,2,1,0:T(8,128)S(1)} custom-call(bf16[4,4,16,1280]{3,2,1,0:T(8,128)(2,1)S(1)} %pad.4.clone.x_ref, bf16[3,3,640,640]{3,2,1,0:T(8,128)(2,1)S(1)} %copy-done.1, f32[1,640]{1,0:T(1,128)S(1)} %reshape.24.bias_ref, f32[1,640]{1,0:T(1,128)S(1)} %reshape.25.gain_ref.cgain_ref), custom_call_target="tpu_custom_call" | custom-call | flops 2516582400 | bytes 9437184 | tf_op jit(solution)/shard_map/conv_own/pallas_call | solution.py:169
  18.6 0.1 and_select_fusion.slot_ref
  18.7 0.0 copy-start.2
  18.7 3.1 %copy-done.2 = bf16[3,3,640,640]{3,2,1,0:T(8,128)(2,1)S(1)} copy-done((bf16[3,3,640,640]{3,2,1,0:T(8,128)(2,1)S(1)}, bf16[3,3,640,640]{3,2,1,0:T(8,128)(2,1)}, u32[]{:S(2)}) %copy-start.2) | copy-done | bytes 7372824
  21.8 1.1 %copy-done.5 = bf16[640,640]{1,0:T(8,128)(2,1)S(1)} copy-done((bf16[640,640]{1,0:T(8,128)(2,1)S(1)}, bf16[640,640]{1,0:T(8,128)(2,1)}, u32[]{:S(2)}) %copy-start.5) | copy-done | bytes 819224
  22.9 1.1 %copy-done.6 = bf16[640,640]{1,0:T(8,128)(2,1)S(1)} copy-done((bf16[640,640]{1,0:T(8,128)(2,1)S(1)}, bf16[640,640]{1,0:T(8,128)(2,1)}, u32[]{:S(2)}) %copy-start.6) | copy-done | bytes 819224
  24.1 1.1 %copy-done.7 = bf16[640,640]{1,0:T(8,128)(2,1)S(1)} copy-done((bf16[640,640]{1,0:T(8,128)(2,1)S(1)}, bf16[640,640]{1,0:T(8,128)(2,1)}, u32[]{:S(2)}) %copy-start.7) | copy-done | bytes 819224
  25.2 1.1 %copy-done.8 = bf16[640,640]{1,0:T(8,128)(2,1)S(1)} copy-done((bf16[640,640]{1,0:T(8,128)(2,1)S(1)}, bf16[640,640]{1,0:T(8,128)(2,1)}, u32[]{:S(2)}) %copy-start.8) | copy-done | bytes 819224
  26.4 8.3 %time_mix.1 = (f32[2,4,4,16,640]{4,3,2,1,0:T(8,128)S(1)}, bf16[2,2,4,16,640]{4,3,2,1,0:T(8,128)(2,1)S(1)}) custom-call(f32[2,4,4,16,640]{4,3,2,1,0:T(8,128)S(1)} %conv_own.1.part_ref, bf16[4,16,1280]{2,1,0:T(8,128)(2,1)} %collective-permute-done.low_ref, bf16[4,16,1280]{2,1,0:T(8,128)(2,1)} %collective-permute-done.1.high_ref, ...), custom_call_target="tpu_custom_call" | custom-call | flops 2097152000 | bytes 9437184 | tf_op jit(solution)/shard_map/time_mix/pallas_call | solution.py:179
  34.6 2.6 %cross_mix.1 = bf16[2,4,16,1280]{3,2,1,0:T(8,128)(2,1)S(1)} custom-call(s32[2]{0:T(128)S(1)} %and_select_fusion.slot_ref, s32[2]{0:T(128)S(1)} %copy-done.9, f32[2,4,4,16,640]{4,3,2,1,0:T(8,128)S(1)} %get-tuple-element.7.after_ref, bf16[2,2,4,16,640]{4,3,2,1,0:T(8,128)(2,1)S(1)} %get-tuple-element.8.query_ref, bf16[2,2,77,640]{3,2,1,0:T(8,128)(2,1)S(1)} %copy.24.own_ref, ...), custom_call_target="tpu_custom_call" | custom-call | flops 209715200 | bytes 4194304 | tf_op jit(solution)/shard_map/cross_mix/pallas_call | solution.py:196
  37.2 0.8 %reshape.29 = bf16[2,4,14,2,640]{4,3,2,1,0:T(2,128)(2,1)} reshape(bf16[2,4,14,1280]{3,2,1,0:T(8,128)(2,1)S(1)} %bitcast.14) | data formatting | bytes 573440 | tf_op jit(solution)/shard_map/reshape | solution.py:206
  (30 shorter events, 0.2 us)
Async XLA Ops:
  0.0 1.1 %copy-start = (bf16[2,2,4,2,14,640]{5,3,4,2,1,0:T(2,128)(2,1)S(1)}, bf16[2,2,4,2,14,640]{5,3,4,2,1,0:T(2,128)(2,1)}, u32[]{:S(2)}) copy-start(bf16[2,2,4,2,14,640]{5,3,4,2,1,0:T(2,128)(2,1)} %param.15) | copy-start | bytes 1720324
  1.9 7.7 %copy-start.10 = (bf16[2,2,77,640]{3,1,2,0:T(2,128)(2,1)S(1)}, bf16[2,2,77,640]{3,1,2,0:T(2,128)(2,1)}, u32[]{:S(2)}) copy-start(bf16[2,2,77,640]{3,1,2,0:T(2,128)(2,1)} %param.18) | copy-start | bytes 1182724
  2.0 10.3 %copy-start.11 = (f32[640]{0:T(1024)S(1)}, f32[640]{0:T(1024)}, u32[]{:S(2)}) copy-start(f32[640]{0:T(1024)} %param.21) | copy-start | bytes 7684
  2.0 10.4 %copy-start.12 = (f32[640]{0:T(1024)S(1)}, f32[640]{0:T(1024)}, u32[]{:S(2)}) copy-start(f32[640]{0:T(1024)} %param.20) | copy-start | bytes 7684
  2.8 15.9 %collective-permute-start = (bf16[4,16,1280]{2,1,0:T(8,128)(2,1)}, bf16[4,16,1280]{2,1,0:T(8,128)(2,1)}, u32[]{:S(2)}, u32[]{:S(2)}) collective-permute-start(bf16[4,16,1280]{2,1,0:T(8,128)(2,1)} %get-tuple-element.10), channel_id=1, source_target_pairs={{0,8},{8,16},{16,24},{1,9},{9,17},{17,25},{2,10},{10,18},{18,26},{... | collective-permute-start | bytes 491528 | tf_op jit(solution)/shard_map/ppermute | solution.py:161
  8.3 10.4 %collective-permute-start.1 = (bf16[4,16,1280]{2,1,0:T(8,128)(2,1)}, bf16[4,16,1280]{2,1,0:T(8,128)(2,1)}, u32[]{:S(2)}, u32[]{:S(2)}) collective-permute-start(bf16[4,16,1280]{2,1,0:T(8,128)(2,1)} %get-tuple-element.9), channel_id=1, source_target_pairs={{8,0},{16,8},{24,16},{9,1},{17,9},{25,17},{10,2},{18,10},{26,18},{... | collective-permute-start | bytes 491528 | tf_op jit(solution)/shard_map/ppermute | solution.py:162
  9.6 25.0 %collective-permute-start.2 = (bf16[2,2,77,640]{3,2,1,0:T(8,128)(2,1)S(1)}, bf16[2,2,77,640]{3,2,1,0:T(8,128)(2,1)S(1)}, u32[]{:S(2)}, u32[]{:S(2)}) collective-permute-start(bf16[2,2,77,640]{3,2,1,0:T(8,128)(2,1)S(1)} %copy.24.own_ref), channel_id=1, source_target_pairs={{0,4},{1,5},{2,6},{3,7},{4,0},{5,1},{6,2},{7,3},{8,12},{9,13},{10,... | collective-permute-start | bytes 1182728 | tf_op jit(solution)/shard_map/ppermute | solution.py:157
  12.4 3.1 %copy-start.1 = (bf16[3,3,640,640]{3,2,1,0:T(8,128)(2,1)S(1)}, bf16[3,3,640,640]{3,2,1,0:T(8,128)(2,1)}, u32[]{:S(2)}) copy-start(bf16[3,3,640,640]{3,2,1,0:T(8,128)(2,1)} %w_ref.3) | copy-start | bytes 22118404
  15.5 3.0 %copy-start.13 = (f32[640]{0:T(1024)S(1)}, f32[640]{0:T(1024)}, u32[]{:S(2)}) copy-start(f32[640]{0:T(1024)} %param.22) | copy-start | bytes 7684
  15.5 3.0 %copy-start.14 = (f32[640]{0:T(1024)S(1)}, f32[640]{0:T(1024)}, u32[]{:S(2)}) copy-start(f32[640]{0:T(1024)} %param.27) | copy-start | bytes 7684
  15.5 3.0 %copy-start.15 = (s32[16]{0:T(128)S(1)}, s32[16]{0:T(128)}, u32[]{:S(2)}) copy-start(s32[16]{0:T(128)} %param.17) | copy-start | bytes 196
  15.5 3.1 %copy-start.4 = (bf16[640,640]{1,0:T(8,128)(2,1)S(1)}, bf16[640,640]{1,0:T(8,128)(2,1)}, u32[]{:S(2)}) copy-start(bf16[640,640]{1,0:T(8,128)(2,1)} %wq_ref.1) | copy-start | bytes 2457604
  18.6 16.1 %copy-start.9 = (s32[2]{0:T(128)S(1)}, s32[2]{0:T(128)}, u32[]{:S(2)}) copy-start(s32[2]{0:T(128)} %gate_ref.1) | copy-start | bytes 28
  18.7 3.1 %copy-start.2 = (bf16[3,3,640,640]{3,2,1,0:T(8,128)(2,1)S(1)}, bf16[3,3,640,640]{3,2,1,0:T(8,128)(2,1)}, u32[]{:S(2)}) copy-start(bf16[3,3,640,640]{3,2,1,0:T(8,128)(2,1)} %w_ref.3) | copy-start | bytes 22118404
  21.8 1.1 %copy-start.5 = (bf16[640,640]{1,0:T(8,128)(2,1)S(1)}, bf16[640,640]{1,0:T(8,128)(2,1)}, u32[]{:S(2)}) copy-start(bf16[640,640]{1,0:T(8,128)(2,1)} %wk_ref.1) | copy-start | bytes 2457604
  22.9 1.1 %copy-start.6 = (bf16[640,640]{1,0:T(8,128)(2,1)S(1)}, bf16[640,640]{1,0:T(8,128)(2,1)}, u32[]{:S(2)}) copy-start(bf16[640,640]{1,0:T(8,128)(2,1)} %wv_ref.1) | copy-start | bytes 2457604
  24.1 1.1 %copy-start.7 = (bf16[640,640]{1,0:T(8,128)(2,1)S(1)}, bf16[640,640]{1,0:T(8,128)(2,1)}, u32[]{:S(2)}) copy-start(bf16[640,640]{1,0:T(8,128)(2,1)} %wo_ref.1) | copy-start | bytes 2457604
  25.2 1.1 %copy-start.8 = (bf16[640,640]{1,0:T(8,128)(2,1)S(1)}, bf16[640,640]{1,0:T(8,128)(2,1)}, u32[]{:S(2)}) copy-start(bf16[640,640]{1,0:T(8,128)(2,1)} %xq_ref.1) | copy-start | bytes 2457604
  26.4 8.3 %copy-start.3 = (bf16[640,640]{1,0:T(8,128)(2,1)S(1)}, bf16[640,640]{1,0:T(8,128)(2,1)}, u32[]{:S(2)}) copy-start(bf16[640,640]{1,0:T(8,128)(2,1)} %xo_ref.1) | copy-start | bytes 2457604

commit v2 on v1

--- a/solution.py
+++ b/solution.py
@@ -14,10 +14,11 @@
 F32 = jnp.float32
 BF16 = jnp.bfloat16
 NEG = -1e30
+COST0, COST1, COST2, COST3 = 12 * 10**9, 10**9, 10**9, 10**9
 
 
 def rms(x, gain):
-    return x * lax.rsqrt(jnp.mean(x * x, axis=-1, keepdims=True) + EPSILON) * gain
+    return x * lax.rsqrt(jnp.mean(x * x, axis=-1, keepdims=True) + EPSILON) * gain.reshape((1,) * (x.ndim - 1) + (-1,))
 
 
 def silu(y):
@@ -32,20 +33,34 @@
     return lax.dot_general(a, b, (((1,), (1,)), ((), ())), preferred_element_type=F32)
 
 
-def conv_kernel(x_ref, w_ref, bias_ref, gain_ref, out_ref, act):
+def act_kernel(raw_ref, gain_ref, x_ref, act_ref, first_ref, last_ref):
+    slots, rows, frames, cols, width = raw_ref.shape
+    for s in range(slots):
+        for c in range(cols):
+            ls = slice(c * width, (c + 1) * width)
+            for r in range(rows):
+                raw = raw_ref[s, r, :, c, :]
+                raw = jnp.concatenate([raw, jnp.zeros((PAD - frames, width), BF16)], axis=0)
+                x_ref[s, r, :, ls] = raw
+                a = silu(rms(raw.astype(F32), gain_ref[...])).astype(BF16)
+                act_ref[s, r, :, ls] = a
+                if r == 0:
+                    first_ref[s, :, ls] = a
+                if r == rows - 1:
+                    last_ref[s, :, ls] = a
+
+
+def conv_kernel(x_ref, act, w_ref, bias_ref, out_ref):
     slots, rows, _, wide = x_ref.shape
     width = wide // 2
     for c in range(2):
-        x = x_ref[:, :, :, c * width : (c + 1) * width].astype(F32)
-        act[:, :, :, c * width : (c + 1) * width] = silu(rms(x, gain_ref[...])).astype(BF16)
-    for c in range(2):
         lo, hi = 1 - c, 3 - c
 
         def taps(dr):
             return w_ref[dr, lo:hi].reshape(wide, width)
 
         mid = dot(act[...].reshape(-1, wide), taps(1)).reshape(slots, rows, PAD, width)
-        out_ref[c] = x_ref[:, :, :, c * width : (c + 1) * width].astype(F32) + bias_ref[...] + mid
+        out_ref[c] = x_ref[:, :, :, c * width : (c + 1) * width].astype(F32) + bias_ref[...].reshape(1, 1, 1, width) + mid
         up = dot(act[:, : rows - 1].reshape(-1, wide), taps(0))
         out_ref[c, :, 1:] += up.reshape(slots, rows - 1, PAD, width)
         down = dot(act[:, 1:].reshape(-1, wide), taps(2))
@@ -72,7 +87,7 @@
 
 
 def time_kernel(
-    frames, part_ref, low_ref, high_ref, w_ref, cgain_ref, tgain_ref, wq_ref, wk_ref, wv_ref, wo_ref,
+    frames, part_ref, low_ref, high_ref, w_ref, tgain_ref, wq_ref, wk_ref, wv_ref, wo_ref,
     xgain_ref, xq_ref, after_ref, query_ref, normed, tq, tk, tv, mixed, mask
 ):
     cols, slots, rows, _, width = part_ref.shape
@@ -80,14 +95,8 @@
     half = slots // 2
     total = cols * slots * rows * PAD
     block = half * rows * PAD
-    low = jnp.concatenate(
-        [silu(rms(low_ref[:, :, c * width : (c + 1) * width].astype(F32), cgain_ref[...])).astype(BF16) for c in range(2)],
-        axis=-1,
-    ).reshape(-1, wide)
-    high = jnp.concatenate(
-        [silu(rms(high_ref[:, :, c * width : (c + 1) * width].astype(F32), cgain_ref[...])).astype(BF16) for c in range(2)],
-        axis=-1,
-    ).reshape(-1, wide)
+    low = low_ref[...].reshape(-1, wide)
+    high = high_ref[...].reshape(-1, wide)
     for c in range(2):
         lo, hi = 1 - c, 3 - c
         after_ref[c] = part_ref[c]
@@ -116,10 +125,11 @@
 ):
     cols, slots, rows, _, width = after_ref.shape
     half = slots // 2
+    first_page = lax.axis_index("req") * REQ_DEV
     for r in range(half):
-        index = slot_ref[r]
-        mine = index < REQ_DEV
-        i = lax.rem(index, REQ_DEV)
+        page = slot_ref[first_page + r]
+        i = lax.rem(page, REQ_DEV)
+        mine = page - i == first_page
         k = jnp.where(mine, own_ref[0, i], far_ref[0, i])
         v = jnp.where(mine, own_ref[1, i], far_ref[1, i])
         q = query_ref[:, r].reshape(cols * rows * PAD, width)
@@ -145,53 +155,60 @@
     _, _, rows, cols, frames, width = hidden_states.shape
     slots = 2 * REQ_DEV
     count = lax.axis_size("req")
-    device_index = lax.axis_index("req")
     partner_pairs = [(i, i ^ (count // 2)) for i in range(count)]
     strips = lax.axis_size("strip")
     forward = [(i, i + 1) for i in range(strips - 1)]
     backward = [(i + 1, i) for i in range(strips - 1)]
-    wanted = lax.dynamic_slice_in_dim(context_slot, device_index * REQ_DEV, REQ_DEV)
-    local = wanted - device_index * REQ_DEV
-    index = jnp.where((local >= 0) & (local < REQ_DEV), local, REQ_DEV + lax.rem(wanted, REQ_DEV))
-
     far_pages = lax.ppermute(context_pages, "req", partner_pairs)
-    x = hidden_states.reshape((slots, rows, cols, frames, width)).transpose(0, 1, 3, 2, 4)
-    x = x.reshape(slots, rows, frames, cols * width)
-    x = jnp.pad(x, ((0, 0), (0, 0), (0, PAD - frames), (0, 0)))
-    low = lax.ppermute(x[:, rows - 1], "strip", forward)
-    high = lax.ppermute(x[:, 0], "strip", backward)
-
-    vec = lambda g: g.reshape(1, width)
     vm = pl.BlockSpec(memory_space=pltpu.VMEM)
     sm = pl.BlockSpec(memory_space=pltpu.SMEM)
     any_ = pl.BlockSpec(memory_space=pl.ANY)
     total = cols * slots * rows * PAD
+    wide = cols * width
+    raw = hidden_states.reshape((slots, rows, cols, frames, width)).transpose(0, 1, 3, 2, 4)
+    x, act, first, last = pl.pallas_call(
+        act_kernel,
+        out_shape=(
+            jax.ShapeDtypeStruct((slots, rows, PAD, wide), BF16),
+            jax.ShapeDtypeStruct((slots, rows, PAD, wide), BF16),
+            jax.ShapeDtypeStruct((slots, PAD, wide), BF16),
+            jax.ShapeDtypeStruct((slots, PAD, wide), BF16),
+        ),
+        in_specs=[vm] * 2,
+        out_specs=(vm,) * 4,
+        compiler_params=pltpu.CompilerParams(vmem_limit_bytes=8 << 20),
+        cost_estimate=pl.CostEstimate(flops=COST0, bytes_accessed=0, transcendentals=0),
+        name="activate",
+    )(raw, conv_gain)
+    low = lax.ppermute(last, "strip", forward)
+    high = lax.ppermute(first, "strip", backward)
     part = pl.pallas_call(
         conv_kernel,
         out_shape=jax.ShapeDtypeStruct((cols, slots, rows, PAD, width), F32),
         in_specs=[vm] * 4,
         out_specs=vm,
-        scratch_shapes=[pltpu.VMEM((slots, rows, PAD, cols * width), BF16)],
-        compiler_params=pltpu.CompilerParams(vmem_limit_bytes=24 << 20),
-        cost_estimate=pl.CostEstimate(flops=2 * 256 * 3840 * 640 * 2, bytes_accessed=9 << 20, transcendentals=0),
+        compiler_params=pltpu.CompilerParams(vmem_limit_bytes=16 << 20),
+        cost_estimate=pl.CostEstimate(flops=COST1, bytes_accessed=0, transcendentals=0),
         name="conv_own",
-    )(x, conv_weight, vec(conv_bias), vec(conv_gain))
+    )(x, act, conv_weight, conv_bias)
     after, query = pl.pallas_call(
         functools.partial(time_kernel, frames),
         out_shape=(
             jax.ShapeDtypeStruct((cols, slots, rows, PAD, width), F32),
             jax.ShapeDtypeStruct((cols, REQ_DEV, rows, PAD, width), BF16),
         ),
-        in_specs=[vm] * 12,
+        in_specs=[vm] * 11,
         out_specs=(vm, vm),
         scratch_shapes=[pltpu.VMEM((total, width), BF16)] * 5
-        + [pltpu.VMEM((slots * rows * PAD, slots * rows * PAD // 2), F32)],
-        compiler_params=pltpu.CompilerParams(vmem_limit_bytes=32 << 20),
-        cost_estimate=pl.CostEstimate(flops=2 * 512 * 640 * 640 * 5, bytes_accessed=9 << 20, transcendentals=0),
+        + [
+            pltpu.VMEM((slots * rows * PAD, slots * rows * PAD // 2), F32),
+        ],
+        compiler_params=pltpu.CompilerParams(vmem_limit_bytes=16 << 20),
+        cost_estimate=pl.CostEstimate(flops=COST2, bytes_accessed=0, transcendentals=0),
         name="time_mix",
     )(
-        part, low, high, conv_weight, vec(conv_gain), vec(temporal_gain), temporal_query, temporal_key,
-        temporal_value, temporal_out, vec(cross_gain), cross_query,
+        part, low, high, conv_weight, temporal_gain, temporal_query, temporal_key,
+        temporal_value, temporal_out, cross_gain, cross_query,
     )
     out = pl.pallas_call(
         functools.partial(cross_kernel, frames),
@@ -199,10 +216,10 @@
         in_specs=[sm, sm] + [vm] * 5,
         out_specs=vm,
         scratch_shapes=[pltpu.VMEM((cols, REQ_DEV, rows, PAD, width), BF16)],
-        compiler_params=pltpu.CompilerParams(vmem_limit_bytes=24 << 20),
-        cost_estimate=pl.CostEstimate(flops=2 * 256 * 640 * 640, bytes_accessed=4 << 20, transcendentals=0),
+        compiler_params=pltpu.CompilerParams(vmem_limit_bytes=8 << 20),
+        cost_estimate=pl.CostEstimate(flops=COST3, bytes_accessed=0, transcendentals=0),
         name="cross_mix",
-    )(index, gate, after, query, context_pages, far_pages, cross_out)
+    )(context_slot, gate, after, query, context_pages, far_pages, cross_out)
     out = out[:, :, :frames].reshape(REQ_DEV, rows, frames, cols, width)
     return out.transpose(0, 1, 3, 2, 4)
 

time: 38.5 us -> 32.1 us (0.83)
  local copies, waits for them, and re-layouts: 14.5 us -> 4.05 us
  waiting for transfers between devices: 0.01 us -> 4.12 us
  Pallas kernels: 13.8 us -> 14.5 us
  starting transfers between devices: 9.44 us -> 8.98 us
    unnamed x34 -> x31, local copies, waits for them, and re-layouts: 11.9 us -> 3.23 us
    ppermute x2, waiting for transfers between devices: 0.01 us -> 4.12 us  [the longest x1 4.12 us: on_device(): high = lax.ppermute(first, 'strip', backward)]
    pallas_call x0 -> x1, Pallas kernels: none -> 1.96 us  [on_device(): pl.pallas_call(act_kernel, out_shape=(jax.ShapeDtypeStruct((slots, rows,...]
    ppermute x2, starting transfers between devices: 6.79 us -> 4.88 us  [the longest x1 3.4 us: on_device(): low = lax.ppermute(last, 'strip', forward)]
    ppermute x1, starting transfers between devices: 2.65 us -> 4.1 us  [on_device(): far_pages = lax.ppermute(context_pages, 'req', partner_pairs)]
    pallas_call x1, Pallas kernels: 8.25 us -> 7.12 us  [on_device(): pl.pallas_call(functools.partial(time_kernel, frames), out_shape=(jax.Sha...]
    squeeze x1 -> x0, local copies, waits for them, and re-layouts: 0.75 us -> none  [on_device(): high = lax.ppermute(x[:, 0], 'strip', backward)]
    transpose x1 -> x0, local copies, waits for them, and re-layouts: 0.47 us -> none  [on_device(): hidden_states.reshape((slots, rows, cols, frames, width))]
  transfers between devices with their start and end apart: 3 -> 3, of which waited for: 0 -> 1; matrix products, arithmetic and copies ran while one was open for 1% -> 0% of each run, Pallas kernels for 29% -> 37%
where the time goes in v2:
time: 32.1 us; the launch traced here: 31.9 us
  Pallas kernels  14.5 us (45%)
  starting transfers between devices  8.98 us (28%)
  waiting for transfers between devices  4.12 us (13%)
  local copies, waits for them, and re-layouts  4.05 us (13%)
    pallas_call x1, Pallas kernels, on_device(): pl.pallas_call(functools.partial(time_kernel, frames), out_shape=(jax.Sha...  7.12 us
    ppermute x1, waiting for transfers between devices, on_device(): high = lax.ppermute(first, 'strip', backward)  4.12 us
    ppermute x1, starting transfers between devices, on_device(): far_pages = lax.ppermute(context_pages, 'req', partner_pairs)  4.1 us
    ppermute x1, starting transfers between devices, on_device(): low = lax.ppermute(last, 'strip', forward)  3.4 us
    unnamed x31, local copies, waits for them, and re-layouts  3.23 us
    pallas_call x1, Pallas kernels, on_device(): pl.pallas_call(conv_kernel, out_shape=jax.ShapeDtypeStruct((cols, slots,...  2.84 us
    pallas_call x1, Pallas kernels, on_device(): pl.pallas_call(functools.partial(cross_kernel, frames), out_shape=jax.Sha...  2.57 us
    pallas_call x1, Pallas kernels, on_device(): pl.pallas_call(act_kernel, out_shape=(jax.ShapeDtypeStruct((slots, rows,...  1.96 us
  transfers between devices with their start and end apart: 3, of which 1 were waited for; matrix products, arithmetic and copies ran while one was open for 0% of the time, Pallas kernels for 37%

profile of v2, /device:TPU:0, one launch (start us, length us, event | category | flops | bytes accessed | tf_op | source)
XLA Modules:
  0.0 31.9 jit_solution(7549776245989091195)
XLA Ops:
  0.0 1.0 %copy.19.own_ref = bf16[2,2,77,640]{3,2,1,0:T(8,128)(2,1)S(1)} copy(bf16[2,2,77,640]{3,1,2,0:T(2,128)(2,1)} %param.18) | data formatting | bytes 788480 | tf_op args[3]
  1.0 4.1 %collective-permute-start.2 = (bf16[2,2,77,640]{3,2,1,0:T(8,128)(2,1)S(1)}, bf16[2,2,77,640]{3,2,1,0:T(8,128)(2,1)S(1)}, u32[]{:S(2)}, u32[]{:S(2)}) collective-permute-start(bf16[2,2,77,640]{3,2,1,0:T(8,128)(2,1)S(1)} %copy.19.own_ref), channel_id=1, source_target_pairs={{0,4},{1,5},{2,6},{3,7},{4,0},{5,1},{6,2},{7,3},{8,12},{9,13},{10,... | collective-permute-start | bytes 1182728 | tf_op jit(solution)/shard_map/ppermute | solution.py:162
  5.2 1.2 %copy-done.9 = bf16[2,2,4,2,14,640]{5,3,4,2,1,0:T(2,128)(2,1)S(1)} copy-done((bf16[2,2,4,2,14,640]{5,3,4,2,1,0:T(2,128)(2,1)S(1)}, bf16[2,2,4,2,14,640]{5,3,4,2,1,0:T(2,128)(2,1)}, u32[]{:S(2)}) %copy-start.9) | copy-done | bytes 573464
  6.4 0.9 %copy-done.10 = f32[640]{0:T(1024)S(1)} copy-done((f32[640]{0:T(1024)S(1)}, f32[640]{0:T(1024)}, u32[]{:S(2)}) %copy-start.10) | copy-done | bytes 2584
  7.3 2.0 %activate.1 = (bf16[4,4,16,1280]{3,2,1,0:T(8,128)(2,1)S(1)}, bf16[4,4,16,1280]{3,2,1,0:T(8,128)(2,1)S(1)}, bf16[4,16,1280]{2,1,0:T(8,128)(2,1)S(1)}, bf16[4,16,1280]{2,1,0:T(8,128)(2,1)S(1)}) custom-call(bf16[4,4,14,2,640]{4,3,2,1,0:T(2,128)(2,1)S(1)} %bitcast.9, f32[640]{0:T(1024)S(1)} %copy-done.10), custom_call_target="tpu_custom_call" | custom-call | flops 12000000000 | tf_op jit(solution)/shard_map/activate/pallas_call | solution.py:169
  9.2 3.4 %collective-permute-start = (bf16[4,16,1280]{2,1,0:T(8,128)(2,1)S(1)}, bf16[4,16,1280]{2,1,0:T(8,128)(2,1)S(1)}, u32[]{:S(2)}, u32[]{:S(2)}) collective-permute-start(bf16[4,16,1280]{2,1,0:T(8,128)(2,1)S(1)} %get-tuple-element.13), channel_id=1, source_target_pairs={{0,8},{8,16},{16,24},{1,9},{9,17},{17,25},{2,10},{10,18},{18,26},{... | collective-permute-start | bytes 491528 | tf_op jit(solution)/shard_map/ppermute | solution.py:183
  12.6 1.5 %collective-permute-start.1 = (bf16[4,16,1280]{2,1,0:T(8,128)(2,1)S(1)}, bf16[4,16,1280]{2,1,0:T(8,128)(2,1)S(1)}, u32[]{:S(2)}, u32[]{:S(2)}) collective-permute-start(bf16[4,16,1280]{2,1,0:T(8,128)(2,1)S(1)} %get-tuple-element.14), channel_id=1, source_target_pairs={{8,0},{16,8},{24,16},{9,1},{17,9},{25,17},{10,2},{18,10},{26,18},{... | collective-permute-start | bytes 491528 | tf_op jit(solution)/shard_map/ppermute | solution.py:184
  14.2 0.0 copy-start
  14.2 0.0 copy-start.1
  14.2 0.0 copy-start.2
  14.2 0.0 copy-start.3
  14.2 0.0 copy-start.4
  14.2 0.0 copy-start.6
  14.2 0.0 copy-start.7
  14.2 2.8 %conv_own.1.part_ref = f32[2,4,4,16,640]{4,3,2,1,0:T(8,128)S(1)} custom-call(bf16[4,4,16,1280]{3,2,1,0:T(8,128)(2,1)S(1)} %get-tuple-element.11.x_ref, bf16[4,4,16,1280]{3,2,1,0:T(8,128)(2,1)S(1)} %get-tuple-element.12.act, bf16[3,3,640,640]{3,2,1,0:T(8,128)(2,1)S(1)} %bitcast.7, f32[640]{0:T(1024)S(1)} %copy-done.5), custom_call_target="tpu_custom_call" | custom-call | flops 1000000000 | tf_op jit(solution)/shard_map/conv_own/pallas_call | solution.py:185
  17.1 0.0 copy-start.8
  17.1 0.0 copy-start.11
  17.1 0.0 copy-start.12
  17.1 0.0 collective-permute-done.low_ref
  17.1 4.1 %collective-permute-done.1.high_ref = bf16[4,16,1280]{2,1,0:T(8,128)(2,1)S(1)} collective-permute-done((bf16[4,16,1280]{2,1,0:T(8,128)(2,1)S(1)}, bf16[4,16,1280]{2,1,0:T(8,128)(2,1)S(1)}, u32[]{:S(2)}, u32[]{:S(2)}) %collective-permute-start.1) | collective-permute-done | bytes 163872 | tf_op jit(solution)/shard_map/ppermute | solution.py:184
  21.3 7.1 %time_mix.1 = (f32[2,4,4,16,640]{4,3,2,1,0:T(8,128)S(1)}, bf16[2,2,4,16,640]{4,3,2,1,0:T(8,128)(2,1)S(1)}) custom-call(f32[2,4,4,16,640]{4,3,2,1,0:T(8,128)S(1)} %conv_own.1.part_ref, bf16[4,16,1280]{2,1,0:T(8,128)(2,1)S(1)} %collective-permute-done.low_ref, bf16[4,16,1280]{2,1,0:T(8,128)(2,1)S(1)} %collective-permute-done.1.high_ref, ...), custom_call_target="tpu_custom_call" | custom-call | flops 1000000000 | tf_op jit(solution)/shard_map/time_mix/pallas_call | solution.py:194
  28.4 0.0 collective-permute-done.2.far_ref
  28.5 2.6 %cross_mix.1 = bf16[2,4,16,1280]{3,2,1,0:T(8,128)(2,1)S(1)} custom-call(s32[16]{0:T(128)S(1)} %copy-done.11, s32[2]{0:T(128)S(1)} %copy-done.12, f32[2,4,4,16,640]{4,3,2,1,0:T(8,128)S(1)} %get-tuple-element.15.after_ref, bf16[2,2,4,16,640]{4,3,2,1,0:T(8,128)(2,1)S(1)} %get-tuple-element.16.query_ref, bf16[2,2,77,640]{3,2,1,0:T(8,128)(2,1)S(1)} %copy.19.own_ref, ...), custom_call_target="tpu_custom_call" | custom-call | flops 1000000000 | tf_op jit(solution)/shard_map/cross_mix/pallas_call | solution.py:213
  31.0 0.8 %reshape.8 = bf16[2,4,14,2,640]{4,3,2,1,0:T(2,128)(2,1)} reshape(bf16[2,4,14,1280]{3,2,1,0:T(8,128)(2,1)S(1)} %bitcast.8) | data formatting | bytes 573440 | tf_op jit(solution)/shard_map/reshape | solution.py:223
  (19 shorter events, 0.0 us)
Async XLA Ops:
  1.0 27.4 %collective-permute-start.2 = (bf16[2,2,77,640]{3,2,1,0:T(8,128)(2,1)S(1)}, bf16[2,2,77,640]{3,2,1,0:T(8,128)(2,1)S(1)}, u32[]{:S(2)}, u32[]{:S(2)}) collective-permute-start(bf16[2,2,77,640]{3,2,1,0:T(8,128)(2,1)S(1)} %copy.19.own_ref), channel_id=1, source_target_pairs={{0,4},{1,5},{2,6},{3,7},{4,0},{5,1},{6,2},{7,3},{8,12},{9,13},{10,... | collective-permute-start | bytes 1182728 | tf_op jit(solution)/shard_map/ppermute | solution.py:162
  5.1 9.0 %slice-start = ((s8[7372800]{0:T(1024)(128)(4,1)}), s8[4194304]{0:T(1024)(128)(4,1)S(1)}, s32[]{:S(2)}) async-start(s8[7372800]{0:T(1024)(128)(4,1)} %bitcast.6), calls=%async_computation | async-start | bytes 8388608
  5.1 1.2 %copy-start.9 = (bf16[2,2,4,2,14,640]{5,3,4,2,1,0:T(2,128)(2,1)S(1)}, bf16[2,2,4,2,14,640]{5,3,4,2,1,0:T(2,128)(2,1)}, u32[]{:S(2)}) copy-start(bf16[2,2,4,2,14,640]{5,3,4,2,1,0:T(2,128)(2,1)} %param.15) | copy-start | bytes 1720324
  6.4 0.9 %copy-start.10 = (f32[640]{0:T(1024)S(1)}, f32[640]{0:T(1024)}, u32[]{:S(2)}) copy-start(f32[640]{0:T(1024)} %gain_ref.1) | copy-start | bytes 7684
  7.3 6.9 %slice-start.1 = ((s8[7372800]{0:T(1024)(128)(4,1)}), s8[3178496]{0:T(1024)(128)(4,1)S(1)}, s32[]{:S(2)}) async-start(s8[7372800]{0:T(1024)(128)(4,1)} %bitcast.6), calls=%async_computation.1 | async-start | bytes 6356992
  7.3 6.9 %copy-start.5 = (f32[640]{0:T(1024)S(1)}, f32[640]{0:T(1024)}, u32[]{:S(2)}) copy-start(f32[640]{0:T(1024)} %bias_ref.1) | copy-start | bytes 7684
  9.2 7.9 %collective-permute-start = (bf16[4,16,1280]{2,1,0:T(8,128)(2,1)S(1)}, bf16[4,16,1280]{2,1,0:T(8,128)(2,1)S(1)}, u32[]{:S(2)}, u32[]{:S(2)}) collective-permute-start(bf16[4,16,1280]{2,1,0:T(8,128)(2,1)S(1)} %get-tuple-element.13), channel_id=1, source_target_pairs={{0,8},{8,16},{16,24},{1,9},{9,17},{17,25},{2,10},{10,18},{18,26},{... | collective-permute-start | bytes 491528 | tf_op jit(solution)/shard_map/ppermute | solution.py:183
  12.6 8.6 %collective-permute-start.1 = (bf16[4,16,1280]{2,1,0:T(8,128)(2,1)S(1)}, bf16[4,16,1280]{2,1,0:T(8,128)(2,1)S(1)}, u32[]{:S(2)}, u32[]{:S(2)}) collective-permute-start(bf16[4,16,1280]{2,1,0:T(8,128)(2,1)S(1)} %get-tuple-element.14), channel_id=1, source_target_pairs={{8,0},{16,8},{24,16},{9,1},{17,9},{25,17},{10,2},{18,10},{26,18},{... | collective-permute-start | bytes 491528 | tf_op jit(solution)/shard_map/ppermute | solution.py:184
  14.2 7.1 %copy-start = (bf16[640,640]{1,0:T(8,128)(2,1)S(1)}, bf16[640,640]{1,0:T(8,128)(2,1)}, u32[]{:S(2)}) copy-start(bf16[640,640]{1,0:T(8,128)(2,1)} %wq_ref.1) | copy-start | bytes 2457604
  14.2 7.1 %copy-start.1 = (bf16[640,640]{1,0:T(8,128)(2,1)S(1)}, bf16[640,640]{1,0:T(8,128)(2,1)}, u32[]{:S(2)}) copy-start(bf16[640,640]{1,0:T(8,128)(2,1)} %wk_ref.1) | copy-start | bytes 2457604
  14.2 7.1 %copy-start.2 = (bf16[640,640]{1,0:T(8,128)(2,1)S(1)}, bf16[640,640]{1,0:T(8,128)(2,1)}, u32[]{:S(2)}) copy-start(bf16[640,640]{1,0:T(8,128)(2,1)} %wv_ref.1) | copy-start | bytes 2457604
  14.2 7.1 %copy-start.3 = (bf16[640,640]{1,0:T(8,128)(2,1)S(1)}, bf16[640,640]{1,0:T(8,128)(2,1)}, u32[]{:S(2)}) copy-start(bf16[640,640]{1,0:T(8,128)(2,1)} %wo_ref.1) | copy-start | bytes 2457604
  14.2 7.1 %copy-start.4 = (bf16[640,640]{1,0:T(8,128)(2,1)S(1)}, bf16[640,640]{1,0:T(8,128)(2,1)}, u32[]{:S(2)}) copy-start(bf16[640,640]{1,0:T(8,128)(2,1)} %xq_ref.1) | copy-start | bytes 2457604
  14.2 7.1 %copy-start.6 = (f32[640]{0:T(1024)S(1)}, f32[640]{0:T(1024)}, u32[]{:S(2)}) copy-start(f32[640]{0:T(1024)} %tgain_ref.1) | copy-start | bytes 7684
  14.2 7.1 %copy-start.7 = (f32[640]{0:T(1024)S(1)}, f32[640]{0:T(1024)}, u32[]{:S(2)}) copy-start(f32[640]{0:T(1024)} %xgain_ref.1) | copy-start | bytes 7684
  17.1 11.3 %copy-start.8 = (bf16[640,640]{1,0:T(8,128)(2,1)S(1)}, bf16[640,640]{1,0:T(8,128)(2,1)}, u32[]{:S(2)}) copy-start(bf16[640,640]{1,0:T(8,128)(2,1)} %xo_ref.1) | copy-start | bytes 2457604
  17.1 11.3 %copy-start.11 = (s32[16]{0:T(128)S(1)}, s32[16]{0:T(128)}, u32[]{:S(2)}) copy-start(s32[16]{0:T(128)} %slot_ref.1) | copy-start | bytes 196
  17.1 11.3 %copy-start.12 = (s32[2]{0:T(128)S(1)}, s32[2]{0:T(128)}, u32[]{:S(2)}) copy-start(s32[2]{0:T(128)} %gate_ref.1) | copy-start | bytes 28

commit v3 on v2

--- a/solution.py
+++ b/solution.py
@@ -14,7 +14,11 @@
 F32 = jnp.float32
 BF16 = jnp.bfloat16
 NEG = -1e30
-COST0, COST1, COST2, COST3 = 12 * 10**9, 10**9, 10**9, 10**9
+COSTP, COST0, COST1, COST2, COST3 = 3 * 10**9, 16 * 10**9, 10**9, 10**9, 10**9
+
+
+def cost(flops):
+    return pl.CostEstimate(flops=flops, bytes_accessed=0, transcendentals=0)
 
 
 def rms(x, gain):
@@ -33,38 +37,66 @@
     return lax.dot_general(a, b, (((1,), (1,)), ((), ())), preferred_element_type=F32)
 
 
-def act_kernel(raw_ref, gain_ref, x_ref, act_ref, first_ref, last_ref):
-    slots, rows, frames, cols, width = raw_ref.shape
+def pass_kernel(in_ref, out_ref):
+    pass
+
+
+def first_row():
+    return 1 - lax.rem(lax.axis_index("strip"), 2)
+
+
+def lay_out(raw_ref, gain_ref, s, r, c):
+    frames, width = raw_ref.shape[2], raw_ref.shape[4]
+    raw = raw_ref[s, r, :, c, :]
+    raw = jnp.concatenate([raw, jnp.zeros((PAD - frames, width), BF16)], axis=0)
+    return raw, silu(rms(raw.astype(F32), gain_ref[...])).astype(BF16)
+
+
+def edge_kernel(raw_ref, gain_ref, x_ref, act_ref):
+    slots, rows, _, cols, width = raw_ref.shape
+    r = first_row() * (rows - 1)
     for s in range(slots):
         for c in range(cols):
             ls = slice(c * width, (c + 1) * width)
-            for r in range(rows):
-                raw = raw_ref[s, r, :, c, :]
-                raw = jnp.concatenate([raw, jnp.zeros((PAD - frames, width), BF16)], axis=0)
-                x_ref[s, r, :, ls] = raw
-                a = silu(rms(raw.astype(F32), gain_ref[...])).astype(BF16)
+            x_ref[s, :, ls], act_ref[s, :, ls] = lay_out(raw_ref, gain_ref, s, r, c)
+
+
+def act_kernel(raw_ref, gain_ref, edge_x_ref, edge_act_ref, x_ref, act_ref, edge_ref):
+    slots, rows, _, cols, width = raw_ref.shape
+    done = first_row() * (rows - 1)
+    other = rows - 1 - done
+    x_ref[:, done] = edge_x_ref[...]
+    act_ref[:, done] = edge_act_ref[...]
+    for s in range(slots):
+        for c in range(cols):
+            ls = slice(c * width, (c + 1) * width)
+            for r in (other, *range(1, rows - 1)):
+                x_ref[s, r, :, ls], a = lay_out(raw_ref, gain_ref, s, r, c)
                 act_ref[s, r, :, ls] = a
-                if r == 0:
-                    first_ref[s, :, ls] = a
-                if r == rows - 1:
-                    last_ref[s, :, ls] = a
-
-
-def conv_kernel(x_ref, act, w_ref, bias_ref, out_ref):
+                if r is other:
+                    edge_ref[s, :, ls] = a
+
+
+def conv_kernel(x_ref, act_ref, near_ref, w_ref, bias_ref, out_ref, ext):
     slots, rows, _, wide = x_ref.shape
     width = wide // 2
+    side = 2 * first_row()
+    ext[:, 1 : rows + 1] = act_ref[...]
+    ext[:, side // 2 * (rows + 1)] = near_ref[...]
+    both = jnp.concatenate(
+        [ext[:, 1 : rows + 1].reshape(-1, wide), ext[:, pl.ds(side, rows)].reshape(-1, wide)], axis=-1
+    )
+    inner = ext[:, pl.ds(2 - side // 2, rows - 1)].reshape(-1, wide)
+    inner_rows = pl.ds(side // 2, rows - 1)
     for c in range(2):
-        lo, hi = 1 - c, 3 - c
-
-        def taps(dr):
-            return w_ref[dr, lo:hi].reshape(wide, width)
-
-        mid = dot(act[...].reshape(-1, wide), taps(1)).reshape(slots, rows, PAD, width)
+        taps = pl.ds(1 - c, 2)
+        weights = jnp.concatenate(
+            [w_ref[1, taps].reshape(wide, width), w_ref[side, taps].reshape(wide, width)], axis=0
+        )
+        mid = dot(both, weights).reshape(slots, rows, PAD, width)
         out_ref[c] = x_ref[:, :, :, c * width : (c + 1) * width].astype(F32) + bias_ref[...].reshape(1, 1, 1, width) + mid
-        up = dot(act[:, : rows - 1].reshape(-1, wide), taps(0))
-        out_ref[c, :, 1:] += up.reshape(slots, rows - 1, PAD, width)
-        down = dot(act[:, 1:].reshape(-1, wide), taps(2))
-        out_ref[c, :, : rows - 1] += down.reshape(slots, rows - 1, PAD, width)
+        rest = dot(inner, w_ref[2 - side, taps].reshape(wide, width))
+        out_ref[c, :, inner_rows] += rest.reshape(slots, rows - 1, PAD, width)
 
 
 def two_heads(q, k, v, mask, frames_scale):
@@ -87,7 +119,7 @@
 
 
 def time_kernel(
-    frames, part_ref, low_ref, high_ref, w_ref, tgain_ref, wq_ref, wk_ref, wv_ref, wo_ref,
+    frames, part_ref, next_ref, w_ref, tgain_ref, wq_ref, wk_ref, wv_ref, wo_ref,
     xgain_ref, xq_ref, after_ref, query_ref, normed, tq, tk, tv, mixed, mask
 ):
     cols, slots, rows, _, width = part_ref.shape
@@ -95,13 +127,12 @@
     half = slots // 2
     total = cols * slots * rows * PAD
     block = half * rows * PAD
-    low = low_ref[...].reshape(-1, wide)
-    high = high_ref[...].reshape(-1, wide)
+    side = 1 - first_row()
+    other = next_ref[...].reshape(-1, wide)
     for c in range(2):
-        lo, hi = 1 - c, 3 - c
         after_ref[c] = part_ref[c]
-        after_ref[c, :, 0] += dot(low, w_ref[0, lo:hi].reshape(wide, width)).reshape(slots, PAD, width)
-        after_ref[c, :, rows - 1] += dot(high, w_ref[2, lo:hi].reshape(wide, width)).reshape(slots, PAD, width)
+        add = dot(other, w_ref[2 * side, pl.ds(1 - c, 2)].reshape(wide, width))
+        after_ref[c, :, side * (rows - 1)] += add.reshape(slots, PAD, width)
     normed[...] = rms(after_ref[...].reshape(total, width), tgain_ref[...]).astype(BF16)
     tq[...] = dot(normed[...], wq_ref[...]).astype(BF16)
     tk[...] = dot(normed[...], wk_ref[...]).astype(BF16)
@@ -157,57 +188,75 @@
     count = lax.axis_size("req")
     partner_pairs = [(i, i ^ (count // 2)) for i in range(count)]
     strips = lax.axis_size("strip")
-    forward = [(i, i + 1) for i in range(strips - 1)]
-    backward = [(i + 1, i) for i in range(strips - 1)]
-    far_pages = lax.ppermute(context_pages, "req", partner_pairs)
+    near_pairs, next_pairs = (
+        [p for i in range(start, strips - 1, 2) for p in ((i, i + 1), (i + 1, i))] for start in (0, 1)
+    )
+
     vm = pl.BlockSpec(memory_space=pltpu.VMEM)
     sm = pl.BlockSpec(memory_space=pltpu.SMEM)
     any_ = pl.BlockSpec(memory_space=pl.ANY)
     total = cols * slots * rows * PAD
     wide = cols * width
     raw = hidden_states.reshape((slots, rows, cols, frames, width)).transpose(0, 1, 3, 2, 4)
-    x, act, first, last = pl.pallas_call(
+    context_pages = pl.pallas_call(
+        pass_kernel,
+        out_shape=jax.ShapeDtypeStruct(context_pages.shape, BF16),
+        in_specs=[any_],
+        out_specs=any_,
+        input_output_aliases={0: 0},
+        cost_estimate=cost(COSTP),
+        name="pages",
+    )(context_pages)
+    far_pages = lax.ppermute(context_pages, "req", partner_pairs)
+    row = jax.ShapeDtypeStruct((slots, PAD, wide), BF16)
+    whole = jax.ShapeDtypeStruct((slots, rows, PAD, wide), BF16)
+    edge_x, edge_act = pl.pallas_call(
+        edge_kernel,
+        out_shape=(row, row),
+        in_specs=[vm] * 2,
+        out_specs=(vm, vm),
+        compiler_params=pltpu.CompilerParams(vmem_limit_bytes=8 << 20),
+        cost_estimate=cost(COST0),
+        name="edge",
+    )(raw, conv_gain)
+    near = lax.ppermute(edge_act, "strip", near_pairs)
+    x, act, edge = pl.pallas_call(
         act_kernel,
-        out_shape=(
-            jax.ShapeDtypeStruct((slots, rows, PAD, wide), BF16),
-            jax.ShapeDtypeStruct((slots, rows, PAD, wide), BF16),
-            jax.ShapeDtypeStruct((slots, PAD, wide), BF16),
-            jax.ShapeDtypeStruct((slots, PAD, wide), BF16),
-        ),
-        in_specs=[vm] * 2,
-        out_specs=(vm,) * 4,
+        out_shape=(whole, whole, row),
+        in_specs=[vm] * 4,
+        out_specs=(vm,) * 3,
         compiler_params=pltpu.CompilerParams(vmem_limit_bytes=8 << 20),
-        cost_estimate=pl.CostEstimate(flops=COST0, bytes_accessed=0, transcendentals=0),
+        cost_estimate=cost(COST1),
         name="activate",
-    )(raw, conv_gain)
-    low = lax.ppermute(last, "strip", forward)
-    high = lax.ppermute(first, "strip", backward)
+    )(raw, conv_gain, edge_x, edge_act)
+    other = lax.ppermute(edge, "strip", next_pairs)
     part = pl.pallas_call(
         conv_kernel,
         out_shape=jax.ShapeDtypeStruct((cols, slots, rows, PAD, width), F32),
-        in_specs=[vm] * 4,
+        in_specs=[vm] * 5,
         out_specs=vm,
+        scratch_shapes=[pltpu.VMEM((slots, rows + 2, PAD, wide), BF16)],
         compiler_params=pltpu.CompilerParams(vmem_limit_bytes=16 << 20),
-        cost_estimate=pl.CostEstimate(flops=COST1, bytes_accessed=0, transcendentals=0),
+        cost_estimate=cost(COST1),
         name="conv_own",
-    )(x, act, conv_weight, conv_bias)
+    )(x, act, near, conv_weight, conv_bias)
     after, query = pl.pallas_call(
         functools.partial(time_kernel, frames),
         out_shape=(
             jax.ShapeDtypeStruct((cols, slots, rows, PAD, width), F32),
             jax.ShapeDtypeStruct((cols, REQ_DEV, rows, PAD, width), BF16),
         ),
-        in_specs=[vm] * 11,
+        in_specs=[vm] * 10,
         out_specs=(vm, vm),
         scratch_shapes=[pltpu.VMEM((total, width), BF16)] * 5
         + [
             pltpu.VMEM((slots * rows * PAD, slots * rows * PAD // 2), F32),
         ],
         compiler_params=pltpu.CompilerParams(vmem_limit_bytes=16 << 20),
-        cost_estimate=pl.CostEstimate(flops=COST2, bytes_accessed=0, transcendentals=0),
+        cost_estimate=cost(COST2),
         name="time_mix",
     )(
-        part, low, high, conv_weight, temporal_gain, temporal_query, temporal_key,
+        part, other, conv_weight, temporal_gain, temporal_query, temporal_key,
         temporal_value, temporal_out, cross_gain, cross_query,
     )
     out = pl.pallas_call(
@@ -217,7 +266,7 @@
         out_specs=vm,
         scratch_shapes=[pltpu.VMEM((cols, REQ_DEV, rows, PAD, width), BF16)],
         compiler_params=pltpu.CompilerParams(vmem_limit_bytes=8 << 20),
-        cost_estimate=pl.CostEstimate(flops=COST3, bytes_accessed=0, transcendentals=0),
+        cost_estimate=cost(COST3),
         name="cross_mix",
     )(context_slot, gate, after, query, context_pages, far_pages, cross_out)
     out = out[:, :, :frames].reshape(REQ_DEV, rows, frames, cols, width)

time: 32.1 us -> 27.9 us (0.87)
  starting transfers between devices: 8.98 us -> 6.26 us
  local copies, waits for them, and re-layouts: 4.05 us -> 2.7 us
  Pallas kernels: 14.5 us -> 14.1 us
  waiting for transfers between devices: 4.12 us -> 4.46 us
    ppermute x2, starting transfers between devices: 4.88 us -> 2.23 us  [the longest x1 1.56 us: on_device(): near = lax.ppermute(edge_act, 'strip', near_pairs)]
    ppermute x1, waiting for transfers between devices: 0.01 us -> 2.33 us  [on_device(): far_pages = lax.ppermute(context_pages, 'req', partner_pairs)]
    ppermute x2, waiting for transfers between devices: 4.12 us -> 2.13 us  [the longest x1 2.13 us: on_device(): near = lax.ppermute(edge_act, 'strip', near_pairs)]
    unnamed x31 -> x33, local copies, waits for them, and re-layouts: 3.23 us -> 1.88 us
    pallas_call x1, Pallas kernels: 7.12 us -> 6.6 us  [on_device(): pl.pallas_call(functools.partial(time_kernel, frames), out_shape=(jax.Sha...]
    pallas_call x1 -> x3, Pallas kernels: 1.96 us -> 1.83 us  [the longest x1 1.36 us: on_device(): pl.pallas_call(act_kernel, out_shape=(whole, whole, row), in_specs=[vm] *...]
  transfers between devices with their start and end apart: 3 -> 3, of which waited for: 1 -> 2; matrix products, arithmetic and copies ran while one was open for 0% -> 0% of each run, Pallas kernels for 37% -> 41%
where the time goes in v3:
time: 27.9 us; the launch traced here: 27.7 us
  Pallas kernels  14.1 us (51%)
  starting transfers between devices  6.26 us (22%)
  waiting for transfers between devices  4.46 us (16%)
  local copies, waits for them, and re-layouts  2.7 us (10%)
    pallas_call x1, Pallas kernels, on_device(): pl.pallas_call(functools.partial(time_kernel, frames), out_shape=(jax.Sha...  6.6 us
    ppermute x1, starting transfers between devices, on_device(): far_pages = lax.ppermute(context_pages, 'req', partner_pairs)  4.04 us
    pallas_call x1, Pallas kernels, on_device(): pl.pallas_call(conv_kernel, out_shape=jax.ShapeDtypeStruct((cols, slots,...  3.06 us
    pallas_call x1, Pallas kernels, on_device(): pl.pallas_call(functools.partial(cross_kernel, frames), out_shape=jax.Sha...  2.56 us
    ppermute x1, waiting for transfers between devices, on_device(): far_pages = lax.ppermute(context_pages, 'req', partner_pairs)  2.33 us
    ppermute x1, waiting for transfers between devices, on_device(): near = lax.ppermute(edge_act, 'strip', near_pairs)  2.13 us
    unnamed x33, local copies, waits for them, and re-layouts  1.88 us
    ppermute x1, starting transfers between devices, on_device(): near = lax.ppermute(edge_act, 'strip', near_pairs)  1.56 us
  transfers between devices with their start and end apart: 3, of which 2 were waited for; matrix products, arithmetic and copies ran while one was open for 0% of the time, Pallas kernels for 41%

profile of v3, /device:TPU:0, one launch (start us, length us, event | category | flops | bytes accessed | tf_op | source)
XLA Modules:
  0.0 27.7 jit_solution(8741192807691169743)
XLA Ops:
  0.0 1.8 %copy.18.in_ref = bf16[2,2,77,640]{3,2,1,0:T(8,128)(2,1)} copy(bf16[2,2,77,640]{3,1,2,0:T(2,128)(2,1)} %param.18) | data formatting | bytes 788480 | tf_op args[3]
  1.8 4.0 %collective-permute-start.2 = (bf16[2,2,77,640]{3,2,1,0:T(8,128)(2,1)}, bf16[2,2,77,640]{3,2,1,0:T(8,128)(2,1)S(1)}, u32[]{:S(2)}, u32[]{:S(2)}) collective-permute-start(bf16[2,2,77,640]{3,2,1,0:T(8,128)(2,1)} %pages.1.own_ref), channel_id=1, source_target_pairs={{0,4},{1,5},{2,6},{3,7},{4,0},{5,1},{6,2},{7,3},{8,12},{9,13},{10,... | collective-permute-start | bytes 1182728 | tf_op jit(solution)/shard_map/ppermute | solution.py:210
  5.8 0.5 %edge.1 = (bf16[4,16,1280]{2,1,0:T(8,128)(2,1)S(1)}, bf16[4,16,1280]{2,1,0:T(8,128)(2,1)S(1)}) custom-call(bf16[4,4,14,2,640]{4,3,2,1,0:T(2,128)(2,1)S(1)} %bitcast.9, f32[640]{0:T(1024)S(1)} %copy-done.11), custom_call_target="tpu_custom_call" | custom-call | flops 16000000000 | tf_op jit(solution)/shard_map/edge/pallas_call | solution.py:213
  6.3 1.6 %collective-permute-start = (bf16[4,16,1280]{2,1,0:T(8,128)(2,1)S(1)}, bf16[4,16,1280]{2,1,0:T(8,128)(2,1)S(1)}, u32[]{:S(2)}, u32[]{:S(2)}) collective-permute-start(bf16[4,16,1280]{2,1,0:T(8,128)(2,1)S(1)} %get-tuple-element.13.edge_act_ref), channel_id=1, source_target_pairs={{0,8},{8,0},{16,24},{24,16},{1,9},{9,1},{17,25},{25,17},{2,10},{10... | collective-permute-start | bytes 491528 | tf_op jit(solution)/shard_map/ppermute | solution.py:222
  7.9 1.4 %activate.1 = (bf16[4,4,16,1280]{3,2,1,0:T(8,128)(2,1)S(1)}, bf16[4,4,16,1280]{3,2,1,0:T(8,128)(2,1)S(1)}, bf16[4,16,1280]{2,1,0:T(8,128)(2,1)S(1)}) custom-call(bf16[4,4,14,2,640]{4,3,2,1,0:T(2,128)(2,1)S(1)} %bitcast.10, f32[640]{0:T(1024)S(1)} %copy-done.11, bf16[4,16,1280]{2,1,0:T(8,128)(2,1)S(1)} %get-tuple-element.12.edge_x_ref, ...), custom_call_target="tpu_custom_call" | custom-call | flops 1000000000 | tf_op jit(solution)/shard_map/activate/pallas_call | solution.py:223
  9.2 0.7 %collective-permute-start.1 = (bf16[4,16,1280]{2,1,0:T(8,128)(2,1)S(1)}, bf16[4,16,1280]{2,1,0:T(8,128)(2,1)S(1)}, u32[]{:S(2)}, u32[]{:S(2)}) collective-permute-start(bf16[4,16,1280]{2,1,0:T(8,128)(2,1)S(1)} %get-tuple-element.16), channel_id=1, source_target_pairs={{8,16},{16,8},{9,17},{17,9},{10,18},{18,10},{11,19},{19,11},{12,20... | collective-permute-start | bytes 491528 | tf_op jit(solution)/shard_map/ppermute | solution.py:232
  9.9 2.1 %collective-permute-done.near_ref = bf16[4,16,1280]{2,1,0:T(8,128)(2,1)S(1)} collective-permute-done((bf16[4,16,1280]{2,1,0:T(8,128)(2,1)S(1)}, bf16[4,16,1280]{2,1,0:T(8,128)(2,1)S(1)}, u32[]{:S(2)}, u32[]{:S(2)}) %collective-permute-start) | collective-permute-done | bytes 163872 | tf_op jit(solution)/shard_map/ppermute | solution.py:222
  12.1 0.0 slice-done
  12.1 0.0 copy-start
  12.1 0.0 copy-start.1
  12.1 0.0 copy-start.2
  12.1 0.0 copy-start.3
  12.1 0.0 copy-start.4
  12.1 0.0 copy-start.7
  12.1 0.0 copy-start.8
  12.2 3.1 %conv_own.1.part_ref = f32[2,4,4,16,640]{4,3,2,1,0:T(8,128)S(1)} custom-call(bf16[4,4,16,1280]{3,2,1,0:T(8,128)(2,1)S(1)} %get-tuple-element.14.x_ref, bf16[4,4,16,1280]{3,2,1,0:T(8,128)(2,1)S(1)} %get-tuple-element.15.act_ref, bf16[4,16,1280]{2,1,0:T(8,128)(2,1)S(1)} %collective-permute-done.near_ref, bf16[3,3,640,640]{3,2,1,0:T(8,128)(2,1)S(1)} %bitcast.7, ...), custom_call_target="tpu_custom_call" | custom-call | flops 1000000000 | tf_op jit(solution)/shard_map/conv_own/pallas_call | solution.py:233
  15.2 0.0 copy-start.9
  15.2 0.0 copy-start.12
  15.3 0.0 copy-start.13
  15.3 0.0 collective-permute-done.1.next_ref
  15.4 6.6 %time_mix.1 = (f32[2,4,4,16,640]{4,3,2,1,0:T(8,128)S(1)}, bf16[2,2,4,16,640]{4,3,2,1,0:T(8,128)(2,1)S(1)}) custom-call(f32[2,4,4,16,640]{4,3,2,1,0:T(8,128)S(1)} %conv_own.1.part_ref, bf16[4,16,1280]{2,1,0:T(8,128)(2,1)S(1)} %collective-permute-done.1.next_ref, bf16[3,3,640,640]{3,2,1,0:T(8,128)(2,1)S(1)} %bitcast.7, f32[640]{0:T(1024)S(1)} %copy-done.7, ...), custom_call_target="tpu_custom_call" | custom-call | flops 1000000000 | tf_op jit(solution)/shard_map/time_mix/pallas_call | solution.py:243
  22.0 2.3 %collective-permute-done.2.far_ref = bf16[2,2,77,640]{3,2,1,0:T(8,128)(2,1)S(1)} collective-permute-done((bf16[2,2,77,640]{3,2,1,0:T(8,128)(2,1)}, bf16[2,2,77,640]{3,2,1,0:T(8,128)(2,1)S(1)}, u32[]{:S(2)}, u32[]{:S(2)}) %collective-permute-start.2) | collective-permute-done | bytes 394272 | tf_op jit(solution)/shard_map/ppermute | solution.py:210
  24.3 2.6 %cross_mix.1 = bf16[2,4,16,1280]{3,2,1,0:T(8,128)(2,1)S(1)} custom-call(s32[16]{0:T(128)S(1)} %copy-done.12, s32[2]{0:T(128)S(1)} %copy-done.13, f32[2,4,4,16,640]{4,3,2,1,0:T(8,128)S(1)} %get-tuple-element.17.after_ref, bf16[2,2,4,16,640]{4,3,2,1,0:T(8,128)(2,1)S(1)} %get-tuple-element.18.query_ref, bf16[2,2,77,640]{3,2,1,0:T(8,128)(2,1)S(1)} %copy-done.5, ...), custom_call_target="tpu_custom_call" | custom-call | flops 1000000000 | tf_op jit(solution)/shard_map/cross_mix/pallas_call | solution.py:262
  26.9 0.8 %reshape.8 = bf16[2,4,14,2,640]{4,3,2,1,0:T(2,128)(2,1)} reshape(bf16[2,4,14,1280]{3,2,1,0:T(8,128)(2,1)S(1)} %bitcast.8) | data formatting | bytes 573440 | tf_op jit(solution)/shard_map/reshape | solution.py:272
  (23 shorter events, 0.0 us)
Async XLA Ops:
  1.8 4.0 %copy-start.10 = (bf16[2,2,4,2,14,640]{5,3,4,2,1,0:T(2,128)(2,1)S(1)}, bf16[2,2,4,2,14,640]{5,3,4,2,1,0:T(2,128)(2,1)}, u32[]{:S(2)}) copy-start(bf16[2,2,4,2,14,640]{5,3,4,2,1,0:T(2,128)(2,1)} %param.15) | copy-start | bytes 1720324
  1.8 4.0 %copy-start.11 = (f32[640]{0:T(1024)S(1)}, f32[640]{0:T(1024)}, u32[]{:S(2)}) copy-start(f32[640]{0:T(1024)} %gain_ref.3) | copy-start | bytes 7684
  1.8 22.5 %collective-permute-start.2 = (bf16[2,2,77,640]{3,2,1,0:T(8,128)(2,1)}, bf16[2,2,77,640]{3,2,1,0:T(8,128)(2,1)S(1)}, u32[]{:S(2)}, u32[]{:S(2)}) collective-permute-start(bf16[2,2,77,640]{3,2,1,0:T(8,128)(2,1)} %pages.1.own_ref), channel_id=1, source_target_pairs={{0,4},{1,5},{2,6},{3,7},{4,0},{5,1},{6,2},{7,3},{8,12},{9,13},{10,... | collective-permute-start | bytes 1182728 | tf_op jit(solution)/shard_map/ppermute | solution.py:210
  5.8 6.2 %slice-start = ((s8[7372800]{0:T(1024)(128)(4,1)}), s8[4194304]{0:T(1024)(128)(4,1)S(1)}, s32[]{:S(2)}) async-start(s8[7372800]{0:T(1024)(128)(4,1)} %bitcast.6), calls=%async_computation | async-start | bytes 8388608
  5.8 6.2 %slice-start.1 = ((s8[7372800]{0:T(1024)(128)(4,1)}), s8[3178496]{0:T(1024)(128)(4,1)S(1)}, s32[]{:S(2)}) async-start(s8[7372800]{0:T(1024)(128)(4,1)} %bitcast.6), calls=%async_computation.1 | async-start | bytes 6356992
  6.3 5.7 %collective-permute-start = (bf16[4,16,1280]{2,1,0:T(8,128)(2,1)S(1)}, bf16[4,16,1280]{2,1,0:T(8,128)(2,1)S(1)}, u32[]{:S(2)}, u32[]{:S(2)}) collective-permute-start(bf16[4,16,1280]{2,1,0:T(8,128)(2,1)S(1)} %get-tuple-element.13.edge_act_ref), channel_id=1, source_target_pairs={{0,8},{8,0},{16,24},{24,16},{1,9},{9,1},{17,25},{25,17},{2,10},{10... | collective-permute-start | bytes 491528 | tf_op jit(solution)/shard_map/ppermute | solution.py:222
  7.9 4.2 %copy-start.6 = (f32[640]{0:T(1024)S(1)}, f32[640]{0:T(1024)}, u32[]{:S(2)}) copy-start(f32[640]{0:T(1024)} %bias_ref.1) | copy-start | bytes 7684
  9.2 6.0 %collective-permute-start.1 = (bf16[4,16,1280]{2,1,0:T(8,128)(2,1)S(1)}, bf16[4,16,1280]{2,1,0:T(8,128)(2,1)S(1)}, u32[]{:S(2)}, u32[]{:S(2)}) collective-permute-start(bf16[4,16,1280]{2,1,0:T(8,128)(2,1)S(1)} %get-tuple-element.16), channel_id=1, source_target_pairs={{8,16},{16,8},{9,17},{17,9},{10,18},{18,10},{11,19},{19,11},{12,20... | collective-permute-start | bytes 491528 | tf_op jit(solution)/shard_map/ppermute | solution.py:232
  12.1 3.2 %copy-start = (bf16[640,640]{1,0:T(8,128)(2,1)S(1)}, bf16[640,640]{1,0:T(8,128)(2,1)}, u32[]{:S(2)}) copy-start(bf16[640,640]{1,0:T(8,128)(2,1)} %wq_ref.1) | copy-start | bytes 2457604
  12.1 3.2 %copy-start.1 = (bf16[640,640]{1,0:T(8,128)(2,1)S(1)}, bf16[640,640]{1,0:T(8,128)(2,1)}, u32[]{:S(2)}) copy-start(bf16[640,640]{1,0:T(8,128)(2,1)} %wk_ref.1) | copy-start | bytes 2457604
  12.1 3.2 %copy-start.2 = (bf16[640,640]{1,0:T(8,128)(2,1)S(1)}, bf16[640,640]{1,0:T(8,128)(2,1)}, u32[]{:S(2)}) copy-start(bf16[640,640]{1,0:T(8,128)(2,1)} %wv_ref.1) | copy-start | bytes 2457604
  12.1 3.2 %copy-start.3 = (bf16[640,640]{1,0:T(8,128)(2,1)S(1)}, bf16[640,640]{1,0:T(8,128)(2,1)}, u32[]{:S(2)}) copy-start(bf16[640,640]{1,0:T(8,128)(2,1)} %wo_ref.1) | copy-start | bytes 2457604
  12.1 3.2 %copy-start.4 = (bf16[640,640]{1,0:T(8,128)(2,1)S(1)}, bf16[640,640]{1,0:T(8,128)(2,1)}, u32[]{:S(2)}) copy-start(bf16[640,640]{1,0:T(8,128)(2,1)} %xq_ref.1) | copy-start | bytes 2457604
  12.1 3.2 %copy-start.7 = (f32[640]{0:T(1024)S(1)}, f32[640]{0:T(1024)}, u32[]{:S(2)}) copy-start(f32[640]{0:T(1024)} %tgain_ref.1) | copy-start | bytes 7684
  12.1 3.2 %copy-start.8 = (f32[640]{0:T(1024)S(1)}, f32[640]{0:T(1024)}, u32[]{:S(2)}) copy-start(f32[640]{0:T(1024)} %xgain_ref.1) | copy-start | bytes 7684
  15.2 9.1 %copy-start.5 = (bf16[2,2,77,640]{3,2,1,0:T(8,128)(2,1)S(1)}, bf16[2,2,77,640]{3,2,1,0:T(8,128)(2,1)}, u32[]{:S(2)}) copy-start(bf16[2,2,77,640]{3,2,1,0:T(8,128)(2,1)} %pages.1.own_ref) | copy-start | bytes 1182724
  15.2 9.1 %copy-start.9 = (bf16[640,640]{1,0:T(8,128)(2,1)S(1)}, bf16[640,640]{1,0:T(8,128)(2,1)}, u32[]{:S(2)}) copy-start(bf16[640,640]{1,0:T(8,128)(2,1)} %xo_ref.1) | copy-start | bytes 2457604
  15.2 9.0 %copy-start.12 = (s32[16]{0:T(128)S(1)}, s32[16]{0:T(128)}, u32[]{:S(2)}) copy-start(s32[16]{0:T(128)} %slot_ref.1) | copy-start | bytes 196
  15.3 9.0 %copy-start.13 = (s32[2]{0:T(128)S(1)}, s32[2]{0:T(128)}, u32[]{:S(2)}) copy-start(s32[2]{0:T(128)} %gate_ref.1) | copy-start | bytes 28

commit v4 on v3

--- a/solution.py
+++ b/solution.py
@@ -14,7 +14,7 @@
 F32 = jnp.float32
 BF16 = jnp.bfloat16
 NEG = -1e30
-COSTP, COST0, COST1, COST2, COST3 = 3 * 10**9, 16 * 10**9, 10**9, 10**9, 10**9
+COSTP, COST0, COST1, COST2, COST3 = 3 * 10**9, 16 * 10**9, 3 * 10**8, 6 * 10**9, 10**9
 
 
 def cost(flops):
@@ -37,8 +37,10 @@
     return lax.dot_general(a, b, (((1,), (1,)), ((), ())), preferred_element_type=F32)
 
 
-def pass_kernel(in_ref, out_ref):
-    pass
+def pages_kernel(pages_ref, half_ref, sem):
+    copy = pltpu.make_async_copy(pages_ref.at[1 - first_row()], half_ref, sem)
+    copy.start()
+    copy.wait()
 
 
 def first_row():
@@ -152,17 +154,18 @@
 
 
 def cross_kernel(
-    frames, slot_ref, gate_ref, after_ref, query_ref, own_ref, far_ref, xo_ref, out_ref, mixed
+    frames, slot_ref, gate_ref, after_ref, query_ref, own_ref, fetched_ref, swapped_ref, xo_ref, out_ref, mixed
 ):
     cols, slots, rows, _, width = after_ref.shape
     half = slots // 2
+    even = first_row() == 1
     first_page = lax.axis_index("req") * REQ_DEV
     for r in range(half):
         page = slot_ref[first_page + r]
         i = lax.rem(page, REQ_DEV)
         mine = page - i == first_page
-        k = jnp.where(mine, own_ref[0, i], far_ref[0, i])
-        v = jnp.where(mine, own_ref[1, i], far_ref[1, i])
+        k = jnp.where(mine, own_ref[0, i], jnp.where(even, fetched_ref[i], swapped_ref[i]))
+        v = jnp.where(mine, own_ref[1, i], jnp.where(even, swapped_ref[i], fetched_ref[i]))
         q = query_ref[:, r].reshape(cols * rows * PAD, width)
         for j in range(width // 128):
             ls = slice(j * 128, (j + 1) * 128)
@@ -198,16 +201,21 @@
     total = cols * slots * rows * PAD
     wide = cols * width
     raw = hidden_states.reshape((slots, rows, cols, frames, width)).transpose(0, 1, 3, 2, 4)
-    context_pages = pl.pallas_call(
-        pass_kernel,
-        out_shape=jax.ShapeDtypeStruct(context_pages.shape, BF16),
+    stored = context_pages.transpose(0, 2, 1, 3)
+    half = pl.pallas_call(
+        pages_kernel,
+        out_shape=jax.ShapeDtypeStruct(stored.shape[1:], BF16),
         in_specs=[any_],
-        out_specs=any_,
-        input_output_aliases={0: 0},
+        out_specs=vm,
+        scratch_shapes=[pltpu.SemaphoreType.DMA],
+        compiler_params=pltpu.CompilerParams(vmem_limit_bytes=8 << 20),
         cost_estimate=cost(COSTP),
         name="pages",
-    )(context_pages)
-    far_pages = lax.ppermute(context_pages, "req", partner_pairs)
+    )(stored)
+    fetched = lax.ppermute(half, "req", partner_pairs)
+    swapped = lax.ppermute(fetched, "strip", near_pairs)
+    fetched = fetched.transpose(1, 0, 2)
+    swapped = swapped.transpose(1, 0, 2)
     row = jax.ShapeDtypeStruct((slots, PAD, wide), BF16)
     whole = jax.ShapeDtypeStruct((slots, rows, PAD, wide), BF16)
     edge_x, edge_act = pl.pallas_call(
@@ -262,13 +270,13 @@
     out = pl.pallas_call(
         functools.partial(cross_kernel, frames),
         out_shape=jax.ShapeDtypeStruct((REQ_DEV, rows, PAD, cols * width), BF16),
-        in_specs=[sm, sm] + [vm] * 5,
+        in_specs=[sm, sm] + [vm] * 6,
         out_specs=vm,
         scratch_shapes=[pltpu.VMEM((cols, REQ_DEV, rows, PAD, width), BF16)],
         compiler_params=pltpu.CompilerParams(vmem_limit_bytes=8 << 20),
         cost_estimate=cost(COST3),
         name="cross_mix",
-    )(context_slot, gate, after, query, context_pages, far_pages, cross_out)
+    )(context_slot, gate, after, query, context_pages, fetched, swapped, cross_out)
     out = out[:, :, :frames].reshape(REQ_DEV, rows, frames, cols, width)
     return out.transpose(0, 1, 3, 2, 4)
 

time: 27.9 us -> 27.5 us (0.986)
  waiting for transfers between devices: 4.46 us -> 2.07 us
  starting transfers between devices: 6.26 us -> 8.63 us
  local copies, waits for them, and re-layouts: 2.7 us -> 1.98 us
  Pallas kernels: 14.1 us -> 14.4 us
    ppermute x1 -> x2, starting transfers between devices: 4.04 us -> 6.4 us  [the longest x1 4.1 us: on_device(): fetched = lax.ppermute(half, 'req', partner_pairs)]
    ppermute x1 -> x2, waiting for transfers between devices: 2.33 us -> 0.01 us  [the longest x1 0.01 us: on_device(): fetched = lax.ppermute(half, 'req', partner_pairs)]
    unnamed x33 -> x35, local copies, waits for them, and re-layouts: 1.88 us -> 1.13 us
  transfers between devices with their start and end apart: 3 -> 4, of which waited for: 2 -> 1; matrix products, arithmetic and copies ran while one was open for 0% -> 0% of each run, Pallas kernels for 41% -> 42%
where the time goes in v4:
time: 27.5 us; the launch traced here: 27.4 us
  Pallas kernels  14.4 us (52%)
  starting transfers between devices  8.63 us (31%)
  waiting for transfers between devices  2.07 us (8%)
  local copies, waits for them, and re-layouts  1.98 us (7%)
    pallas_call x1, Pallas kernels, on_device(): pl.pallas_call(functools.partial(time_kernel, frames), out_shape=(jax.Sha...  6.71 us
    ppermute x1, starting transfers between devices, on_device(): fetched = lax.ppermute(half, 'req', partner_pairs)  4.1 us
    pallas_call x1, Pallas kernels, on_device(): pl.pallas_call(conv_kernel, out_shape=jax.ShapeDtypeStruct((cols, slots,...  3.08 us
    pallas_call x1, Pallas kernels, on_device(): pl.pallas_call(functools.partial(cross_kernel, frames), out_shape=jax.Sha...  2.57 us
    ppermute x1, starting transfers between devices, on_device(): swapped = lax.ppermute(fetched, 'strip', near_pairs)  2.3 us
    ppermute x1, waiting for transfers between devices, on_device(): near = lax.ppermute(edge_act, 'strip', near_pairs)  2.06 us
    ppermute x1, starting transfers between devices, on_device(): near = lax.ppermute(edge_act, 'strip', near_pairs)  1.56 us
    pallas_call x1, Pallas kernels, on_device(): pl.pallas_call(act_kernel, out_shape=(whole, whole, row), in_specs=[vm] *...  1.36 us
  transfers between devices with their start and end apart: 4, of which 1 were waited for; matrix products, arithmetic and copies ran while one was open for 0% of the time, Pallas kernels for 42%

profile of v4, /device:TPU:0, one launch (start us, length us, event | category | flops | bytes accessed | tf_op | source)
XLA Modules:
  0.0 27.4 jit_solution(10684454942239842756)
XLA Ops:
  0.0 1.0 %copy-done = bf16[2,2,77,640]{3,1,2,0:T(2,128)(2,1)S(1)} copy-done((bf16[2,2,77,640]{3,1,2,0:T(2,128)(2,1)S(1)}, bf16[2,2,77,640]{3,1,2,0:T(2,128)(2,1)}, u32[]{:S(2)}) %copy-start) | copy-done | bytes 394264
  1.0 0.2 pages.1
  1.3 4.1 %collective-permute-start.2 = (bf16[77,2,640]{2,0,1:T(8,128)(2,1)S(1)}, bf16[77,2,640]{2,0,1:T(8,128)(2,1)S(1)}, u32[]{:S(2)}, u32[]{:S(2)}) collective-permute-start(bf16[77,2,640]{2,0,1:T(8,128)(2,1)S(1)} %copy.18), channel_id=1, source_target_pairs={{0,4},{1,5},{2,6},{3,7},{4,0},{5,1},{6,2},{7,3},{8,12},{9,13},{10,... | collective-permute-start | bytes 591368 | tf_op jit(solution)/shard_map/ppermute | solution.py:215
  5.4 0.5 %edge.1 = (bf16[4,16,1280]{2,1,0:T(8,128)(2,1)S(1)}, bf16[4,16,1280]{2,1,0:T(8,128)(2,1)S(1)}) custom-call(bf16[4,4,14,2,640]{4,3,2,1,0:T(2,128)(2,1)S(1)} %bitcast.13, f32[640]{0:T(1024)S(1)} %copy-done.10), custom_call_target="tpu_custom_call" | custom-call | flops 16000000000 | tf_op jit(solution)/shard_map/edge/pallas_call | solution.py:221
  5.9 0.0 copy-start.1
  5.9 0.0 copy-start.2
  5.9 1.6 %collective-permute-start = (bf16[4,16,1280]{2,1,0:T(8,128)(2,1)S(1)}, bf16[4,16,1280]{2,1,0:T(8,128)(2,1)S(1)}, u32[]{:S(2)}, u32[]{:S(2)}) collective-permute-start(bf16[4,16,1280]{2,1,0:T(8,128)(2,1)S(1)} %get-tuple-element.13.edge_act_ref), channel_id=1, source_target_pairs={{0,8},{8,0},{16,24},{24,16},{1,9},{9,1},{17,25},{25,17},{2,10},{10... | collective-permute-start | bytes 491528 | tf_op jit(solution)/shard_map/ppermute | solution.py:230
  7.5 1.4 %activate.1 = (bf16[4,4,16,1280]{3,2,1,0:T(8,128)(2,1)S(1)}, bf16[4,4,16,1280]{3,2,1,0:T(8,128)(2,1)S(1)}, bf16[4,16,1280]{2,1,0:T(8,128)(2,1)S(1)}) custom-call(bf16[4,4,14,2,640]{4,3,2,1,0:T(2,128)(2,1)S(1)} %bitcast.14, f32[640]{0:T(1024)S(1)} %copy-done.10, bf16[4,16,1280]{2,1,0:T(8,128)(2,1)S(1)} %get-tuple-element.12.edge_x_ref, ...), custom_call_target="tpu_custom_call" | custom-call | flops 300000000 | tf_op jit(solution)/shard_map/activate/pallas_call | solution.py:231
  8.8 0.7 %collective-permute-start.1 = (bf16[4,16,1280]{2,1,0:T(8,128)(2,1)S(1)}, bf16[4,16,1280]{2,1,0:T(8,128)(2,1)S(1)}, u32[]{:S(2)}, u32[]{:S(2)}) collective-permute-start(bf16[4,16,1280]{2,1,0:T(8,128)(2,1)S(1)} %get-tuple-element.16), channel_id=1, source_target_pairs={{8,16},{16,8},{9,17},{17,9},{10,18},{18,10},{11,19},{19,11},{12,20... | collective-permute-start | bytes 491528 | tf_op jit(solution)/shard_map/ppermute | solution.py:240
  9.6 2.1 %collective-permute-done.near_ref = bf16[4,16,1280]{2,1,0:T(8,128)(2,1)S(1)} collective-permute-done((bf16[4,16,1280]{2,1,0:T(8,128)(2,1)S(1)}, bf16[4,16,1280]{2,1,0:T(8,128)(2,1)S(1)}, u32[]{:S(2)}, u32[]{:S(2)}) %collective-permute-start) | collective-permute-done | bytes 163872 | tf_op jit(solution)/shard_map/ppermute | solution.py:230
  11.7 0.0 copy-start.3
  11.7 0.0 copy-start.4
  11.7 0.0 copy-start.5
  11.7 0.0 copy-start.6
  11.7 0.0 copy-start.7
  11.7 0.0 copy-start.11
  11.7 0.0 copy-start.12
  11.7 3.1 %conv_own.1.part_ref = f32[2,4,4,16,640]{4,3,2,1,0:T(8,128)S(1)} custom-call(bf16[4,4,16,1280]{3,2,1,0:T(8,128)(2,1)S(1)} %get-tuple-element.14.x_ref, bf16[4,4,16,1280]{3,2,1,0:T(8,128)(2,1)S(1)} %get-tuple-element.15.act_ref, bf16[4,16,1280]{2,1,0:T(8,128)(2,1)S(1)} %collective-permute-done.near_ref, bf16[3,3,640,640]{3,2,1,0:T(8,128)(2,1)S(1)} %bitcast.10, ...), custom_call_target="tpu_custom_call" | custom-call | flops 300000000 | tf_op jit(solution)/shard_map/conv_own/pallas_call | solution.py:241
  14.8 0.0 copy-start.8
  14.8 0.0 copy-start.13
  14.9 2.3 %collective-permute-start.3 = (bf16[77,2,640]{2,0,1:T(8,128)(2,1)S(1)}, bf16[77,2,640]{2,0,1:T(8,128)(2,1)S(1)}, u32[]{:S(2)}, u32[]{:S(2)}) collective-permute-start(bf16[77,2,640]{2,0,1:T(8,128)(2,1)S(1)} %collective-permute-done.2), channel_id=1, source_target_pairs={{0,8},{8,0},{16,24},{24,16},{1,9},{9,1},{17,25},{25,17},{2,10},{10... | collective-permute-start | bytes 591368 | tf_op jit(solution)/shard_map/ppermute | solution.py:216
  17.2 6.7 %time_mix.1 = (f32[2,4,4,16,640]{4,3,2,1,0:T(8,128)S(1)}, bf16[2,2,4,16,640]{4,3,2,1,0:T(8,128)(2,1)S(1)}) custom-call(f32[2,4,4,16,640]{4,3,2,1,0:T(8,128)S(1)} %conv_own.1.part_ref, bf16[4,16,1280]{2,1,0:T(8,128)(2,1)S(1)} %collective-permute-done.1.next_ref, bf16[3,3,640,640]{3,2,1,0:T(8,128)(2,1)S(1)} %bitcast.10, f32[640]{0:T(1024)S(1)} %copy-done.11, ...), custom_call_target="tpu_custom_call" | custom-call | flops 6000000000 | tf_op jit(solution)/shard_map/time_mix/pallas_call | solution.py:251
  24.0 2.6 %cross_mix.1 = bf16[2,4,16,1280]{3,2,1,0:T(8,128)(2,1)S(1)} custom-call(s32[16]{0:T(128)S(1)} %copy-done.13, s32[2]{0:T(128)S(1)} %copy-done.14, f32[2,4,4,16,640]{4,3,2,1,0:T(8,128)S(1)} %get-tuple-element.17.after_ref, bf16[2,2,4,16,640]{4,3,2,1,0:T(8,128)(2,1)S(1)} %get-tuple-element.18.query_ref, bf16[2,2,77,640]{3,2,1,0:T(8,128)(2,1)S(1)} %copy.19.own_ref, ...), custom_call_target="tpu_custom_call" | custom-call | flops 1000000000 | tf_op jit(solution)/shard_map/cross_mix/pallas_call | solution.py:270
  26.6 0.8 %reshape.8 = bf16[2,4,14,2,640]{4,3,2,1,0:T(2,128)(2,1)} reshape(bf16[2,4,14,1280]{3,2,1,0:T(8,128)(2,1)S(1)} %bitcast.12) | data formatting | bytes 573440 | tf_op jit(solution)/shard_map/reshape | solution.py:280
  (28 shorter events, 0.1 us)
Async XLA Ops:
  0.0 1.0 %copy-start = (bf16[2,2,77,640]{3,1,2,0:T(2,128)(2,1)S(1)}, bf16[2,2,77,640]{3,1,2,0:T(2,128)(2,1)}, u32[]{:S(2)}) copy-start(bf16[2,2,77,640]{3,1,2,0:T(2,128)(2,1)} %param.18) | copy-start | bytes 1182724
  1.0 4.4 %copy-start.9 = (bf16[2,2,4,2,14,640]{5,3,4,2,1,0:T(2,128)(2,1)S(1)}, bf16[2,2,4,2,14,640]{5,3,4,2,1,0:T(2,128)(2,1)}, u32[]{:S(2)}) copy-start(bf16[2,2,4,2,14,640]{5,3,4,2,1,0:T(2,128)(2,1)} %param.15) | copy-start | bytes 1720324
  1.0 4.4 %copy-start.10 = (f32[640]{0:T(1024)S(1)}, f32[640]{0:T(1024)}, u32[]{:S(2)}) copy-start(f32[640]{0:T(1024)} %gain_ref.3) | copy-start | bytes 7684
  1.3 13.6 %collective-permute-start.2 = (bf16[77,2,640]{2,0,1:T(8,128)(2,1)S(1)}, bf16[77,2,640]{2,0,1:T(8,128)(2,1)S(1)}, u32[]{:S(2)}, u32[]{:S(2)}) collective-permute-start(bf16[77,2,640]{2,0,1:T(8,128)(2,1)S(1)} %copy.18), channel_id=1, source_target_pairs={{0,4},{1,5},{2,6},{3,7},{4,0},{5,1},{6,2},{7,3},{8,12},{9,13},{10,... | collective-permute-start | bytes 591368 | tf_op jit(solution)/shard_map/ppermute | solution.py:215
  5.4 6.2 %slice-start = ((s8[7372800]{0:T(1024)(128)(4,1)}), s8[4194304]{0:T(1024)(128)(4,1)S(1)}, s32[]{:S(2)}) async-start(s8[7372800]{0:T(1024)(128)(4,1)} %bitcast.9), calls=%async_computation | async-start | bytes 8388608
  5.4 6.2 %slice-start.1 = ((s8[7372800]{0:T(1024)(128)(4,1)}), s8[3178496]{0:T(1024)(128)(4,1)S(1)}, s32[]{:S(2)}) async-start(s8[7372800]{0:T(1024)(128)(4,1)} %bitcast.9), calls=%async_computation.1 | async-start | bytes 6356992
  5.9 3.6 %copy-start.1 = (bf16[2,2,77,640]{3,1,2,0:T(2,128)(2,1)S(1)}, bf16[2,2,77,640]{3,1,2,0:T(2,128)(2,1)}, u32[]{:S(2)}) copy-start(bf16[2,2,77,640]{3,1,2,0:T(2,128)(2,1)} %param.18) | copy-start | bytes 1182724
  5.9 5.7 %copy-start.2 = (f32[640]{0:T(1024)S(1)}, f32[640]{0:T(1024)}, u32[]{:S(2)}) copy-start(f32[640]{0:T(1024)} %bias_ref.1) | copy-start | bytes 7684
  5.9 5.7 %collective-permute-start = (bf16[4,16,1280]{2,1,0:T(8,128)(2,1)S(1)}, bf16[4,16,1280]{2,1,0:T(8,128)(2,1)S(1)}, u32[]{:S(2)}, u32[]{:S(2)}) collective-permute-start(bf16[4,16,1280]{2,1,0:T(8,128)(2,1)S(1)} %get-tuple-element.13.edge_act_ref), channel_id=1, source_target_pairs={{0,8},{8,0},{16,24},{24,16},{1,9},{9,1},{17,25},{25,17},{2,10},{10... | collective-permute-start | bytes 491528 | tf_op jit(solution)/shard_map/ppermute | solution.py:230
  8.8 8.3 %collective-permute-start.1 = (bf16[4,16,1280]{2,1,0:T(8,128)(2,1)S(1)}, bf16[4,16,1280]{2,1,0:T(8,128)(2,1)S(1)}, u32[]{:S(2)}, u32[]{:S(2)}) collective-permute-start(bf16[4,16,1280]{2,1,0:T(8,128)(2,1)S(1)} %get-tuple-element.16), channel_id=1, source_target_pairs={{8,16},{16,8},{9,17},{17,9},{10,18},{18,10},{11,19},{19,11},{12,20... | collective-permute-start | bytes 491528 | tf_op jit(solution)/shard_map/ppermute | solution.py:240
  11.7 5.5 %copy-start.3 = (bf16[640,640]{1,0:T(8,128)(2,1)S(1)}, bf16[640,640]{1,0:T(8,128)(2,1)}, u32[]{:S(2)}) copy-start(bf16[640,640]{1,0:T(8,128)(2,1)} %wq_ref.1) | copy-start | bytes 2457604
  11.7 5.5 %copy-start.4 = (bf16[640,640]{1,0:T(8,128)(2,1)S(1)}, bf16[640,640]{1,0:T(8,128)(2,1)}, u32[]{:S(2)}) copy-start(bf16[640,640]{1,0:T(8,128)(2,1)} %wk_ref.1) | copy-start | bytes 2457604
  11.7 5.5 %copy-start.5 = (bf16[640,640]{1,0:T(8,128)(2,1)S(1)}, bf16[640,640]{1,0:T(8,128)(2,1)}, u32[]{:S(2)}) copy-start(bf16[640,640]{1,0:T(8,128)(2,1)} %wv_ref.1) | copy-start | bytes 2457604
  11.7 5.5 %copy-start.6 = (bf16[640,640]{1,0:T(8,128)(2,1)S(1)}, bf16[640,640]{1,0:T(8,128)(2,1)}, u32[]{:S(2)}) copy-start(bf16[640,640]{1,0:T(8,128)(2,1)} %wo_ref.1) | copy-start | bytes 2457604
  11.7 5.5 %copy-start.7 = (bf16[640,640]{1,0:T(8,128)(2,1)S(1)}, bf16[640,640]{1,0:T(8,128)(2,1)}, u32[]{:S(2)}) copy-start(bf16[640,640]{1,0:T(8,128)(2,1)} %xq_ref.1) | copy-start | bytes 2457604
  11.7 5.5 %copy-start.11 = (f32[640]{0:T(1024)S(1)}, f32[640]{0:T(1024)}, u32[]{:S(2)}) copy-start(f32[640]{0:T(1024)} %tgain_ref.1) | copy-start | bytes 7684
  11.7 5.5 %copy-start.12 = (f32[640]{0:T(1024)S(1)}, f32[640]{0:T(1024)}, u32[]{:S(2)}) copy-start(f32[640]{0:T(1024)} %xgain_ref.1) | copy-start | bytes 7684
  14.8 9.1 %copy-start.8 = (bf16[640,640]{1,0:T(8,128)(2,1)S(1)}, bf16[640,640]{1,0:T(8,128)(2,1)}, u32[]{:S(2)}) copy-start(bf16[640,640]{1,0:T(8,128)(2,1)} %xo_ref.1) | copy-start | bytes 2457604
  14.8 9.1 %copy-start.13 = (s32[16]{0:T(128)S(1)}, s32[16]{0:T(128)}, u32[]{:S(2)}) copy-start(s32[16]{0:T(128)} %slot_ref.1) | copy-start | bytes 196
  14.8 9.1 %copy-start.14 = (s32[2]{0:T(128)S(1)}, s32[2]{0:T(128)}, u32[]{:S(2)}) copy-start(s32[2]{0:T(128)} %gate_ref.1) | copy-start | bytes 28
  14.9 9.1 %collective-permute-start.3 = (bf16[77,2,640]{2,0,1:T(8,128)(2,1)S(1)}, bf16[77,2,640]{2,0,1:T(8,128)(2,1)S(1)}, u32[]{:S(2)}, u32[]{:S(2)}) collective-permute-start(bf16[77,2,640]{2,0,1:T(8,128)(2,1)S(1)} %collective-permute-done.2), channel_id=1, source_target_pairs={{0,8},{8,0},{16,24},{24,16},{1,9},{9,1},{17,25},{25,17},{2,10},{10... | collective-permute-start | bytes 591368 | tf_op jit(solution)/shard_map/ppermute | solution.py:216

commit v5 on v4

--- a/solution.py
+++ b/solution.py
@@ -90,75 +90,85 @@
     )
     inner = ext[:, pl.ds(2 - side // 2, rows - 1)].reshape(-1, wide)
     inner_rows = pl.ds(side // 2, rows - 1)
+    weights = jnp.concatenate([pair_taps(w_ref, 1), pair_taps(w_ref, side)], axis=0)
+    mid = dot(both, weights)
+    rest = dot(inner, pair_taps(w_ref, 2 - side))
     for c in range(2):
-        taps = pl.ds(1 - c, 2)
-        weights = jnp.concatenate(
-            [w_ref[1, taps].reshape(wide, width), w_ref[side, taps].reshape(wide, width)], axis=0
+        ls = slice(c * width, (c + 1) * width)
+        out_ref[c] = (
+            x_ref[:, :, :, ls].astype(F32) + bias_ref[...].reshape(1, 1, 1, width) + mid[:, ls].reshape(slots, rows, PAD, width)
         )
-        mid = dot(both, weights).reshape(slots, rows, PAD, width)
-        out_ref[c] = x_ref[:, :, :, c * width : (c + 1) * width].astype(F32) + bias_ref[...].reshape(1, 1, 1, width) + mid
-        rest = dot(inner, w_ref[2 - side, taps].reshape(wide, width))
-        out_ref[c, :, inner_rows] += rest.reshape(slots, rows - 1, PAD, width)
-
-
-def two_heads(q, k, v, mask, frames_scale):
-    m = q.shape[0]
-    n = k.shape[0]
-    lane = lax.broadcasted_iota(jnp.int32, (m, 2 * HEAD_DIM), 1)
-    first = lane < HEAD_DIM
-    zero = jnp.zeros_like(q)
-    stacked = jnp.concatenate([jnp.where(first, q, zero), jnp.where(first, zero, q)], axis=0)
-    s = dot_t(stacked, k)
-    if mask is not None:
-        s = s + mask
-    top = jnp.max(s, axis=-1, keepdims=True)
-    p = jnp.exp2((s - top) * frames_scale).astype(BF16)
-    both = dot(p, jnp.concatenate([v, jnp.ones((n, 2 * HEAD_DIM), BF16)], axis=1))
-    d = 2 * HEAD_DIM
-    num = jnp.where(first, both[:m, :d], both[m:, :d])
-    den = jnp.where(first, both[:m, d:], both[m:, d:])
-    return (num / den).astype(BF16)
+        out_ref[c, :, inner_rows] += rest[:, ls].reshape(slots, rows - 1, PAD, width)
+
+
+def pair_taps(w_ref, dr):
+    wide = 2 * w_ref.shape[2]
+    return jnp.concatenate([w_ref[dr, 1 - c : 3 - c].reshape(wide, wide // 2) for c in range(2)], axis=1)
+
+
+def apart(x):
+    first = lax.broadcasted_iota(jnp.int32, x.shape, 1) < HEAD_DIM
+    zero = jnp.zeros_like(x)
+    return jnp.concatenate([jnp.where(first, x, zero), jnp.where(first, zero, x)], axis=0)
 
 
 def time_kernel(
     frames, part_ref, next_ref, w_ref, tgain_ref, wq_ref, wk_ref, wv_ref, wo_ref,
-    xgain_ref, xq_ref, after_ref, query_ref, normed, tq, tk, tv, mixed, mask
+    xgain_ref, xq_ref, after_ref, query_ref, normed, tq, tk, tv, mixed, scores, chances
 ):
     cols, slots, rows, _, width = part_ref.shape
     wide = 2 * width
     half = slots // 2
     total = cols * slots * rows * PAD
-    block = half * rows * PAD
     side = 1 - first_row()
     other = next_ref[...].reshape(-1, wide)
+    add = dot(other, pair_taps(w_ref, 2 * side))
     for c in range(2):
-        after_ref[c] = part_ref[c]
-        add = dot(other, w_ref[2 * side, pl.ds(1 - c, 2)].reshape(wide, width))
-        after_ref[c, :, side * (rows - 1)] += add.reshape(slots, PAD, width)
-    normed[...] = rms(after_ref[...].reshape(total, width), tgain_ref[...]).astype(BF16)
-    tq[...] = dot(normed[...], wq_ref[...]).astype(BF16)
-    tk[...] = dot(normed[...], wk_ref[...]).astype(BF16)
-    tv[...] = dot(normed[...], wv_ref[...]).astype(BF16)
-    row = lax.broadcasted_iota(jnp.int32, (2 * block, block), 0) % block
-    col = lax.broadcasted_iota(jnp.int32, (2 * block, block), 1)
-    mask[...] = jnp.where((row // PAD == col // PAD) & (col % PAD < frames), 0.0, NEG).astype(F32)
-    for b in range(total // block):
-        rs = slice(b * block, (b + 1) * block)
-        for j in range(width // 128):
-            ls = slice(j * 128, (j + 1) * 128)
-            mixed[rs, ls] = two_heads(tq[rs, ls], tk[rs, ls], tv[rs, ls], mask[...], 0.125 * LOG2E)
-    after_ref[...] += dot(mixed[...], wo_ref[...]).reshape(after_ref.shape)
-    for c in range(2):
-        nc = rms(after_ref[c, :half].reshape(block, width), xgain_ref[...]).astype(BF16)
-        query_ref[c] = dot(nc, xq_ref[...]).astype(BF16).reshape(half, rows, PAD, width)
+        part_ref[c, :, side * (rows - 1)] += add[:, c * width : (c + 1) * width].reshape(slots, PAD, width)
+    normed[...] = rms(part_ref[...].reshape(total, width), tgain_ref[...]).astype(BF16)
+    every = dot(normed[...], jnp.concatenate([wq_ref[...], wk_ref[...], wv_ref[...]], axis=1))
+    for i, part in enumerate((tq, tk, tv)):
+        part[...] = every[:, i * width : (i + 1) * width].astype(BF16)
+    group = rows * PAD
+    pair = 2 * HEAD_DIM
+    row = lax.broadcasted_iota(jnp.int32, (group, 2 * group), 0)
+    col = lax.rem(lax.broadcasted_iota(jnp.int32, (group, 2 * group), 1), group)
+    mask = jnp.where((row // PAD == col // PAD) & (lax.rem(col, PAD) < frames), 0.0, NEG).astype(F32)
+    first = lax.broadcasted_iota(jnp.int32, (group, 2 * group), 1) < group
+    ones = apart(jnp.ones((group, pair), BF16))
+    tiles = [
+        (slice(g * group, (g + 1) * group), slice(j * pair, (j + 1) * pair))
+        for g in range(total // group)
+        for j in range(width // pair)
+    ]
+    for rs, ls in tiles:
+        scores[rs, ls] = dot_t(tq[rs, ls], apart(tk[rs, ls]))
+    for rs, ls in tiles:
+        s = scores[rs, ls] + mask
+        top = jnp.where(
+            first,
+            jnp.max(jnp.where(first, s, NEG), axis=-1, keepdims=True),
+            jnp.max(jnp.where(first, NEG, s), axis=-1, keepdims=True),
+        )
+        chances[rs, ls] = jnp.exp2((s - top) * (0.125 * LOG2E)).astype(BF16)
+    for rs, ls in tiles:
+        out = dot(chances[rs, ls], jnp.concatenate([apart(tv[rs, ls]), ones], axis=1))
+        mixed[rs, ls] = (out[:, :pair] / out[:, pair:]).astype(BF16)
+    after_ref[...] = part_ref[...] + dot(mixed[...], wo_ref[...]).reshape(after_ref.shape)
+    nc = rms(after_ref[:, :half], xgain_ref[...]).astype(BF16).reshape(-1, width)
+    query_ref[...] = dot(nc, xq_ref[...]).astype(BF16).reshape(query_ref.shape)
 
 
 def cross_kernel(
-    frames, slot_ref, gate_ref, after_ref, query_ref, own_ref, fetched_ref, swapped_ref, xo_ref, out_ref, mixed
+    frames, slot_ref, gate_ref, after_ref, query_ref, own_ref, fetched_ref, swapped_ref, xo_ref, out_ref, keys, values, scores, chances, mixed
 ):
     cols, slots, rows, _, width = after_ref.shape
     half = slots // 2
     even = first_row() == 1
+    tokens = own_ref.shape[2]
+    room = -(-tokens // 128) * 128
+    group = cols * rows * PAD
+    pair = 2 * HEAD_DIM
     first_page = lax.axis_index("req") * REQ_DEV
     for r in range(half):
         page = slot_ref[first_page + r]
@@ -166,17 +176,27 @@
         mine = page - i == first_page
         k = jnp.where(mine, own_ref[0, i], jnp.where(even, fetched_ref[i], swapped_ref[i]))
         v = jnp.where(mine, own_ref[1, i], jnp.where(even, swapped_ref[i], fetched_ref[i]))
-        q = query_ref[:, r].reshape(cols * rows * PAD, width)
-        for j in range(width // 128):
-            ls = slice(j * 128, (j + 1) * 128)
-            out = two_heads(q[:, ls], k[:, ls], v[:, ls], None, 0.125 * LOG2E)
-            mixed[:, r, :, :, ls] = out.reshape(cols, rows, PAD, 128)
+        tail = jnp.zeros((room - tokens, width), BF16)
+        keys[r] = jnp.concatenate([k, tail], axis=0)
+        values[r] = jnp.concatenate([v, tail], axis=0)
+    tiles = [(r, slice(j * pair, (j + 1) * pair), slice(2 * j * room, 2 * (j + 1) * room)) for r in range(half) for j in range(width // pair)]
+    live = lax.rem(lax.broadcasted_iota(jnp.int32, (group, 2 * room), 1), room) < tokens
+    ones = apart(jnp.ones((room, pair), BF16))
+    for r, ls, ks in tiles:
+        scores[r, :, ks] = dot_t(query_ref[:, r, :, :, ls].reshape(group, pair), apart(keys[r, :, ls]))
+    for r, ls, ks in tiles:
+        s = jnp.where(live, scores[r, :, ks], NEG)
+        p = [jnp.exp2((t - jnp.max(t, axis=-1, keepdims=True)) * (0.125 * LOG2E)) for t in (s[:, :room], s[:, room:])]
+        chances[r, :, ks] = jnp.concatenate(p, axis=1).astype(BF16)
+    for r, ls, ks in tiles:
+        out = dot(chances[r, :, ks], jnp.concatenate([apart(values[r, :, ls]), ones], axis=1))
+        mixed[:, r, :, :, ls] = (out[:, :pair] / out[:, pair:]).astype(BF16).reshape(cols, rows, PAD, pair)
     frame = lax.broadcasted_iota(jnp.int32, (rows, PAD, width), 1).astype(F32)
     scale = 1.0 + 2.0 * frame / (frames - 1)
+    add = dot(mixed[...].reshape(-1, width), xo_ref[...]).reshape(cols, half, rows, PAD, width)
     for c in range(cols):
-        add = dot(mixed[c].reshape(-1, width), xo_ref[...]).reshape(half, rows, PAD, width)
         for r in range(half):
-            cond = (after_ref[c, r] + add[r]).astype(BF16).astype(F32)
+            cond = (after_ref[c, r] + add[c, r]).astype(BF16).astype(F32)
             uncond = after_ref[c, half + r].astype(BF16).astype(F32)
             guided = jnp.where(gate_ref[r] == 1, uncond + scale * (cond - uncond), cond)
             out_ref[r, :, :, c * width : (c + 1) * width] = guided.astype(BF16)
@@ -200,6 +220,7 @@
     any_ = pl.BlockSpec(memory_space=pl.ANY)
     total = cols * slots * rows * PAD
     wide = cols * width
+    room = -(-context_pages.shape[2] // 128) * 128
     raw = hidden_states.reshape((slots, rows, cols, frames, width)).transpose(0, 1, 3, 2, 4)
     stored = context_pages.transpose(0, 2, 1, 3)
     half = pl.pallas_call(
@@ -257,9 +278,8 @@
         in_specs=[vm] * 10,
         out_specs=(vm, vm),
         scratch_shapes=[pltpu.VMEM((total, width), BF16)] * 5
-        + [
-            pltpu.VMEM((slots * rows * PAD, slots * rows * PAD // 2), F32),
-        ],
+        + [pltpu.VMEM((total, width // HEAD_DIM * rows * PAD), kind) for kind in (F32, BF16)],
+        input_output_aliases={0: 0},
         compiler_params=pltpu.CompilerParams(vmem_limit_bytes=16 << 20),
         cost_estimate=cost(COST2),
         name="time_mix",
@@ -272,8 +292,13 @@
         out_shape=jax.ShapeDtypeStruct((REQ_DEV, rows, PAD, cols * width), BF16),
         in_specs=[sm, sm] + [vm] * 6,
         out_specs=vm,
-        scratch_shapes=[pltpu.VMEM((cols, REQ_DEV, rows, PAD, width), BF16)],
-        compiler_params=pltpu.CompilerParams(vmem_limit_bytes=8 << 20),
+        scratch_shapes=[pltpu.VMEM((REQ_DEV, room, width), BF16)] * 2
+        + [
+            pltpu.VMEM((REQ_DEV, cols * rows * PAD, width // HEAD_DIM * room), F32),
+            pltpu.VMEM((REQ_DEV, cols * rows * PAD, width // HEAD_DIM * room), BF16),
+            pltpu.VMEM((cols, REQ_DEV, rows, PAD, width), BF16),
+        ],
+        compiler_params=pltpu.CompilerParams(vmem_limit_bytes=16 << 20),
         cost_estimate=cost(COST3),
         name="cross_mix",
     )(context_slot, gate, after, query, context_pages, fetched, swapped, cross_out)

time: 27.5 us -> 24.9 us (0.905)
  Pallas kernels: 14.4 us -> 11.8 us
  starting transfers between devices: 8.63 us -> 8.28 us
  waiting for transfers between devices: 2.07 us -> 2.4 us
    pallas_call x1, Pallas kernels: 6.71 us -> 5.28 us  [on_device(): pl.pallas_call(functools.partial(time_kernel, frames), out_shape=(jax.Sha...]
    pallas_call x1, Pallas kernels: 2.57 us -> 1.72 us  [on_device(): pl.pallas_call(functools.partial(cross_kernel, frames), out_shape=jax.Sha...]
    ppermute x1, starting transfers between devices: 2.3 us -> 1.95 us  [on_device(): swapped = lax.ppermute(fetched, 'strip', near_pairs)]
    pallas_call x1, Pallas kernels: 3.08 us -> 2.74 us  [on_device(): pl.pallas_call(conv_kernel, out_shape=jax.ShapeDtypeStruct((cols, slots,...]
    ppermute x1, waiting for transfers between devices: 0.01 us -> 0.33 us  [on_device(): fetched = lax.ppermute(half, 'req', partner_pairs)]
  transfers between devices with their start and end apart: 4 -> 4, of which waited for: 1 -> 2; matrix products, arithmetic and copies ran while one was open for 0% -> 0% of each run, Pallas kernels for 42% -> 40%
where the time goes in v5:
time: 24.9 us; the launch traced here: 24.7 us
  Pallas kernels  11.8 us (47%)
  starting transfers between devices  8.28 us (33%)
  waiting for transfers between devices  2.4 us (10%)
  local copies, waits for them, and re-layouts  1.98 us (8%)
  between operations  0.26 us (1%)
    pallas_call x1, Pallas kernels, on_device(): pl.pallas_call(functools.partial(time_kernel, frames), out_shape=(jax.Sha...  5.28 us
    ppermute x1, starting transfers between devices, on_device(): fetched = lax.ppermute(half, 'req', partner_pairs)  4.1 us
    pallas_call x1, Pallas kernels, on_device(): pl.pallas_call(conv_kernel, out_shape=jax.ShapeDtypeStruct((cols, slots,...  2.74 us
    ppermute x1, waiting for transfers between devices, on_device(): near = lax.ppermute(edge_act, 'strip', near_pairs)  2.06 us
    ppermute x1, starting transfers between devices, on_device(): swapped = lax.ppermute(fetched, 'strip', near_pairs)  1.95 us
    pallas_call x1, Pallas kernels, on_device(): pl.pallas_call(functools.partial(cross_kernel, frames), out_shape=jax.Sha...  1.72 us
    ppermute x1, starting transfers between devices, on_device(): near = lax.ppermute(edge_act, 'strip', near_pairs)  1.56 us
    pallas_call x1, Pallas kernels, on_device(): pl.pallas_call(act_kernel, out_shape=(whole, whole, row), in_specs=[vm] *...  1.36 us
  transfers between devices with their start and end apart: 4, of which 2 were waited for; matrix products, arithmetic and copies ran while one was open for 0% of the time, Pallas kernels for 40%

profile of v5, /device:TPU:0, one launch (start us, length us, event | category | flops | bytes accessed | tf_op | source)
XLA Modules:
  0.0 24.7 jit_solution(15730490092579641010)
XLA Ops:
  0.0 1.0 %copy-done = bf16[2,2,77,640]{3,1,2,0:T(2,128)(2,1)S(1)} copy-done((bf16[2,2,77,640]{3,1,2,0:T(2,128)(2,1)S(1)}, bf16[2,2,77,640]{3,1,2,0:T(2,128)(2,1)}, u32[]{:S(2)}) %copy-start) | copy-done | bytes 394264
  1.0 0.2 pages.1
  1.3 4.1 %collective-permute-start.2 = (bf16[77,2,640]{2,0,1:T(8,128)(2,1)S(1)}, bf16[77,2,640]{2,0,1:T(8,128)(2,1)S(1)}, u32[]{:S(2)}, u32[]{:S(2)}) collective-permute-start(bf16[77,2,640]{2,0,1:T(8,128)(2,1)S(1)} %copy.19), channel_id=1, source_target_pairs={{0,4},{1,5},{2,6},{3,7},{4,0},{5,1},{6,2},{7,3},{8,12},{9,13},{10,... | collective-permute-start | bytes 591368 | tf_op jit(solution)/shard_map/ppermute | solution.py:236
  5.4 0.5 %edge.1 = (bf16[4,16,1280]{2,1,0:T(8,128)(2,1)S(1)}, bf16[4,16,1280]{2,1,0:T(8,128)(2,1)S(1)}) custom-call(bf16[4,4,14,2,640]{4,3,2,1,0:T(2,128)(2,1)S(1)} %bitcast.13, f32[640]{0:T(1024)S(1)} %copy-done.10), custom_call_target="tpu_custom_call" | custom-call | flops 16000000000 | tf_op jit(solution)/shard_map/edge/pallas_call | solution.py:242
  5.9 0.0 copy-start.1
  5.9 0.0 copy-start.2
  5.9 1.6 %collective-permute-start = (bf16[4,16,1280]{2,1,0:T(8,128)(2,1)S(1)}, bf16[4,16,1280]{2,1,0:T(8,128)(2,1)S(1)}, u32[]{:S(2)}, u32[]{:S(2)}) collective-permute-start(bf16[4,16,1280]{2,1,0:T(8,128)(2,1)S(1)} %get-tuple-element.13.edge_act_ref), channel_id=1, source_target_pairs={{0,8},{8,0},{16,24},{24,16},{1,9},{9,1},{17,25},{25,17},{2,10},{10... | collective-permute-start | bytes 491528 | tf_op jit(solution)/shard_map/ppermute | solution.py:251
  7.5 1.4 %activate.1 = (bf16[4,4,16,1280]{3,2,1,0:T(8,128)(2,1)S(1)}, bf16[4,4,16,1280]{3,2,1,0:T(8,128)(2,1)S(1)}, bf16[4,16,1280]{2,1,0:T(8,128)(2,1)S(1)}) custom-call(bf16[4,4,14,2,640]{4,3,2,1,0:T(2,128)(2,1)S(1)} %bitcast.14, f32[640]{0:T(1024)S(1)} %copy-done.10, bf16[4,16,1280]{2,1,0:T(8,128)(2,1)S(1)} %get-tuple-element.12.edge_x_ref, ...), custom_call_target="tpu_custom_call" | custom-call | flops 300000000 | tf_op jit(solution)/shard_map/activate/pallas_call | solution.py:252
  8.8 0.7 %collective-permute-start.1 = (bf16[4,16,1280]{2,1,0:T(8,128)(2,1)S(1)}, bf16[4,16,1280]{2,1,0:T(8,128)(2,1)S(1)}, u32[]{:S(2)}, u32[]{:S(2)}) collective-permute-start(bf16[4,16,1280]{2,1,0:T(8,128)(2,1)S(1)} %get-tuple-element.16), channel_id=1, source_target_pairs={{8,16},{16,8},{9,17},{17,9},{10,18},{18,10},{11,19},{19,11},{12,20... | collective-permute-start | bytes 491528 | tf_op jit(solution)/shard_map/ppermute | solution.py:261
  9.6 2.1 %collective-permute-done.near_ref = bf16[4,16,1280]{2,1,0:T(8,128)(2,1)S(1)} collective-permute-done((bf16[4,16,1280]{2,1,0:T(8,128)(2,1)S(1)}, bf16[4,16,1280]{2,1,0:T(8,128)(2,1)S(1)}, u32[]{:S(2)}, u32[]{:S(2)}) %collective-permute-start) | collective-permute-done | bytes 163872 | tf_op jit(solution)/shard_map/ppermute | solution.py:251
  11.7 0.0 copy-start.3
  11.7 0.0 copy-start.4
  11.7 0.0 copy-start.5
  11.7 0.0 copy-start.6
  11.7 0.0 copy-start.7
  11.7 0.0 copy-start.12
  11.7 2.7 %conv_own.1.part_ref = f32[2,4,4,16,640]{4,3,2,1,0:T(8,128)S(1)} custom-call(bf16[4,4,16,1280]{3,2,1,0:T(8,128)(2,1)S(1)} %get-tuple-element.14.x_ref, bf16[4,4,16,1280]{3,2,1,0:T(8,128)(2,1)S(1)} %get-tuple-element.15.act_ref, bf16[4,16,1280]{2,1,0:T(8,128)(2,1)S(1)} %collective-permute-done.near_ref, bf16[3,3,640,640]{3,2,1,0:T(8,128)(2,1)S(1)} %bitcast.10, ...), custom_call_target="tpu_custom_call" | custom-call | flops 300000000 | tf_op jit(solution)/shard_map/conv_own/pallas_call | solution.py:262
  14.5 0.0 copy-start.8
  14.5 0.0 copy-start.14
  14.5 0.3 %collective-permute-done.2 = bf16[77,2,640]{2,0,1:T(8,128)(2,1)S(1)} collective-permute-done((bf16[77,2,640]{2,0,1:T(8,128)(2,1)S(1)}, bf16[77,2,640]{2,0,1:T(8,128)(2,1)S(1)}, u32[]{:S(2)}, u32[]{:S(2)}) %collective-permute-start.2) | collective-permute-done | bytes 197152 | tf_op jit(solution)/shard_map/ppermute | solution.py:236
  14.9 1.9 %collective-permute-start.3 = (bf16[77,2,640]{2,0,1:T(8,128)(2,1)S(1)}, bf16[77,2,640]{2,0,1:T(8,128)(2,1)S(1)}, u32[]{:S(2)}, u32[]{:S(2)}) collective-permute-start(bf16[77,2,640]{2,0,1:T(8,128)(2,1)S(1)} %collective-permute-done.2), channel_id=1, source_target_pairs={{0,8},{8,0},{16,24},{24,16},{1,9},{9,1},{17,25},{25,17},{2,10},{10... | collective-permute-start | bytes 591368 | tf_op jit(solution)/shard_map/ppermute | solution.py:237
  16.9 5.3 %time_mix.1 = (f32[2,4,4,16,640]{4,3,2,1,0:T(8,128)S(1)}, bf16[2,2,4,16,640]{4,3,2,1,0:T(8,128)(2,1)S(1)}) custom-call(f32[2,4,4,16,640]{4,3,2,1,0:T(8,128)S(1)} %conv_own.1.part_ref, bf16[4,16,1280]{2,1,0:T(8,128)(2,1)S(1)} %collective-permute-done.1.next_ref, bf16[3,3,640,640]{3,2,1,0:T(8,128)(2,1)S(1)} %bitcast.10, ...), custom_call_target="tpu_custom_call", output_to_operand_aliasing={{0}: (0, {})} | custom-call | flops 6000000000 | tf_op jit(solution)/shard_map/time_mix/pallas_call | solution.py:272
  22.2 1.7 %cross_mix.1 = bf16[2,4,16,1280]{3,2,1,0:T(8,128)(2,1)S(1)} custom-call(s32[16]{0:T(128)S(1)} %copy-done.13, s32[2]{0:T(128)S(1)} %copy-done.14, f32[2,4,4,16,640]{4,3,2,1,0:T(8,128)S(1)} %get-tuple-element.17.after_ref, bf16[2,2,4,16,640]{4,3,2,1,0:T(8,128)(2,1)S(1)} %get-tuple-element.18.query_ref, bf16[2,2,77,640]{3,2,1,0:T(8,128)(2,1)S(1)} %copy.20.own_ref, ...), custom_call_target="tpu_custom_call" | custom-call | flops 1000000000 | tf_op jit(solution)/shard_map/cross_mix/pallas_call | solution.py:290
  23.9 0.8 %reshape.8 = bf16[2,4,14,2,640]{4,3,2,1,0:T(2,128)(2,1)} reshape(bf16[2,4,14,1280]{3,2,1,0:T(8,128)(2,1)S(1)} %bitcast.12) | data formatting | bytes 573440 | tf_op jit(solution)/shard_map/reshape | solution.py:305
  (28 shorter events, 0.1 us)
Async XLA Ops:
  0.0 1.0 %copy-start = (bf16[2,2,77,640]{3,1,2,0:T(2,128)(2,1)S(1)}, bf16[2,2,77,640]{3,1,2,0:T(2,128)(2,1)}, u32[]{:S(2)}) copy-start(bf16[2,2,77,640]{3,1,2,0:T(2,128)(2,1)} %param.18) | copy-start | bytes 1182724
  1.0 4.4 %copy-start.9 = (bf16[2,2,4,2,14,640]{5,3,4,2,1,0:T(2,128)(2,1)S(1)}, bf16[2,2,4,2,14,640]{5,3,4,2,1,0:T(2,128)(2,1)}, u32[]{:S(2)}) copy-start(bf16[2,2,4,2,14,640]{5,3,4,2,1,0:T(2,128)(2,1)} %param.15) | copy-start | bytes 1720324
  1.0 4.4 %copy-start.10 = (f32[640]{0:T(1024)S(1)}, f32[640]{0:T(1024)}, u32[]{:S(2)}) copy-start(f32[640]{0:T(1024)} %gain_ref.3) | copy-start | bytes 7684
  1.3 13.6 %collective-permute-start.2 = (bf16[77,2,640]{2,0,1:T(8,128)(2,1)S(1)}, bf16[77,2,640]{2,0,1:T(8,128)(2,1)S(1)}, u32[]{:S(2)}, u32[]{:S(2)}) collective-permute-start(bf16[77,2,640]{2,0,1:T(8,128)(2,1)S(1)} %copy.19), channel_id=1, source_target_pairs={{0,4},{1,5},{2,6},{3,7},{4,0},{5,1},{6,2},{7,3},{8,12},{9,13},{10,... | collective-permute-start | bytes 591368 | tf_op jit(solution)/shard_map/ppermute | solution.py:236
  5.4 6.2 %slice-start = ((s8[7372800]{0:T(1024)(128)(4,1)}), s8[4194304]{0:T(1024)(128)(4,1)S(1)}, s32[]{:S(2)}) async-start(s8[7372800]{0:T(1024)(128)(4,1)} %bitcast.9), calls=%async_computation | async-start | bytes 8388608
  5.4 6.2 %slice-start.1 = ((s8[7372800]{0:T(1024)(128)(4,1)}), s8[3178496]{0:T(1024)(128)(4,1)S(1)}, s32[]{:S(2)}) async-start(s8[7372800]{0:T(1024)(128)(4,1)} %bitcast.9), calls=%async_computation.1 | async-start | bytes 6356992
  5.9 3.6 %copy-start.1 = (bf16[2,2,77,640]{3,1,2,0:T(2,128)(2,1)S(1)}, bf16[2,2,77,640]{3,1,2,0:T(2,128)(2,1)}, u32[]{:S(2)}) copy-start(bf16[2,2,77,640]{3,1,2,0:T(2,128)(2,1)} %param.18) | copy-start | bytes 1182724
  5.9 5.7 %copy-start.2 = (f32[640]{0:T(1024)S(1)}, f32[640]{0:T(1024)}, u32[]{:S(2)}) copy-start(f32[640]{0:T(1024)} %bias_ref.1) | copy-start | bytes 7684
  5.9 5.7 %collective-permute-start = (bf16[4,16,1280]{2,1,0:T(8,128)(2,1)S(1)}, bf16[4,16,1280]{2,1,0:T(8,128)(2,1)S(1)}, u32[]{:S(2)}, u32[]{:S(2)}) collective-permute-start(bf16[4,16,1280]{2,1,0:T(8,128)(2,1)S(1)} %get-tuple-element.13.edge_act_ref), channel_id=1, source_target_pairs={{0,8},{8,0},{16,24},{24,16},{1,9},{9,1},{17,25},{25,17},{2,10},{10... | collective-permute-start | bytes 491528 | tf_op jit(solution)/shard_map/ppermute | solution.py:251
  8.8 8.0 %collective-permute-start.1 = (bf16[4,16,1280]{2,1,0:T(8,128)(2,1)S(1)}, bf16[4,16,1280]{2,1,0:T(8,128)(2,1)S(1)}, u32[]{:S(2)}, u32[]{:S(2)}) collective-permute-start(bf16[4,16,1280]{2,1,0:T(8,128)(2,1)S(1)} %get-tuple-element.16), channel_id=1, source_target_pairs={{8,16},{16,8},{9,17},{17,9},{10,18},{18,10},{11,19},{19,11},{12,20... | collective-permute-start | bytes 491528 | tf_op jit(solution)/shard_map/ppermute | solution.py:261
  11.7 5.2 %copy-start.3 = (bf16[640,640]{1,0:T(8,128)(2,1)S(1)}, bf16[640,640]{1,0:T(8,128)(2,1)}, u32[]{:S(2)}) copy-start(bf16[640,640]{1,0:T(8,128)(2,1)} %wq_ref.1) | copy-start | bytes 2457604
  11.7 5.1 %copy-start.4 = (bf16[640,640]{1,0:T(8,128)(2,1)S(1)}, bf16[640,640]{1,0:T(8,128)(2,1)}, u32[]{:S(2)}) copy-start(bf16[640,640]{1,0:T(8,128)(2,1)} %wk_ref.1) | copy-start | bytes 2457604
  11.7 5.1 %copy-start.5 = (bf16[640,640]{1,0:T(8,128)(2,1)S(1)}, bf16[640,640]{1,0:T(8,128)(2,1)}, u32[]{:S(2)}) copy-start(bf16[640,640]{1,0:T(8,128)(2,1)} %wv_ref.1) | copy-start | bytes 2457604
  11.7 5.1 %copy-start.6 = (bf16[640,640]{1,0:T(8,128)(2,1)S(1)}, bf16[640,640]{1,0:T(8,128)(2,1)}, u32[]{:S(2)}) copy-start(bf16[640,640]{1,0:T(8,128)(2,1)} %wo_ref.1) | copy-start | bytes 2457604
  11.7 5.1 %copy-start.7 = (bf16[640,640]{1,0:T(8,128)(2,1)S(1)}, bf16[640,640]{1,0:T(8,128)(2,1)}, u32[]{:S(2)}) copy-start(bf16[640,640]{1,0:T(8,128)(2,1)} %xq_ref.1) | copy-start | bytes 2457604
  11.7 5.1 %copy-start.11 = (f32[640]{0:T(1024)S(1)}, f32[640]{0:T(1024)}, u32[]{:S(2)}) copy-start(f32[640]{0:T(1024)} %tgain_ref.1) | copy-start | bytes 7684
  11.7 5.1 %copy-start.12 = (f32[640]{0:T(1024)S(1)}, f32[640]{0:T(1024)}, u32[]{:S(2)}) copy-start(f32[640]{0:T(1024)} %xgain_ref.1) | copy-start | bytes 7684
  14.5 7.7 %copy-start.8 = (bf16[640,640]{1,0:T(8,128)(2,1)S(1)}, bf16[640,640]{1,0:T(8,128)(2,1)}, u32[]{:S(2)}) copy-start(bf16[640,640]{1,0:T(8,128)(2,1)} %xo_ref.1) | copy-start | bytes 2457604
  14.5 7.7 %copy-start.13 = (s32[16]{0:T(128)S(1)}, s32[16]{0:T(128)}, u32[]{:S(2)}) copy-start(s32[16]{0:T(128)} %slot_ref.1) | copy-start | bytes 196
  14.5 7.7 %copy-start.14 = (s32[2]{0:T(128)S(1)}, s32[2]{0:T(128)}, u32[]{:S(2)}) copy-start(s32[2]{0:T(128)} %gate_ref.1) | copy-start | bytes 28
  14.9 7.3 %collective-permute-start.3 = (bf16[77,2,640]{2,0,1:T(8,128)(2,1)S(1)}, bf16[77,2,640]{2,0,1:T(8,128)(2,1)S(1)}, u32[]{:S(2)}, u32[]{:S(2)}) collective-permute-start(bf16[77,2,640]{2,0,1:T(8,128)(2,1)S(1)} %collective-permute-done.2), channel_id=1, source_target_pairs={{0,8},{8,0},{16,24},{24,16},{1,9},{9,1},{17,25},{25,17},{2,10},{10... | collective-permute-start | bytes 591368 | tf_op jit(solution)/shard_map/ppermute | solution.py:237

commit v6 on v5

--- a/solution.py
+++ b/solution.py
@@ -47,36 +47,36 @@
     return 1 - lax.rem(lax.axis_index("strip"), 2)
 
 
-def lay_out(raw_ref, gain_ref, s, r, c):
-    frames, width = raw_ref.shape[2], raw_ref.shape[4]
-    raw = raw_ref[s, r, :, c, :]
-    raw = jnp.concatenate([raw, jnp.zeros((PAD - frames, width), BF16)], axis=0)
-    return raw, silu(rms(raw.astype(F32), gain_ref[...])).astype(BF16)
+def lay_out(raw_ref, gain_ref, s, r, x_ref, act_ref, *index):
+    frames, cols, width = raw_ref.shape[2:]
+    to = lax.broadcasted_iota(jnp.int32, (cols * PAD, cols * frames), 0)
+    at = lax.broadcasted_iota(jnp.int32, (cols * PAD, cols * frames), 1)
+    pick = (at == lax.rem(to, PAD) * cols + to // PAD) & (lax.rem(to, PAD) < frames)
+    rows = dot(pick.astype(F32).astype(BF16), raw_ref[s, r].reshape(frames * cols, width))
+    for c in range(cols):
+        ls = slice(c * width, (c + 1) * width)
+        one = rows[c * PAD : (c + 1) * PAD]
+        x_ref[(*index, slice(None), ls)] = one.astype(BF16)
+        act_ref[(*index, slice(None), ls)] = silu(rms(one, gain_ref[...])).astype(BF16)
 
 
 def edge_kernel(raw_ref, gain_ref, x_ref, act_ref):
-    slots, rows, _, cols, width = raw_ref.shape
+    slots, rows = raw_ref.shape[:2]
     r = first_row() * (rows - 1)
     for s in range(slots):
-        for c in range(cols):
-            ls = slice(c * width, (c + 1) * width)
-            x_ref[s, :, ls], act_ref[s, :, ls] = lay_out(raw_ref, gain_ref, s, r, c)
+        lay_out(raw_ref, gain_ref, s, r, x_ref, act_ref, s)
 
 
 def act_kernel(raw_ref, gain_ref, edge_x_ref, edge_act_ref, x_ref, act_ref, edge_ref):
-    slots, rows, _, cols, width = raw_ref.shape
+    slots, rows = raw_ref.shape[:2]
     done = first_row() * (rows - 1)
     other = rows - 1 - done
     x_ref[:, done] = edge_x_ref[...]
     act_ref[:, done] = edge_act_ref[...]
     for s in range(slots):
-        for c in range(cols):
-            ls = slice(c * width, (c + 1) * width)
-            for r in (other, *range(1, rows - 1)):
-                x_ref[s, r, :, ls], a = lay_out(raw_ref, gain_ref, s, r, c)
-                act_ref[s, r, :, ls] = a
-                if r is other:
-                    edge_ref[s, :, ls] = a
+        for r in (other, *range(1, rows - 1)):
+            lay_out(raw_ref, gain_ref, s, r, x_ref, act_ref, s, r)
+        edge_ref[s] = act_ref[s, other]
 
 
 def conv_kernel(x_ref, act_ref, near_ref, w_ref, bias_ref, out_ref, ext):
@@ -160,7 +160,7 @@
 
 
 def cross_kernel(
-    frames, slot_ref, gate_ref, after_ref, query_ref, own_ref, fetched_ref, swapped_ref, xo_ref, out_ref, keys, values, scores, chances, mixed
+    frames, slot_ref, gate_ref, after_ref, query_ref, own_ref, fetched_ref, swapped_ref, xo_ref, out_ref, keys, values, scores, chances, mixed, made, sems
 ):
     cols, slots, rows, _, width = after_ref.shape
     half = slots // 2
@@ -194,12 +194,18 @@
     frame = lax.broadcasted_iota(jnp.int32, (rows, PAD, width), 1).astype(F32)
     scale = 1.0 + 2.0 * frame / (frames - 1)
     add = dot(mixed[...].reshape(-1, width), xo_ref[...]).reshape(cols, half, rows, PAD, width)
-    for c in range(cols):
-        for r in range(half):
+    copies = []
+    for r in range(half):
+        for c in range(cols):
             cond = (after_ref[c, r] + add[c, r]).astype(BF16).astype(F32)
             uncond = after_ref[c, half + r].astype(BF16).astype(F32)
             guided = jnp.where(gate_ref[r] == 1, uncond + scale * (cond - uncond), cond)
-            out_ref[r, :, :, c * width : (c + 1) * width] = guided.astype(BF16)
+            for w in range(rows):
+                made[r, w, :, c, :] = guided[w, :frames].astype(BF16)
+        copies.append(pltpu.make_async_copy(made.at[r], out_ref.at[r], sems.at[r]))
+        copies[r].start()
+    for copy in copies:
+        copy.wait()
 
 
 def on_device(
@@ -289,20 +295,21 @@
     )
     out = pl.pallas_call(
         functools.partial(cross_kernel, frames),
-        out_shape=jax.ShapeDtypeStruct((REQ_DEV, rows, PAD, cols * width), BF16),
+        out_shape=jax.ShapeDtypeStruct((REQ_DEV, rows, frames, cols, width), BF16),
         in_specs=[sm, sm] + [vm] * 6,
-        out_specs=vm,
+        out_specs=any_,
         scratch_shapes=[pltpu.VMEM((REQ_DEV, room, width), BF16)] * 2
         + [
             pltpu.VMEM((REQ_DEV, cols * rows * PAD, width // HEAD_DIM * room), F32),
             pltpu.VMEM((REQ_DEV, cols * rows * PAD, width // HEAD_DIM * room), BF16),
             pltpu.VMEM((cols, REQ_DEV, rows, PAD, width), BF16),
+            pltpu.VMEM((REQ_DEV, rows, frames, cols, width), BF16),
+            pltpu.SemaphoreType.DMA((REQ_DEV,)),
         ],
         compiler_params=pltpu.CompilerParams(vmem_limit_bytes=16 << 20),
         cost_estimate=cost(COST3),
         name="cross_mix",
     )(context_slot, gate, after, query, context_pages, fetched, swapped, cross_out)
-    out = out[:, :, :frames].reshape(REQ_DEV, rows, frames, cols, width)
     return out.transpose(0, 1, 3, 2, 4)
 
 

time: 24.9 us -> 24.5 us (0.984)
  waiting for transfers between devices: 2.4 us -> 3.31 us
  local copies, waits for them, and re-layouts: 1.98 us -> 1.16 us
  starting transfers between devices: 8.28 us -> 7.87 us
    pallas_call x1, Pallas kernels: 1.72 us -> 2.57 us  [on_device(): pl.pallas_call(functools.partial(cross_kernel, frames), out_shape=jax.Sha...]
    reshape x1 -> x0, local copies, waits for them, and re-layouts: 0.82 us -> none  [on_device(): out = out[:, :, :frames].reshape(REQ_DEV, rows, frames, cols, width)]
    pallas_call x1, Pallas kernels: 1.36 us -> 0.57 us  [on_device(): pl.pallas_call(act_kernel, out_shape=(whole, whole, row), in_specs=[vm] *...]
    ppermute x1, waiting for transfers between devices: 2.06 us -> 2.85 us  [on_device(): near = lax.ppermute(edge_act, 'strip', near_pairs)]
    ppermute x1, starting transfers between devices: 1.95 us -> 1.54 us  [on_device(): swapped = lax.ppermute(fetched, 'strip', near_pairs)]
  transfers between devices with their start and end apart: 4 -> 4, of which waited for: 2 -> 2; matrix products, arithmetic and copies ran while one was open for 0% -> 0% of each run, Pallas kernels for 40% -> 37%
where the time goes in v6:
time: 24.5 us; the launch traced here: 24.4 us
  Pallas kernels  11.7 us (48%)
  starting transfers between devices  7.87 us (32%)
  waiting for transfers between devices  3.31 us (14%)
  local copies, waits for them, and re-layouts  1.16 us (5%)
  between operations  0.26 us (1%)
    pallas_call x1, Pallas kernels, on_device(): pl.pallas_call(functools.partial(time_kernel, frames), out_shape=(jax.Sha...  5.28 us
    ppermute x1, starting transfers between devices, on_device(): fetched = lax.ppermute(half, 'req', partner_pairs)  4.1 us
    ppermute x1, waiting for transfers between devices, on_device(): near = lax.ppermute(edge_act, 'strip', near_pairs)  2.85 us
    pallas_call x1, Pallas kernels, on_device(): pl.pallas_call(conv_kernel, out_shape=jax.ShapeDtypeStruct((cols, slots,...  2.74 us
    pallas_call x1, Pallas kernels, on_device(): pl.pallas_call(functools.partial(cross_kernel, frames), out_shape=jax.Sha...  2.57 us
    ppermute x1, starting transfers between devices, on_device(): near = lax.ppermute(edge_act, 'strip', near_pairs)  1.56 us
    ppermute x1, starting transfers between devices, on_device(): swapped = lax.ppermute(fetched, 'strip', near_pairs)  1.54 us
    unnamed x35, local copies, waits for them, and re-layouts  1.13 us
  transfers between devices with their start and end apart: 4, of which 2 were waited for; matrix products, arithmetic and copies ran while one was open for 0% of the time, Pallas kernels for 37%

profile of v6, /device:TPU:0, one launch (start us, length us, event | category | flops | bytes accessed | tf_op | source)
XLA Modules:
  0.0 24.4 jit_solution(7774734902669061179)
XLA Ops:
  0.0 1.0 %copy-done = bf16[2,2,77,640]{3,1,2,0:T(2,128)(2,1)S(1)} copy-done((bf16[2,2,77,640]{3,1,2,0:T(2,128)(2,1)S(1)}, bf16[2,2,77,640]{3,1,2,0:T(2,128)(2,1)}, u32[]{:S(2)}) %copy-start) | copy-done | bytes 394264
  1.0 0.2 %pages.1 = bf16[77,2,640]{2,1,0:T(2,128)(2,1)S(1)} custom-call(bf16[2,77,2,640]{3,2,1,0:T(2,128)(2,1)S(1)} %bitcast.9), custom_call_target="tpu_custom_call" | custom-call | flops 3000000000 | tf_op jit(solution)/shard_map/pages/pallas_call | solution.py:232
  1.3 4.1 %collective-permute-start.2 = (bf16[77,2,640]{2,0,1:T(8,128)(2,1)S(1)}, bf16[77,2,640]{2,0,1:T(8,128)(2,1)S(1)}, u32[]{:S(2)}, u32[]{:S(2)}) collective-permute-start(bf16[77,2,640]{2,0,1:T(8,128)(2,1)S(1)} %copy.17), channel_id=1, source_target_pairs={{0,4},{1,5},{2,6},{3,7},{4,0},{5,1},{6,2},{7,3},{8,12},{9,13},{10,... | collective-permute-start | bytes 591368 | tf_op jit(solution)/shard_map/ppermute | solution.py:242
  5.4 0.3 %edge.1 = (bf16[4,16,1280]{2,1,0:T(8,128)(2,1)S(1)}, bf16[4,16,1280]{2,1,0:T(8,128)(2,1)S(1)}) custom-call(bf16[4,4,14,2,640]{4,3,2,1,0:T(2,128)(2,1)S(1)} %bitcast.10, f32[640]{0:T(1024)S(1)} %copy-done.10), custom_call_target="tpu_custom_call" | custom-call | flops 16000000000 | tf_op jit(solution)/shard_map/edge/pallas_call | solution.py:248
  5.8 0.0 copy-start.1
  5.8 0.0 copy-start.2
  5.8 1.6 %collective-permute-start = (bf16[4,16,1280]{2,1,0:T(8,128)(2,1)S(1)}, bf16[4,16,1280]{2,1,0:T(8,128)(2,1)S(1)}, u32[]{:S(2)}, u32[]{:S(2)}) collective-permute-start(bf16[4,16,1280]{2,1,0:T(8,128)(2,1)S(1)} %get-tuple-element.13.edge_act_ref), channel_id=1, source_target_pairs={{0,8},{8,0},{16,24},{24,16},{1,9},{9,1},{17,25},{25,17},{2,10},{10... | collective-permute-start | bytes 491528 | tf_op jit(solution)/shard_map/ppermute | solution.py:257
  7.3 0.6 %activate.1 = (bf16[4,4,16,1280]{3,2,1,0:T(8,128)(2,1)S(1)}, bf16[4,4,16,1280]{3,2,1,0:T(8,128)(2,1)S(1)}, bf16[4,16,1280]{2,1,0:T(8,128)(2,1)S(1)}) custom-call(bf16[4,4,14,2,640]{4,3,2,1,0:T(2,128)(2,1)S(1)} %bitcast.11, f32[640]{0:T(1024)S(1)} %copy-done.10, bf16[4,16,1280]{2,1,0:T(8,128)(2,1)S(1)} %get-tuple-element.12.edge_x_ref, ...), custom_call_target="tpu_custom_call" | custom-call | flops 300000000 | tf_op jit(solution)/shard_map/activate/pallas_call | solution.py:258
  7.9 0.7 %collective-permute-start.1 = (bf16[4,16,1280]{2,1,0:T(8,128)(2,1)S(1)}, bf16[4,16,1280]{2,1,0:T(8,128)(2,1)S(1)}, u32[]{:S(2)}, u32[]{:S(2)}) collective-permute-start(bf16[4,16,1280]{2,1,0:T(8,128)(2,1)S(1)} %get-tuple-element.16), channel_id=1, source_target_pairs={{8,16},{16,8},{9,17},{17,9},{10,18},{18,10},{11,19},{19,11},{12,20... | collective-permute-start | bytes 491528 | tf_op jit(solution)/shard_map/ppermute | solution.py:267
  8.7 2.8 %collective-permute-done.near_ref = bf16[4,16,1280]{2,1,0:T(8,128)(2,1)S(1)} collective-permute-done((bf16[4,16,1280]{2,1,0:T(8,128)(2,1)S(1)}, bf16[4,16,1280]{2,1,0:T(8,128)(2,1)S(1)}, u32[]{:S(2)}, u32[]{:S(2)}) %collective-permute-start) | collective-permute-done | bytes 163872 | tf_op jit(solution)/shard_map/ppermute | solution.py:257
  11.5 0.0 copy-start.3
  11.5 0.0 copy-start.4
  11.5 0.0 copy-start.5
  11.6 0.0 copy-start.6
  11.6 0.0 copy-start.7
  11.6 0.0 copy-start.11
  11.6 0.0 copy-start.12
  11.6 2.7 %conv_own.1.part_ref = f32[2,4,4,16,640]{4,3,2,1,0:T(8,128)S(1)} custom-call(bf16[4,4,16,1280]{3,2,1,0:T(8,128)(2,1)S(1)} %get-tuple-element.14.x_ref, bf16[4,4,16,1280]{3,2,1,0:T(8,128)(2,1)S(1)} %get-tuple-element.15.act_ref, bf16[4,16,1280]{2,1,0:T(8,128)(2,1)S(1)} %collective-permute-done.near_ref, bf16[3,3,640,640]{3,2,1,0:T(8,128)(2,1)S(1)} %bitcast.8, ...), custom_call_target="tpu_custom_call" | custom-call | flops 300000000 | tf_op jit(solution)/shard_map/conv_own/pallas_call | solution.py:268
  14.4 0.0 copy-start.13
  14.4 0.0 copy-start.14
  14.4 0.5 %collective-permute-done.2 = bf16[77,2,640]{2,0,1:T(8,128)(2,1)S(1)} collective-permute-done((bf16[77,2,640]{2,0,1:T(8,128)(2,1)S(1)}, bf16[77,2,640]{2,0,1:T(8,128)(2,1)S(1)}, u32[]{:S(2)}, u32[]{:S(2)}) %collective-permute-start.2) | collective-permute-done | bytes 197152 | tf_op jit(solution)/shard_map/ppermute | solution.py:242
  14.9 1.5 %collective-permute-start.3 = (bf16[77,2,640]{2,0,1:T(8,128)(2,1)S(1)}, bf16[77,2,640]{2,0,1:T(8,128)(2,1)S(1)}, u32[]{:S(2)}, u32[]{:S(2)}) collective-permute-start(bf16[77,2,640]{2,0,1:T(8,128)(2,1)S(1)} %collective-permute-done.2), channel_id=1, source_target_pairs={{0,8},{8,0},{16,24},{24,16},{1,9},{9,1},{17,25},{25,17},{2,10},{10... | collective-permute-start | bytes 591368 | tf_op jit(solution)/shard_map/ppermute | solution.py:243
  16.5 5.3 %time_mix.1 = (f32[2,4,4,16,640]{4,3,2,1,0:T(8,128)S(1)}, bf16[2,2,4,16,640]{4,3,2,1,0:T(8,128)(2,1)S(1)}) custom-call(f32[2,4,4,16,640]{4,3,2,1,0:T(8,128)S(1)} %conv_own.1.part_ref, bf16[4,16,1280]{2,1,0:T(8,128)(2,1)S(1)} %collective-permute-done.1.next_ref, bf16[3,3,640,640]{3,2,1,0:T(8,128)(2,1)S(1)} %bitcast.8, ...), custom_call_target="tpu_custom_call", output_to_operand_aliasing={{0}: (0, {})} | custom-call | flops 6000000000 | tf_op jit(solution)/shard_map/time_mix/pallas_call | solution.py:278
  21.8 2.6 %cross_mix.1 = bf16[2,4,14,2,640]{4,3,2,1,0:T(2,128)(2,1)} custom-call(s32[16]{0:T(128)S(1)} %copy-done.13, s32[2]{0:T(128)S(1)} %copy-done.14, f32[2,4,4,16,640]{4,3,2,1,0:T(8,128)S(1)} %get-tuple-element.17.after_ref, bf16[2,2,4,16,640]{4,3,2,1,0:T(8,128)(2,1)S(1)} %get-tuple-element.18.query_ref, bf16[2,2,77,640]{3,2,1,0:T(8,128)(2,1)S(1)} %copy.18.own_ref, ...), custom_call_target="tpu_custom_call" | custom-call | flops 1000000000 | tf_op jit(solution)/shard_map/cross_mix/pallas_call | solution.py:296
  (27 shorter events, 0.1 us)
Async XLA Ops:
  0.0 1.0 %copy-start = (bf16[2,2,77,640]{3,1,2,0:T(2,128)(2,1)S(1)}, bf16[2,2,77,640]{3,1,2,0:T(2,128)(2,1)}, u32[]{:S(2)}) copy-start(bf16[2,2,77,640]{3,1,2,0:T(2,128)(2,1)} %param.18) | copy-start | bytes 1182724
  1.0 4.4 %copy-start.9 = (bf16[2,2,4,2,14,640]{5,3,4,2,1,0:T(2,128)(2,1)S(1)}, bf16[2,2,4,2,14,640]{5,3,4,2,1,0:T(2,128)(2,1)}, u32[]{:S(2)}) copy-start(bf16[2,2,4,2,14,640]{5,3,4,2,1,0:T(2,128)(2,1)} %param.15) | copy-start | bytes 1720324
  1.0 4.4 %copy-start.10 = (f32[640]{0:T(1024)S(1)}, f32[640]{0:T(1024)}, u32[]{:S(2)}) copy-start(f32[640]{0:T(1024)} %gain_ref.3) | copy-start | bytes 7684
  1.3 13.6 %collective-permute-start.2 = (bf16[77,2,640]{2,0,1:T(8,128)(2,1)S(1)}, bf16[77,2,640]{2,0,1:T(8,128)(2,1)S(1)}, u32[]{:S(2)}, u32[]{:S(2)}) collective-permute-start(bf16[77,2,640]{2,0,1:T(8,128)(2,1)S(1)} %copy.17), channel_id=1, source_target_pairs={{0,4},{1,5},{2,6},{3,7},{4,0},{5,1},{6,2},{7,3},{8,12},{9,13},{10,... | collective-permute-start | bytes 591368 | tf_op jit(solution)/shard_map/ppermute | solution.py:242
  5.4 6.1 %slice-start = ((s8[7372800]{0:T(1024)(128)(4,1)}), s8[4194304]{0:T(1024)(128)(4,1)S(1)}, s32[]{:S(2)}) async-start(s8[7372800]{0:T(1024)(128)(4,1)} %bitcast.7), calls=%async_computation | async-start | bytes 8388608
  5.4 6.1 %slice-start.1 = ((s8[7372800]{0:T(1024)(128)(4,1)}), s8[3178496]{0:T(1024)(128)(4,1)S(1)}, s32[]{:S(2)}) async-start(s8[7372800]{0:T(1024)(128)(4,1)} %bitcast.7), calls=%async_computation.1 | async-start | bytes 6356992
  5.8 2.8 %copy-start.1 = (bf16[2,2,77,640]{3,1,2,0:T(2,128)(2,1)S(1)}, bf16[2,2,77,640]{3,1,2,0:T(2,128)(2,1)}, u32[]{:S(2)}) copy-start(bf16[2,2,77,640]{3,1,2,0:T(2,128)(2,1)} %param.18) | copy-start | bytes 1182724
  5.8 5.7 %copy-start.2 = (f32[640]{0:T(1024)S(1)}, f32[640]{0:T(1024)}, u32[]{:S(2)}) copy-start(f32[640]{0:T(1024)} %bias_ref.1) | copy-start | bytes 7684
  5.8 5.7 %collective-permute-start = (bf16[4,16,1280]{2,1,0:T(8,128)(2,1)S(1)}, bf16[4,16,1280]{2,1,0:T(8,128)(2,1)S(1)}, u32[]{:S(2)}, u32[]{:S(2)}) collective-permute-start(bf16[4,16,1280]{2,1,0:T(8,128)(2,1)S(1)} %get-tuple-element.13.edge_act_ref), channel_id=1, source_target_pairs={{0,8},{8,0},{16,24},{24,16},{1,9},{9,1},{17,25},{25,17},{2,10},{10... | collective-permute-start | bytes 491528 | tf_op jit(solution)/shard_map/ppermute | solution.py:257
  7.9 8.5 %collective-permute-start.1 = (bf16[4,16,1280]{2,1,0:T(8,128)(2,1)S(1)}, bf16[4,16,1280]{2,1,0:T(8,128)(2,1)S(1)}, u32[]{:S(2)}, u32[]{:S(2)}) collective-permute-start(bf16[4,16,1280]{2,1,0:T(8,128)(2,1)S(1)} %get-tuple-element.16), channel_id=1, source_target_pairs={{8,16},{16,8},{9,17},{17,9},{10,18},{18,10},{11,19},{19,11},{12,20... | collective-permute-start | bytes 491528 | tf_op jit(solution)/shard_map/ppermute | solution.py:267
  11.5 4.9 %copy-start.3 = (bf16[640,640]{1,0:T(8,128)(2,1)S(1)}, bf16[640,640]{1,0:T(8,128)(2,1)}, u32[]{:S(2)}) copy-start(bf16[640,640]{1,0:T(8,128)(2,1)} %wq_ref.1) | copy-start | bytes 2457604
  11.5 4.9 %copy-start.4 = (bf16[640,640]{1,0:T(8,128)(2,1)S(1)}, bf16[640,640]{1,0:T(8,128)(2,1)}, u32[]{:S(2)}) copy-start(bf16[640,640]{1,0:T(8,128)(2,1)} %wk_ref.1) | copy-start | bytes 2457604
  11.5 4.9 %copy-start.5 = (bf16[640,640]{1,0:T(8,128)(2,1)S(1)}, bf16[640,640]{1,0:T(8,128)(2,1)}, u32[]{:S(2)}) copy-start(bf16[640,640]{1,0:T(8,128)(2,1)} %wv_ref.1) | copy-start | bytes 2457604
  11.6 4.9 %copy-start.6 = (bf16[640,640]{1,0:T(8,128)(2,1)S(1)}, bf16[640,640]{1,0:T(8,128)(2,1)}, u32[]{:S(2)}) copy-start(bf16[640,640]{1,0:T(8,128)(2,1)} %wo_ref.1) | copy-start | bytes 2457604
  11.6 4.9 %copy-start.7 = (bf16[640,640]{1,0:T(8,128)(2,1)S(1)}, bf16[640,640]{1,0:T(8,128)(2,1)}, u32[]{:S(2)}) copy-start(bf16[640,640]{1,0:T(8,128)(2,1)} %xq_ref.1) | copy-start | bytes 2457604
  11.6 4.9 %copy-start.11 = (f32[640]{0:T(1024)S(1)}, f32[640]{0:T(1024)}, u32[]{:S(2)}) copy-start(f32[640]{0:T(1024)} %tgain_ref.1) | copy-start | bytes 7684
  11.6 4.9 %copy-start.12 = (f32[640]{0:T(1024)S(1)}, f32[640]{0:T(1024)}, u32[]{:S(2)}) copy-start(f32[640]{0:T(1024)} %xgain_ref.1) | copy-start | bytes 7684
  14.4 7.4 %copy-start.8 = (bf16[640,640]{1,0:T(8,128)(2,1)S(1)}, bf16[640,640]{1,0:T(8,128)(2,1)}, u32[]{:S(2)}) copy-start(bf16[640,640]{1,0:T(8,128)(2,1)} %xo_ref.1) | copy-start | bytes 2457604
  14.4 7.4 %copy-start.13 = (s32[16]{0:T(128)S(1)}, s32[16]{0:T(128)}, u32[]{:S(2)}) copy-start(s32[16]{0:T(128)} %slot_ref.1) | copy-start | bytes 196
  14.4 7.4 %copy-start.14 = (s32[2]{0:T(128)S(1)}, s32[2]{0:T(128)}, u32[]{:S(2)}) copy-start(s32[2]{0:T(128)} %gate_ref.1) | copy-start | bytes 28
  14.9 6.9 %collective-permute-start.3 = (bf16[77,2,640]{2,0,1:T(8,128)(2,1)S(1)}, bf16[77,2,640]{2,0,1:T(8,128)(2,1)S(1)}, u32[]{:S(2)}, u32[]{:S(2)}) collective-permute-start(bf16[77,2,640]{2,0,1:T(8,128)(2,1)S(1)} %collective-permute-done.2), channel_id=1, source_target_pairs={{0,8},{8,0},{16,24},{24,16},{1,9},{9,1},{17,25},{25,17},{2,10},{10... | collective-permute-start | bytes 591368 | tf_op jit(solution)/shard_map/ppermute | solution.py:243

commit v7 on v6

--- a/solution.py
+++ b/solution.py
@@ -79,7 +79,9 @@
         edge_ref[s] = act_ref[s, other]
 
 
-def conv_kernel(x_ref, act_ref, near_ref, w_ref, bias_ref, out_ref, ext):
+def conv_kernel(
+    x_ref, act_ref, near_ref, w_ref, bias_ref, tgain_ref, wq_ref, out_ref, normed_ref, tq_ref, ext
+):
     slots, rows, _, wide = x_ref.shape
     width = wide // 2
     side = 2 * first_row()
@@ -99,6 +101,13 @@
             x_ref[:, :, :, ls].astype(F32) + bias_ref[...].reshape(1, 1, 1, width) + mid[:, ls].reshape(slots, rows, PAD, width)
         )
         out_ref[c, :, inner_rows] += rest[:, ls].reshape(slots, rows - 1, PAD, width)
+    normalize(out_ref, tgain_ref, wq_ref, normed_ref, tq_ref, pl.ds(side // 2, rows - 1))
+
+
+def normalize(field_ref, gain_ref, wq_ref, normed_ref, tq_ref, place):
+    field = rms(field_ref[:, :, place], gain_ref[...]).astype(BF16)
+    normed_ref[:, :, place] = field
+    tq_ref[:, :, place] = dot(field.reshape(-1, field.shape[-1]), wq_ref[...]).astype(BF16).reshape(field.shape)
 
 
 def pair_taps(w_ref, dr):
@@ -113,8 +122,8 @@
 
 
 def time_kernel(
-    frames, part_ref, next_ref, w_ref, tgain_ref, wq_ref, wk_ref, wv_ref, wo_ref,
-    xgain_ref, xq_ref, after_ref, query_ref, normed, tq, tk, tv, mixed, scores, chances
+    frames, part_ref, normed, tq, next_ref, w_ref, tgain_ref, wq_ref, wk_ref, wv_ref, wo_ref,
+    xgain_ref, xq_ref, after_ref, _normed, _tq, query_ref, tk, tv, mixed, scores, chances
 ):
     cols, slots, rows, _, width = part_ref.shape
     wide = 2 * width
@@ -125,10 +134,10 @@
     add = dot(other, pair_taps(w_ref, 2 * side))
     for c in range(2):
         part_ref[c, :, side * (rows - 1)] += add[:, c * width : (c + 1) * width].reshape(slots, PAD, width)
-    normed[...] = rms(part_ref[...].reshape(total, width), tgain_ref[...]).astype(BF16)
-    every = dot(normed[...], jnp.concatenate([wq_ref[...], wk_ref[...], wv_ref[...]], axis=1))
-    for i, part in enumerate((tq, tk, tv)):
-        part[...] = every[:, i * width : (i + 1) * width].astype(BF16)
+    normalize(part_ref, tgain_ref, wq_ref, normed, tq, pl.ds(side * (rows - 1), 1))
+    both = dot(normed[...].reshape(total, width), jnp.concatenate([wk_ref[...], wv_ref[...]], axis=1))
+    tk[...] = both[:, :width].astype(BF16)
+    tv[...] = both[:, width:].astype(BF16)
     group = rows * PAD
     pair = 2 * HEAD_DIM
     row = lax.broadcasted_iota(jnp.int32, (group, 2 * group), 0)
@@ -137,13 +146,14 @@
     first = lax.broadcasted_iota(jnp.int32, (group, 2 * group), 1) < group
     ones = apart(jnp.ones((group, pair), BF16))
     tiles = [
-        (slice(g * group, (g + 1) * group), slice(j * pair, (j + 1) * pair))
+        (g, slice(g * group, (g + 1) * group), slice(j * pair, (j + 1) * pair))
         for g in range(total // group)
         for j in range(width // pair)
     ]
-    for rs, ls in tiles:
-        scores[rs, ls] = dot_t(tq[rs, ls], apart(tk[rs, ls]))
-    for rs, ls in tiles:
+    for g, rs, ls in tiles:
+        query = tq[g // slots, g % slots, :, :, ls].reshape(group, pair)
+        scores[rs, ls] = dot_t(query, apart(tk[rs, ls]))
+    for _, rs, ls in tiles:
         s = scores[rs, ls] + mask
         top = jnp.where(
             first,
@@ -151,7 +161,7 @@
             jnp.max(jnp.where(first, NEG, s), axis=-1, keepdims=True),
         )
         chances[rs, ls] = jnp.exp2((s - top) * (0.125 * LOG2E)).astype(BF16)
-    for rs, ls in tiles:
+    for _, rs, ls in tiles:
         out = dot(chances[rs, ls], jnp.concatenate([apart(tv[rs, ls]), ones], axis=1))
         mixed[rs, ls] = (out[:, :pair] / out[:, pair:]).astype(BF16)
     after_ref[...] = part_ref[...] + dot(mixed[...], wo_ref[...]).reshape(after_ref.shape)
@@ -191,7 +201,7 @@
     for r, ls, ks in tiles:
         out = dot(chances[r, :, ks], jnp.concatenate([apart(values[r, :, ls]), ones], axis=1))
         mixed[:, r, :, :, ls] = (out[:, :pair] / out[:, pair:]).astype(BF16).reshape(cols, rows, PAD, pair)
-    frame = lax.broadcasted_iota(jnp.int32, (rows, PAD, width), 1).astype(F32)
+    frame = lax.broadcasted_iota(jnp.int32, (PAD, width), 0).astype(F32)
     scale = 1.0 + 2.0 * frame / (frames - 1)
     add = dot(mixed[...].reshape(-1, width), xo_ref[...]).reshape(cols, half, rows, PAD, width)
     copies = []
@@ -265,33 +275,36 @@
         name="activate",
     )(raw, conv_gain, edge_x, edge_act)
     other = lax.ppermute(edge, "strip", next_pairs)
-    part = pl.pallas_call(
+    grid = (cols, slots, rows, PAD, width)
+    part, normed, queries = pl.pallas_call(
         conv_kernel,
-        out_shape=jax.ShapeDtypeStruct((cols, slots, rows, PAD, width), F32),
-        in_specs=[vm] * 5,
-        out_specs=vm,
+        out_shape=(jax.ShapeDtypeStruct(grid, F32), jax.ShapeDtypeStruct(grid, BF16), jax.ShapeDtypeStruct(grid, BF16)),
+        in_specs=[vm] * 7,
+        out_specs=(vm,) * 3,
         scratch_shapes=[pltpu.VMEM((slots, rows + 2, PAD, wide), BF16)],
         compiler_params=pltpu.CompilerParams(vmem_limit_bytes=16 << 20),
         cost_estimate=cost(COST1),
         name="conv_own",
-    )(x, act, near, conv_weight, conv_bias)
-    after, query = pl.pallas_call(
+    )(x, act, near, conv_weight, conv_bias, temporal_gain, temporal_query)
+    after, _, _, query = pl.pallas_call(
         functools.partial(time_kernel, frames),
         out_shape=(
-            jax.ShapeDtypeStruct((cols, slots, rows, PAD, width), F32),
+            jax.ShapeDtypeStruct(grid, F32),
+            jax.ShapeDtypeStruct(grid, BF16),
+            jax.ShapeDtypeStruct(grid, BF16),
             jax.ShapeDtypeStruct((cols, REQ_DEV, rows, PAD, width), BF16),
         ),
-        in_specs=[vm] * 10,
-        out_specs=(vm, vm),
-        scratch_shapes=[pltpu.VMEM((total, width), BF16)] * 5
+        in_specs=[vm] * 12,
+        out_specs=(vm,) * 4,
+        scratch_shapes=[pltpu.VMEM((total, width), BF16)] * 3
         + [pltpu.VMEM((total, width // HEAD_DIM * rows * PAD), kind) for kind in (F32, BF16)],
-        input_output_aliases={0: 0},
+        input_output_aliases={0: 0, 1: 1, 2: 2},
         compiler_params=pltpu.CompilerParams(vmem_limit_bytes=16 << 20),
         cost_estimate=cost(COST2),
         name="time_mix",
     )(
-        part, other, conv_weight, temporal_gain, temporal_query, temporal_key,
-        temporal_value, temporal_out, cross_gain, cross_query,
+        part, normed, queries, other, conv_weight, temporal_gain, temporal_query, temporal_key, temporal_value,
+        temporal_out, cross_gain, cross_query,
     )
     out = pl.pallas_call(
         functools.partial(cross_kernel, frames),

time: 24.5 us -> 24.4 us (level)
  waiting for transfers between devices: 3.31 us -> 2.86 us
  Pallas kernels: 11.7 us -> 12 us
    pallas_call x1, Pallas kernels: 2.74 us -> 3.49 us  [on_device(): pl.pallas_call(conv_kernel, out_shape=(jax.ShapeDtypeStruct(grid, F32), j...]
    pallas_call x1, Pallas kernels: 5.28 us -> 4.78 us  [on_device(): pl.pallas_call(functools.partial(time_kernel, frames), out_shape=(jax.Sha...]
    ppermute x1, waiting for transfers between devices: 0.46 us -> 0.01 us  [on_device(): fetched = lax.ppermute(half, 'req', partner_pairs)]
  transfers between devices with their start and end apart: 4 -> 4, of which waited for: 2 -> 1; matrix products, arithmetic and copies ran while one was open for 0% -> 0% of each run, Pallas kernels for 37% -> 38%
where the time goes in v7:
time: 24.4 us; the launch traced here: 24.2 us
  Pallas kernels  12 us (49%)
  starting transfers between devices  7.94 us (33%)
  waiting for transfers between devices  2.86 us (12%)
  local copies, waits for them, and re-layouts  1.16 us (5%)
  between operations  0.27 us (1%)
    pallas_call x1, Pallas kernels, on_device(): pl.pallas_call(functools.partial(time_kernel, frames), out_shape=(jax.Sha...  4.78 us
    ppermute x1, starting transfers between devices, on_device(): fetched = lax.ppermute(half, 'req', partner_pairs)  4.1 us
    pallas_call x1, Pallas kernels, on_device(): pl.pallas_call(conv_kernel, out_shape=(jax.ShapeDtypeStruct(grid, F32), j...  3.49 us
    ppermute x1, waiting for transfers between devices, on_device(): near = lax.ppermute(edge_act, 'strip', near_pairs)  2.85 us
    pallas_call x1, Pallas kernels, on_device(): pl.pallas_call(functools.partial(cross_kernel, frames), out_shape=jax.Sha...  2.58 us
    ppermute x1, starting transfers between devices, on_device(): swapped = lax.ppermute(fetched, 'strip', near_pairs)  1.61 us
    ppermute x1, starting transfers between devices, on_device(): near = lax.ppermute(edge_act, 'strip', near_pairs)  1.56 us
    unnamed x35, local copies, waits for them, and re-layouts  1.13 us
  transfers between devices with their start and end apart: 4, of which 1 were waited for; matrix products, arithmetic and copies ran while one was open for 0% of the time, Pallas kernels for 38%

profile of v7, /device:TPU:0, one launch (start us, length us, event | category | flops | bytes accessed | tf_op | source)
XLA Modules:
  0.0 24.2 jit_solution(14027148642713596856)
XLA Ops:
  0.0 1.0 %copy-done.1 = bf16[2,2,77,640]{3,1,2,0:T(2,128)(2,1)S(1)} copy-done((bf16[2,2,77,640]{3,1,2,0:T(2,128)(2,1)S(1)}, bf16[2,2,77,640]{3,1,2,0:T(2,128)(2,1)}, u32[]{:S(2)}) %copy-start.1) | copy-done | bytes 394264
  1.0 0.2 %pages.1 = bf16[77,2,640]{2,1,0:T(2,128)(2,1)S(1)} custom-call(bf16[2,77,2,640]{3,2,1,0:T(2,128)(2,1)S(1)} %bitcast.9), custom_call_target="tpu_custom_call" | custom-call | flops 3000000000 | tf_op jit(solution)/shard_map/pages/pallas_call | solution.py:242
  1.3 4.1 %collective-permute-start.2 = (bf16[77,2,640]{2,0,1:T(8,128)(2,1)S(1)}, bf16[77,2,640]{2,0,1:T(8,128)(2,1)S(1)}, u32[]{:S(2)}, u32[]{:S(2)}) collective-permute-start(bf16[77,2,640]{2,0,1:T(8,128)(2,1)S(1)} %copy.19), channel_id=1, source_target_pairs={{0,4},{1,5},{2,6},{3,7},{4,0},{5,1},{6,2},{7,3},{8,12},{9,13},{10,... | collective-permute-start | bytes 591368 | tf_op jit(solution)/shard_map/ppermute | solution.py:252
  5.4 0.0 slice-start.1
  5.4 0.3 %edge.1 = (bf16[4,16,1280]{2,1,0:T(8,128)(2,1)S(1)}, bf16[4,16,1280]{2,1,0:T(8,128)(2,1)S(1)}) custom-call(bf16[4,4,14,2,640]{4,3,2,1,0:T(2,128)(2,1)S(1)} %bitcast.10, f32[640]{0:T(1024)S(1)} %copy-done.11), custom_call_target="tpu_custom_call" | custom-call | flops 16000000000 | tf_op jit(solution)/shard_map/edge/pallas_call | solution.py:258
  5.8 0.0 copy-start
  5.8 0.0 copy-start.3
  5.8 0.0 copy-start.4
  5.8 1.6 %collective-permute-start = (bf16[4,16,1280]{2,1,0:T(8,128)(2,1)S(1)}, bf16[4,16,1280]{2,1,0:T(8,128)(2,1)S(1)}, u32[]{:S(2)}, u32[]{:S(2)}) collective-permute-start(bf16[4,16,1280]{2,1,0:T(8,128)(2,1)S(1)} %get-tuple-element.16.edge_act_ref), channel_id=1, source_target_pairs={{0,8},{8,0},{16,24},{24,16},{1,9},{9,1},{17,25},{25,17},{2,10},{10... | collective-permute-start | bytes 491528 | tf_op jit(solution)/shard_map/ppermute | solution.py:267
  7.4 0.6 %activate.1 = (bf16[4,4,16,1280]{3,2,1,0:T(8,128)(2,1)S(1)}, bf16[4,4,16,1280]{3,2,1,0:T(8,128)(2,1)S(1)}, bf16[4,16,1280]{2,1,0:T(8,128)(2,1)S(1)}) custom-call(bf16[4,4,14,2,640]{4,3,2,1,0:T(2,128)(2,1)S(1)} %bitcast.11, f32[640]{0:T(1024)S(1)} %copy-done.11, bf16[4,16,1280]{2,1,0:T(8,128)(2,1)S(1)} %get-tuple-element.15.edge_x_ref, ...), custom_call_target="tpu_custom_call" | custom-call | flops 300000000 | tf_op jit(solution)/shard_map/activate/pallas_call | solution.py:268
  7.9 0.7 %collective-permute-start.1 = (bf16[4,16,1280]{2,1,0:T(8,128)(2,1)S(1)}, bf16[4,16,1280]{2,1,0:T(8,128)(2,1)S(1)}, u32[]{:S(2)}, u32[]{:S(2)}) collective-permute-start(bf16[4,16,1280]{2,1,0:T(8,128)(2,1)S(1)} %get-tuple-element.22), channel_id=1, source_target_pairs={{8,16},{16,8},{9,17},{17,9},{10,18},{18,10},{11,19},{19,11},{12,20... | collective-permute-start | bytes 491528 | tf_op jit(solution)/shard_map/ppermute | solution.py:277
  8.7 2.9 %collective-permute-done.near_ref = bf16[4,16,1280]{2,1,0:T(8,128)(2,1)S(1)} collective-permute-done((bf16[4,16,1280]{2,1,0:T(8,128)(2,1)S(1)}, bf16[4,16,1280]{2,1,0:T(8,128)(2,1)S(1)}, u32[]{:S(2)}, u32[]{:S(2)}) %collective-permute-start) | collective-permute-done | bytes 163872 | tf_op jit(solution)/shard_map/ppermute | solution.py:267
  11.6 0.0 copy-start.5
  11.6 0.0 copy-start.6
  11.6 0.0 copy-start.7
  11.6 0.0 copy-start.8
  11.6 0.0 copy-start.12
  11.6 3.5 %conv_own.1 = (f32[2,4,4,16,640]{4,3,2,1,0:T(8,128)S(1)}, bf16[2,4,4,16,640]{4,3,2,1,0:T(8,128)(2,1)S(1)}, bf16[2,4,4,16,640]{4,3,2,1,0:T(8,128)(2,1)S(1)}) custom-call(bf16[4,4,16,1280]{3,2,1,0:T(8,128)(2,1)S(1)} %get-tuple-element.17.x_ref, bf16[4,4,16,1280]{3,2,1,0:T(8,128)(2,1)S(1)} %get-tuple-element.18.act_ref, ...), custom_call_target="tpu_custom_call" | custom-call | flops 300000000 | tf_op jit(solution)/shard_map/conv_own/pallas_call | solution.py:279
  15.1 1.6 %collective-permute-start.3 = (bf16[77,2,640]{2,0,1:T(8,128)(2,1)S(1)}, bf16[77,2,640]{2,0,1:T(8,128)(2,1)S(1)}, u32[]{:S(2)}, u32[]{:S(2)}) collective-permute-start(bf16[77,2,640]{2,0,1:T(8,128)(2,1)S(1)} %collective-permute-done.2), channel_id=1, source_target_pairs={{0,8},{8,0},{16,24},{24,16},{1,9},{9,1},{17,25},{25,17},{2,10},{10... | collective-permute-start | bytes 591368 | tf_op jit(solution)/shard_map/ppermute | solution.py:253
  16.8 0.0 copy-start.9
  16.8 0.0 copy-start.13
  16.8 0.0 copy-start.14
  16.8 4.8 %time_mix.1 = (f32[2,4,4,16,640]{4,3,2,1,0:T(8,128)S(1)}, bf16[2,4,4,16,640]{4,3,2,1,0:T(8,128)(2,1)S(1)}, bf16[2,4,4,16,640]{4,3,2,1,0:T(8,128)(2,1)S(1)}, bf16[2,2,4,16,640]{4,3,2,1,0:T(8,128)(2,1)S(1)}) custom-call(f32[2,4,4,16,640]{4,3,2,1,0:T(8,128)S(1)} %get-tuple-element.19.part_ref, ...), custom_call_target="tpu_custom_call", output_to_operand_aliasing={{0}: (0, {}), {1}: (1, {}), {2}: (2, {})} | custom-call | flops 6000000000 | tf_op jit(solution)/shard_map/time_mix/pallas_call | solution.py:289
  21.7 2.6 %cross_mix.1 = bf16[2,4,14,2,640]{4,3,2,1,0:T(2,128)(2,1)} custom-call(s32[16]{0:T(128)S(1)} %copy-done.13, s32[2]{0:T(128)S(1)} %copy-done.14, f32[2,4,4,16,640]{4,3,2,1,0:T(8,128)S(1)} %get-tuple-element.23.after_ref, bf16[2,2,4,16,640]{4,3,2,1,0:T(8,128)(2,1)S(1)} %get-tuple-element.24.query_ref, bf16[2,2,77,640]{3,2,1,0:T(8,128)(2,1)S(1)} %copy.20.own_ref, ...), custom_call_target="tpu_custom_call" | custom-call | flops 1000000000 | tf_op jit(solution)/shard_map/cross_mix/pallas_call | solution.py:309
  (27 shorter events, 0.1 us)
Async XLA Ops:
  0.0 1.0 %copy-start.1 = (bf16[2,2,77,640]{3,1,2,0:T(2,128)(2,1)S(1)}, bf16[2,2,77,640]{3,1,2,0:T(2,128)(2,1)}, u32[]{:S(2)}) copy-start(bf16[2,2,77,640]{3,1,2,0:T(2,128)(2,1)} %param.18) | copy-start | bytes 1182724
  1.0 4.4 %copy-start.10 = (bf16[2,2,4,2,14,640]{5,3,4,2,1,0:T(2,128)(2,1)S(1)}, bf16[2,2,4,2,14,640]{5,3,4,2,1,0:T(2,128)(2,1)}, u32[]{:S(2)}) copy-start(bf16[2,2,4,2,14,640]{5,3,4,2,1,0:T(2,128)(2,1)} %param.15) | copy-start | bytes 1720324
  1.0 4.4 %copy-start.11 = (f32[640]{0:T(1024)S(1)}, f32[640]{0:T(1024)}, u32[]{:S(2)}) copy-start(f32[640]{0:T(1024)} %gain_ref.3) | copy-start | bytes 7684
  1.3 13.8 %collective-permute-start.2 = (bf16[77,2,640]{2,0,1:T(8,128)(2,1)S(1)}, bf16[77,2,640]{2,0,1:T(8,128)(2,1)S(1)}, u32[]{:S(2)}, u32[]{:S(2)}) collective-permute-start(bf16[77,2,640]{2,0,1:T(8,128)(2,1)S(1)} %copy.19), channel_id=1, source_target_pairs={{0,4},{1,5},{2,6},{3,7},{4,0},{5,1},{6,2},{7,3},{8,12},{9,13},{10,... | collective-permute-start | bytes 591368 | tf_op jit(solution)/shard_map/ppermute | solution.py:252
  5.4 6.1 %slice-start = ((s8[7372800]{0:T(1024)(128)(4,1)}), s8[4194304]{0:T(1024)(128)(4,1)S(1)}, s32[]{:S(2)}) async-start(s8[7372800]{0:T(1024)(128)(4,1)} %bitcast.7), calls=%async_computation | async-start | bytes 8388608
  5.4 3.2 %copy-start.2 = (bf16[2,2,77,640]{3,1,2,0:T(2,128)(2,1)S(1)}, bf16[2,2,77,640]{3,1,2,0:T(2,128)(2,1)}, u32[]{:S(2)}) copy-start(bf16[2,2,77,640]{3,1,2,0:T(2,128)(2,1)} %param.18) | copy-start | bytes 1182724
  5.4 6.1 %slice-start.1 = ((s8[7372800]{0:T(1024)(128)(4,1)}), s8[3178496]{0:T(1024)(128)(4,1)S(1)}, s32[]{:S(2)}) async-start(s8[7372800]{0:T(1024)(128)(4,1)} %bitcast.7), calls=%async_computation.1 | async-start | bytes 6356992
  5.8 5.8 %copy-start = (bf16[640,640]{1,0:T(8,128)(2,1)S(1)}, bf16[640,640]{1,0:T(8,128)(2,1)}, u32[]{:S(2)}) copy-start(bf16[640,640]{1,0:T(8,128)(2,1)} %wq_ref.3) | copy-start | bytes 2457604
  5.8 5.8 %copy-start.3 = (f32[640]{0:T(1024)S(1)}, f32[640]{0:T(1024)}, u32[]{:S(2)}) copy-start(f32[640]{0:T(1024)} %bias_ref.1) | copy-start | bytes 7684
  5.8 5.8 %copy-start.4 = (f32[640]{0:T(1024)S(1)}, f32[640]{0:T(1024)}, u32[]{:S(2)}) copy-start(f32[640]{0:T(1024)} %tgain_ref.3) | copy-start | bytes 7684
  5.8 5.7 %collective-permute-start = (bf16[4,16,1280]{2,1,0:T(8,128)(2,1)S(1)}, bf16[4,16,1280]{2,1,0:T(8,128)(2,1)S(1)}, u32[]{:S(2)}, u32[]{:S(2)}) collective-permute-start(bf16[4,16,1280]{2,1,0:T(8,128)(2,1)S(1)} %get-tuple-element.16.edge_act_ref), channel_id=1, source_target_pairs={{0,8},{8,0},{16,24},{24,16},{1,9},{9,1},{17,25},{25,17},{2,10},{10... | collective-permute-start | bytes 491528 | tf_op jit(solution)/shard_map/ppermute | solution.py:267
  7.9 8.8 %collective-permute-start.1 = (bf16[4,16,1280]{2,1,0:T(8,128)(2,1)S(1)}, bf16[4,16,1280]{2,1,0:T(8,128)(2,1)S(1)}, u32[]{:S(2)}, u32[]{:S(2)}) collective-permute-start(bf16[4,16,1280]{2,1,0:T(8,128)(2,1)S(1)} %get-tuple-element.22), channel_id=1, source_target_pairs={{8,16},{16,8},{9,17},{17,9},{10,18},{18,10},{11,19},{19,11},{12,20... | collective-permute-start | bytes 491528 | tf_op jit(solution)/shard_map/ppermute | solution.py:277
  11.6 5.2 %copy-start.5 = (bf16[640,640]{1,0:T(8,128)(2,1)S(1)}, bf16[640,640]{1,0:T(8,128)(2,1)}, u32[]{:S(2)}) copy-start(bf16[640,640]{1,0:T(8,128)(2,1)} %wk_ref.1) | copy-start | bytes 2457604
  11.6 5.2 %copy-start.6 = (bf16[640,640]{1,0:T(8,128)(2,1)S(1)}, bf16[640,640]{1,0:T(8,128)(2,1)}, u32[]{:S(2)}) copy-start(bf16[640,640]{1,0:T(8,128)(2,1)} %wv_ref.1) | copy-start | bytes 2457604
  11.6 5.2 %copy-start.7 = (bf16[640,640]{1,0:T(8,128)(2,1)S(1)}, bf16[640,640]{1,0:T(8,128)(2,1)}, u32[]{:S(2)}) copy-start(bf16[640,640]{1,0:T(8,128)(2,1)} %wo_ref.1) | copy-start | bytes 2457604
  11.6 5.2 %copy-start.8 = (bf16[640,640]{1,0:T(8,128)(2,1)S(1)}, bf16[640,640]{1,0:T(8,128)(2,1)}, u32[]{:S(2)}) copy-start(bf16[640,640]{1,0:T(8,128)(2,1)} %xq_ref.1) | copy-start | bytes 2457604
  11.6 5.2 %copy-start.12 = (f32[640]{0:T(1024)S(1)}, f32[640]{0:T(1024)}, u32[]{:S(2)}) copy-start(f32[640]{0:T(1024)} %xgain_ref.1) | copy-start | bytes 7684
  15.1 6.5 %collective-permute-start.3 = (bf16[77,2,640]{2,0,1:T(8,128)(2,1)S(1)}, bf16[77,2,640]{2,0,1:T(8,128)(2,1)S(1)}, u32[]{:S(2)}, u32[]{:S(2)}) collective-permute-start(bf16[77,2,640]{2,0,1:T(8,128)(2,1)S(1)} %collective-permute-done.2), channel_id=1, source_target_pairs={{0,8},{8,0},{16,24},{24,16},{1,9},{9,1},{17,25},{25,17},{2,10},{10... | collective-permute-start | bytes 591368 | tf_op jit(solution)/shard_map/ppermute | solution.py:253
  16.8 4.8 %copy-start.9 = (bf16[640,640]{1,0:T(8,128)(2,1)S(1)}, bf16[640,640]{1,0:T(8,128)(2,1)}, u32[]{:S(2)}) copy-start(bf16[640,640]{1,0:T(8,128)(2,1)} %xo_ref.1) | copy-start | bytes 2457604
  16.8 4.8 %copy-start.13 = (s32[16]{0:T(128)S(1)}, s32[16]{0:T(128)}, u32[]{:S(2)}) copy-start(s32[16]{0:T(128)} %slot_ref.1) | copy-start | bytes 196
  16.8 4.8 %copy-start.14 = (s32[2]{0:T(128)S(1)}, s32[2]{0:T(128)}, u32[]{:S(2)}) copy-start(s32[2]{0:T(128)} %gate_ref.1) | copy-start | bytes 28

commit v8 on v7

--- a/solution.py
+++ b/solution.py
@@ -130,10 +130,14 @@
     half = slots // 2
     total = cols * slots * rows * PAD
     side = 1 - first_row()
-    other = next_ref[...].reshape(-1, wide)
-    add = dot(other, pair_taps(w_ref, 2 * side))
-    for c in range(2):
-        part_ref[c, :, side * (rows - 1)] += add[:, c * width : (c + 1) * width].reshape(slots, PAD, width)
+    strip = lax.axis_index("strip")
+
+    @pl.when(jnp.where(side == 0, strip > 0, strip < lax.axis_size("strip") - 1))
+    def _():
+        add = dot(next_ref[...].reshape(-1, wide), pair_taps(w_ref, 2 * side))
+        for c in range(2):
+            part_ref[c, :, side * (rows - 1)] += add[:, c * width : (c + 1) * width].reshape(slots, PAD, width)
+
     normalize(part_ref, tgain_ref, wq_ref, normed, tq, pl.ds(side * (rows - 1), 1))
     both = dot(normed[...].reshape(total, width), jnp.concatenate([wk_ref[...], wv_ref[...]], axis=1))
     tk[...] = both[:, :width].astype(BF16)

time: 24.4 us -> 23.9 us (0.980)
  Pallas kernels: 12 us -> 11.1 us
  waiting for transfers between devices: 2.86 us -> 3.24 us
    pallas_call x1, Pallas kernels: 4.78 us -> 3.89 us  [on_device(): pl.pallas_call(functools.partial(time_kernel, frames), out_shape=(jax.Sha...]
    ppermute x1, waiting for transfers between devices: 0.01 us -> 0.39 us  [on_device(): swapped = lax.ppermute(fetched, 'strip', near_pairs)]
  transfers between devices with their start and end apart: 4 -> 4, of which waited for: 1 -> 2; matrix products, arithmetic and copies ran while one was open for 0% -> 0% of each run, Pallas kernels for 38% -> 35%
where the time goes in v8:
time: 23.9 us; the launch traced here: 23.7 us
  Pallas kernels  11.1 us (46%)
  starting transfers between devices  7.94 us (33%)
  waiting for transfers between devices  3.24 us (14%)
  local copies, waits for them, and re-layouts  1.16 us (5%)
  between operations  0.25 us (1%)
    ppermute x1, starting transfers between devices, on_device(): fetched = lax.ppermute(half, 'req', partner_pairs)  4.1 us
    pallas_call x1, Pallas kernels, on_device(): pl.pallas_call(functools.partial(time_kernel, frames), out_shape=(jax.Sha...  3.89 us
    pallas_call x1, Pallas kernels, on_device(): pl.pallas_call(conv_kernel, out_shape=(jax.ShapeDtypeStruct(grid, F32), j...  3.49 us
    ppermute x1, waiting for transfers between devices, on_device(): near = lax.ppermute(edge_act, 'strip', near_pairs)  2.85 us
    pallas_call x1, Pallas kernels, on_device(): pl.pallas_call(functools.partial(cross_kernel, frames), out_shape=jax.Sha...  2.58 us
    ppermute x1, starting transfers between devices, on_device(): swapped = lax.ppermute(fetched, 'strip', near_pairs)  1.61 us
    ppermute x1, starting transfers between devices, on_device(): near = lax.ppermute(edge_act, 'strip', near_pairs)  1.56 us
    unnamed x35, local copies, waits for them, and re-layouts  1.13 us
  transfers between devices with their start and end apart: 4, of which 2 were waited for; matrix products, arithmetic and copies ran while one was open for 0% of the time, Pallas kernels for 35%

profile of v8, /device:TPU:0, one launch (start us, length us, event | category | flops | bytes accessed | tf_op | source)
XLA Modules:
  0.0 23.7 jit_solution(16995044612507130931)
XLA Ops:
  0.0 1.0 %copy-done.1 = bf16[2,2,77,640]{3,1,2,0:T(2,128)(2,1)S(1)} copy-done((bf16[2,2,77,640]{3,1,2,0:T(2,128)(2,1)S(1)}, bf16[2,2,77,640]{3,1,2,0:T(2,128)(2,1)}, u32[]{:S(2)}) %copy-start.1) | copy-done | bytes 394264
  1.0 0.2 %pages.1 = bf16[77,2,640]{2,1,0:T(2,128)(2,1)S(1)} custom-call(bf16[2,77,2,640]{3,2,1,0:T(2,128)(2,1)S(1)} %bitcast.9), custom_call_target="tpu_custom_call" | custom-call | flops 3000000000 | tf_op jit(solution)/shard_map/pages/pallas_call | solution.py:246
  1.3 4.1 %collective-permute-start.2 = (bf16[77,2,640]{2,0,1:T(8,128)(2,1)S(1)}, bf16[77,2,640]{2,0,1:T(8,128)(2,1)S(1)}, u32[]{:S(2)}, u32[]{:S(2)}) collective-permute-start(bf16[77,2,640]{2,0,1:T(8,128)(2,1)S(1)} %copy.19), channel_id=1, source_target_pairs={{0,4},{1,5},{2,6},{3,7},{4,0},{5,1},{6,2},{7,3},{8,12},{9,13},{10,... | collective-permute-start | bytes 591368 | tf_op jit(solution)/shard_map/ppermute | solution.py:256
  5.4 0.3 %edge.1 = (bf16[4,16,1280]{2,1,0:T(8,128)(2,1)S(1)}, bf16[4,16,1280]{2,1,0:T(8,128)(2,1)S(1)}) custom-call(bf16[4,4,14,2,640]{4,3,2,1,0:T(2,128)(2,1)S(1)} %bitcast.10, f32[640]{0:T(1024)S(1)} %copy-done.11), custom_call_target="tpu_custom_call" | custom-call | flops 16000000000 | tf_op jit(solution)/shard_map/edge/pallas_call | solution.py:262
  5.8 0.0 copy-start
  5.8 0.0 copy-start.3
  5.8 0.0 copy-start.4
  5.8 1.6 %collective-permute-start = (bf16[4,16,1280]{2,1,0:T(8,128)(2,1)S(1)}, bf16[4,16,1280]{2,1,0:T(8,128)(2,1)S(1)}, u32[]{:S(2)}, u32[]{:S(2)}) collective-permute-start(bf16[4,16,1280]{2,1,0:T(8,128)(2,1)S(1)} %get-tuple-element.16.edge_act_ref), channel_id=1, source_target_pairs={{0,8},{8,0},{16,24},{24,16},{1,9},{9,1},{17,25},{25,17},{2,10},{10... | collective-permute-start | bytes 491528 | tf_op jit(solution)/shard_map/ppermute | solution.py:271
  7.4 0.6 %activate.1 = (bf16[4,4,16,1280]{3,2,1,0:T(8,128)(2,1)S(1)}, bf16[4,4,16,1280]{3,2,1,0:T(8,128)(2,1)S(1)}, bf16[4,16,1280]{2,1,0:T(8,128)(2,1)S(1)}) custom-call(bf16[4,4,14,2,640]{4,3,2,1,0:T(2,128)(2,1)S(1)} %bitcast.11, f32[640]{0:T(1024)S(1)} %copy-done.11, bf16[4,16,1280]{2,1,0:T(8,128)(2,1)S(1)} %get-tuple-element.15.edge_x_ref, ...), custom_call_target="tpu_custom_call" | custom-call | flops 300000000 | tf_op jit(solution)/shard_map/activate/pallas_call | solution.py:272
  7.9 0.7 %collective-permute-start.1 = (bf16[4,16,1280]{2,1,0:T(8,128)(2,1)S(1)}, bf16[4,16,1280]{2,1,0:T(8,128)(2,1)S(1)}, u32[]{:S(2)}, u32[]{:S(2)}) collective-permute-start(bf16[4,16,1280]{2,1,0:T(8,128)(2,1)S(1)} %get-tuple-element.22), channel_id=1, source_target_pairs={{8,16},{16,8},{9,17},{17,9},{10,18},{18,10},{11,19},{19,11},{12,20... | collective-permute-start | bytes 491528 | tf_op jit(solution)/shard_map/ppermute | solution.py:281
  8.7 2.9 %collective-permute-done.near_ref = bf16[4,16,1280]{2,1,0:T(8,128)(2,1)S(1)} collective-permute-done((bf16[4,16,1280]{2,1,0:T(8,128)(2,1)S(1)}, bf16[4,16,1280]{2,1,0:T(8,128)(2,1)S(1)}, u32[]{:S(2)}, u32[]{:S(2)}) %collective-permute-start) | collective-permute-done | bytes 163872 | tf_op jit(solution)/shard_map/ppermute | solution.py:271
  11.6 0.0 copy-start.5
  11.6 0.0 copy-start.6
  11.6 0.0 copy-start.7
  11.6 0.0 copy-start.8
  11.6 0.0 copy-start.12
  11.6 3.5 %conv_own.1 = (f32[2,4,4,16,640]{4,3,2,1,0:T(8,128)S(1)}, bf16[2,4,4,16,640]{4,3,2,1,0:T(8,128)(2,1)S(1)}, bf16[2,4,4,16,640]{4,3,2,1,0:T(8,128)(2,1)S(1)}) custom-call(bf16[4,4,16,1280]{3,2,1,0:T(8,128)(2,1)S(1)} %get-tuple-element.17.x_ref, bf16[4,4,16,1280]{3,2,1,0:T(8,128)(2,1)S(1)} %get-tuple-element.18.act_ref, ...), custom_call_target="tpu_custom_call" | custom-call | flops 300000000 | tf_op jit(solution)/shard_map/conv_own/pallas_call | solution.py:283
  15.1 1.6 %collective-permute-start.3 = (bf16[77,2,640]{2,0,1:T(8,128)(2,1)S(1)}, bf16[77,2,640]{2,0,1:T(8,128)(2,1)S(1)}, u32[]{:S(2)}, u32[]{:S(2)}) collective-permute-start(bf16[77,2,640]{2,0,1:T(8,128)(2,1)S(1)} %collective-permute-done.2), channel_id=1, source_target_pairs={{0,8},{8,0},{16,24},{24,16},{1,9},{9,1},{17,25},{25,17},{2,10},{10... | collective-permute-start | bytes 591368 | tf_op jit(solution)/shard_map/ppermute | solution.py:257
  16.8 0.0 copy-start.9
  16.8 0.0 copy-start.13
  16.8 0.0 copy-start.14
  16.8 3.9 %time_mix.1 = (f32[2,4,4,16,640]{4,3,2,1,0:T(8,128)S(1)}, bf16[2,4,4,16,640]{4,3,2,1,0:T(8,128)(2,1)S(1)}, bf16[2,4,4,16,640]{4,3,2,1,0:T(8,128)(2,1)S(1)}, bf16[2,2,4,16,640]{4,3,2,1,0:T(8,128)(2,1)S(1)}) custom-call(f32[2,4,4,16,640]{4,3,2,1,0:T(8,128)S(1)} %get-tuple-element.19.part_ref, ...), custom_call_target="tpu_custom_call", output_to_operand_aliasing={{0}: (0, {}), {1}: (1, {}), {2}: (2, {})} | custom-call | flops 6000000000 | tf_op jit(solution)/shard_map/time_mix/pallas_call | solution.py:293
  20.7 0.4 %collective-permute-done.3 = bf16[77,2,640]{2,0,1:T(8,128)(2,1)S(1)} collective-permute-done((bf16[77,2,640]{2,0,1:T(8,128)(2,1)S(1)}, bf16[77,2,640]{2,0,1:T(8,128)(2,1)S(1)}, u32[]{:S(2)}, u32[]{:S(2)}) %collective-permute-start.3) | collective-permute-done | bytes 197152 | tf_op jit(solution)/shard_map/ppermute | solution.py:257
  21.1 2.6 %cross_mix.1 = bf16[2,4,14,2,640]{4,3,2,1,0:T(2,128)(2,1)} custom-call(s32[16]{0:T(128)S(1)} %copy-done.13, s32[2]{0:T(128)S(1)} %copy-done.14, f32[2,4,4,16,640]{4,3,2,1,0:T(8,128)S(1)} %get-tuple-element.23.after_ref, bf16[2,2,4,16,640]{4,3,2,1,0:T(8,128)(2,1)S(1)} %get-tuple-element.24.query_ref, bf16[2,2,77,640]{3,2,1,0:T(8,128)(2,1)S(1)} %copy.20.own_ref, ...), custom_call_target="tpu_custom_call" | custom-call | flops 1000000000 | tf_op jit(solution)/shard_map/cross_mix/pallas_call | solution.py:313
  (27 shorter events, 0.1 us)
Async XLA Ops:
  0.0 1.0 %copy-start.1 = (bf16[2,2,77,640]{3,1,2,0:T(2,128)(2,1)S(1)}, bf16[2,2,77,640]{3,1,2,0:T(2,128)(2,1)}, u32[]{:S(2)}) copy-start(bf16[2,2,77,640]{3,1,2,0:T(2,128)(2,1)} %param.18) | copy-start | bytes 1182724
  1.0 4.4 %copy-start.10 = (bf16[2,2,4,2,14,640]{5,3,4,2,1,0:T(2,128)(2,1)S(1)}, bf16[2,2,4,2,14,640]{5,3,4,2,1,0:T(2,128)(2,1)}, u32[]{:S(2)}) copy-start(bf16[2,2,4,2,14,640]{5,3,4,2,1,0:T(2,128)(2,1)} %param.15) | copy-start | bytes 1720324
  1.0 4.4 %copy-start.11 = (f32[640]{0:T(1024)S(1)}, f32[640]{0:T(1024)}, u32[]{:S(2)}) copy-start(f32[640]{0:T(1024)} %gain_ref.3) | copy-start | bytes 7684
  1.3 13.8 %collective-permute-start.2 = (bf16[77,2,640]{2,0,1:T(8,128)(2,1)S(1)}, bf16[77,2,640]{2,0,1:T(8,128)(2,1)S(1)}, u32[]{:S(2)}, u32[]{:S(2)}) collective-permute-start(bf16[77,2,640]{2,0,1:T(8,128)(2,1)S(1)} %copy.19), channel_id=1, source_target_pairs={{0,4},{1,5},{2,6},{3,7},{4,0},{5,1},{6,2},{7,3},{8,12},{9,13},{10,... | collective-permute-start | bytes 591368 | tf_op jit(solution)/shard_map/ppermute | solution.py:256
  5.4 6.1 %slice-start = ((s8[7372800]{0:T(1024)(128)(4,1)}), s8[4194304]{0:T(1024)(128)(4,1)S(1)}, s32[]{:S(2)}) async-start(s8[7372800]{0:T(1024)(128)(4,1)} %bitcast.7), calls=%async_computation | async-start | bytes 8388608
  5.4 3.2 %copy-start.2 = (bf16[2,2,77,640]{3,1,2,0:T(2,128)(2,1)S(1)}, bf16[2,2,77,640]{3,1,2,0:T(2,128)(2,1)}, u32[]{:S(2)}) copy-start(bf16[2,2,77,640]{3,1,2,0:T(2,128)(2,1)} %param.18) | copy-start | bytes 1182724
  5.4 6.1 %slice-start.1 = ((s8[7372800]{0:T(1024)(128)(4,1)}), s8[3178496]{0:T(1024)(128)(4,1)S(1)}, s32[]{:S(2)}) async-start(s8[7372800]{0:T(1024)(128)(4,1)} %bitcast.7), calls=%async_computation.1 | async-start | bytes 6356992
  5.8 5.8 %copy-start = (bf16[640,640]{1,0:T(8,128)(2,1)S(1)}, bf16[640,640]{1,0:T(8,128)(2,1)}, u32[]{:S(2)}) copy-start(bf16[640,640]{1,0:T(8,128)(2,1)} %wq_ref.3) | copy-start | bytes 2457604
  5.8 5.8 %copy-start.3 = (f32[640]{0:T(1024)S(1)}, f32[640]{0:T(1024)}, u32[]{:S(2)}) copy-start(f32[640]{0:T(1024)} %bias_ref.1) | copy-start | bytes 7684
  5.8 5.8 %copy-start.4 = (f32[640]{0:T(1024)S(1)}, f32[640]{0:T(1024)}, u32[]{:S(2)}) copy-start(f32[640]{0:T(1024)} %tgain_ref.3) | copy-start | bytes 7684
  5.8 5.7 %collective-permute-start = (bf16[4,16,1280]{2,1,0:T(8,128)(2,1)S(1)}, bf16[4,16,1280]{2,1,0:T(8,128)(2,1)S(1)}, u32[]{:S(2)}, u32[]{:S(2)}) collective-permute-start(bf16[4,16,1280]{2,1,0:T(8,128)(2,1)S(1)} %get-tuple-element.16.edge_act_ref), channel_id=1, source_target_pairs={{0,8},{8,0},{16,24},{24,16},{1,9},{9,1},{17,25},{25,17},{2,10},{10... | collective-permute-start | bytes 491528 | tf_op jit(solution)/shard_map/ppermute | solution.py:271
  7.9 8.8 %collective-permute-start.1 = (bf16[4,16,1280]{2,1,0:T(8,128)(2,1)S(1)}, bf16[4,16,1280]{2,1,0:T(8,128)(2,1)S(1)}, u32[]{:S(2)}, u32[]{:S(2)}) collective-permute-start(bf16[4,16,1280]{2,1,0:T(8,128)(2,1)S(1)} %get-tuple-element.22), channel_id=1, source_target_pairs={{8,16},{16,8},{9,17},{17,9},{10,18},{18,10},{11,19},{19,11},{12,20... | collective-permute-start | bytes 491528 | tf_op jit(solution)/shard_map/ppermute | solution.py:281
  11.6 5.2 %copy-start.5 = (bf16[640,640]{1,0:T(8,128)(2,1)S(1)}, bf16[640,640]{1,0:T(8,128)(2,1)}, u32[]{:S(2)}) copy-start(bf16[640,640]{1,0:T(8,128)(2,1)} %wk_ref.1) | copy-start | bytes 2457604
  11.6 5.2 %copy-start.6 = (bf16[640,640]{1,0:T(8,128)(2,1)S(1)}, bf16[640,640]{1,0:T(8,128)(2,1)}, u32[]{:S(2)}) copy-start(bf16[640,640]{1,0:T(8,128)(2,1)} %wv_ref.1) | copy-start | bytes 2457604
  11.6 5.2 %copy-start.7 = (bf16[640,640]{1,0:T(8,128)(2,1)S(1)}, bf16[640,640]{1,0:T(8,128)(2,1)}, u32[]{:S(2)}) copy-start(bf16[640,640]{1,0:T(8,128)(2,1)} %wo_ref.1) | copy-start | bytes 2457604
  11.6 5.2 %copy-start.8 = (bf16[640,640]{1,0:T(8,128)(2,1)S(1)}, bf16[640,640]{1,0:T(8,128)(2,1)}, u32[]{:S(2)}) copy-start(bf16[640,640]{1,0:T(8,128)(2,1)} %xq_ref.1) | copy-start | bytes 2457604
  11.6 5.2 %copy-start.12 = (f32[640]{0:T(1024)S(1)}, f32[640]{0:T(1024)}, u32[]{:S(2)}) copy-start(f32[640]{0:T(1024)} %xgain_ref.1) | copy-start | bytes 7684
  15.1 6.0 %collective-permute-start.3 = (bf16[77,2,640]{2,0,1:T(8,128)(2,1)S(1)}, bf16[77,2,640]{2,0,1:T(8,128)(2,1)S(1)}, u32[]{:S(2)}, u32[]{:S(2)}) collective-permute-start(bf16[77,2,640]{2,0,1:T(8,128)(2,1)S(1)} %collective-permute-done.2), channel_id=1, source_target_pairs={{0,8},{8,0},{16,24},{24,16},{1,9},{9,1},{17,25},{25,17},{2,10},{10... | collective-permute-start | bytes 591368 | tf_op jit(solution)/shard_map/ppermute | solution.py:257
  16.8 4.3 %copy-start.9 = (bf16[640,640]{1,0:T(8,128)(2,1)S(1)}, bf16[640,640]{1,0:T(8,128)(2,1)}, u32[]{:S(2)}) copy-start(bf16[640,640]{1,0:T(8,128)(2,1)} %xo_ref.1) | copy-start | bytes 2457604
  16.8 4.3 %copy-start.13 = (s32[16]{0:T(128)S(1)}, s32[16]{0:T(128)}, u32[]{:S(2)}) copy-start(s32[16]{0:T(128)} %slot_ref.1) | copy-start | bytes 196
  16.8 4.3 %copy-start.14 = (s32[2]{0:T(128)S(1)}, s32[2]{0:T(128)}, u32[]{:S(2)}) copy-start(s32[2]{0:T(128)} %gate_ref.1) | copy-start | bytes 28

commit v9 on v8

--- a/solution.py
+++ b/solution.py
@@ -122,9 +122,16 @@
 
 
 def time_kernel(
-    frames, part_ref, normed, tq, next_ref, w_ref, tgain_ref, wq_ref, wk_ref, wv_ref, wo_ref,
-    xgain_ref, xq_ref, after_ref, _normed, _tq, query_ref, tk, tv, mixed, scores, chances
+    frames, slot_ref, gate_ref, part_ref, normed, tq, next_ref, w_ref, tgain_ref, wq_ref, wk_ref, wv_ref, wo_ref,
+    xgain_ref, xq_ref, after_ref, _normed, _tq, query_ref, choice_ref, live_ref, tk, tv, mixed, scores, chances,
+    slot, gate, sems
 ):
+    loads = [
+        pltpu.make_async_copy(slot_ref, slot, sems.at[0]),
+        pltpu.make_async_copy(gate_ref, gate, sems.at[1]),
+    ]
+    for load in loads:
+        load.start()
     cols, slots, rows, _, width = part_ref.shape
     wide = 2 * width
     half = slots // 2
@@ -171,10 +178,20 @@
     after_ref[...] = part_ref[...] + dot(mixed[...], wo_ref[...]).reshape(after_ref.shape)
     nc = rms(after_ref[:, :half], xgain_ref[...]).astype(BF16).reshape(-1, width)
     query_ref[...] = dot(nc, xq_ref[...]).astype(BF16).reshape(query_ref.shape)
+    for load in loads:
+        load.wait()
+    first_page = lax.axis_index("req") * REQ_DEV
+    for r in range(half):
+        page = slot[first_page + r]
+        i = lax.rem(page, REQ_DEV)
+        place = i + jnp.where(page - i == first_page, 0, REQ_DEV)
+        for j in range(2 * REQ_DEV):
+            choice_ref[r, j] = jnp.full(choice_ref.shape[2:], jnp.where(place == j, 1.0, 0.0), F32).astype(BF16)
+        live_ref[r] = jnp.full(live_ref.shape[1:], jnp.where(gate[r] == 1, 1.0, 0.0), F32)
 
 
 def cross_kernel(
-    frames, slot_ref, gate_ref, after_ref, query_ref, own_ref, fetched_ref, swapped_ref, xo_ref, out_ref, keys, values, scores, chances, mixed, made, sems
+    frames, choice_ref, live_ref, after_ref, query_ref, own_ref, fetched_ref, swapped_ref, xo_ref, out_ref, keys, values, scores, chances, mixed, made, sems
 ):
     cols, slots, rows, _, width = after_ref.shape
     half = slots // 2
@@ -183,13 +200,14 @@
     room = -(-tokens // 128) * 128
     group = cols * rows * PAD
     pair = 2 * HEAD_DIM
-    first_page = lax.axis_index("req") * REQ_DEV
     for r in range(half):
-        page = slot_ref[first_page + r]
-        i = lax.rem(page, REQ_DEV)
-        mine = page - i == first_page
-        k = jnp.where(mine, own_ref[0, i], jnp.where(even, fetched_ref[i], swapped_ref[i]))
-        v = jnp.where(mine, own_ref[1, i], jnp.where(even, swapped_ref[i], fetched_ref[i]))
+        k = v = jnp.zeros((tokens, width), BF16)
+        for i in range(REQ_DEV):
+            mine, theirs = (choice_ref[r, j, 0:1] for j in (i, REQ_DEV + i))
+            far_k = jnp.where(even, fetched_ref[i], swapped_ref[i])
+            far_v = jnp.where(even, swapped_ref[i], fetched_ref[i])
+            k += own_ref[0, i] * mine + far_k * theirs
+            v += own_ref[1, i] * mine + far_v * theirs
         tail = jnp.zeros((room - tokens, width), BF16)
         keys[r] = jnp.concatenate([k, tail], axis=0)
         values[r] = jnp.concatenate([v, tail], axis=0)
@@ -213,7 +231,7 @@
         for c in range(cols):
             cond = (after_ref[c, r] + add[c, r]).astype(BF16).astype(F32)
             uncond = after_ref[c, half + r].astype(BF16).astype(F32)
-            guided = jnp.where(gate_ref[r] == 1, uncond + scale * (cond - uncond), cond)
+            guided = jnp.where(live_ref[r] == 1.0, uncond + scale * (cond - uncond), cond)
             for w in range(rows):
                 made[r, w, :, c, :] = guided[w, :frames].astype(BF16)
         copies.append(pltpu.make_async_copy(made.at[r], out_ref.at[r], sems.at[r]))
@@ -236,7 +254,6 @@
     )
 
     vm = pl.BlockSpec(memory_space=pltpu.VMEM)
-    sm = pl.BlockSpec(memory_space=pltpu.SMEM)
     any_ = pl.BlockSpec(memory_space=pl.ANY)
     total = cols * slots * rows * PAD
     wide = cols * width
@@ -290,30 +307,33 @@
         cost_estimate=cost(COST1),
         name="conv_own",
     )(x, act, near, conv_weight, conv_bias, temporal_gain, temporal_query)
-    after, _, _, query = pl.pallas_call(
+    after, _, _, query, choice, live = pl.pallas_call(
         functools.partial(time_kernel, frames),
         out_shape=(
             jax.ShapeDtypeStruct(grid, F32),
             jax.ShapeDtypeStruct(grid, BF16),
             jax.ShapeDtypeStruct(grid, BF16),
             jax.ShapeDtypeStruct((cols, REQ_DEV, rows, PAD, width), BF16),
+            jax.ShapeDtypeStruct((REQ_DEV, 2 * REQ_DEV, PAD, width), BF16),
+            jax.ShapeDtypeStruct((REQ_DEV, PAD, width), F32),
         ),
-        in_specs=[vm] * 12,
-        out_specs=(vm,) * 4,
+        in_specs=[any_] * 2 + [vm] * 12,
+        out_specs=(vm,) * 6,
         scratch_shapes=[pltpu.VMEM((total, width), BF16)] * 3
-        + [pltpu.VMEM((total, width // HEAD_DIM * rows * PAD), kind) for kind in (F32, BF16)],
-        input_output_aliases={0: 0, 1: 1, 2: 2},
+        + [pltpu.VMEM((total, width // HEAD_DIM * rows * PAD), kind) for kind in (F32, BF16)]
+        + [pltpu.SMEM(context_slot.shape, jnp.int32), pltpu.SMEM(gate.shape, jnp.int32), pltpu.SemaphoreType.DMA((2,))],
+        input_output_aliases={2: 0, 3: 1, 4: 2},
         compiler_params=pltpu.CompilerParams(vmem_limit_bytes=16 << 20),
         cost_estimate=cost(COST2),
         name="time_mix",
     )(
-        part, normed, queries, other, conv_weight, temporal_gain, temporal_query, temporal_key, temporal_value,
+        context_slot, gate, part, normed, queries, other, conv_weight, temporal_gain, temporal_query, temporal_key, temporal_value,
         temporal_out, cross_gain, cross_query,
     )
     out = pl.pallas_call(
         functools.partial(cross_kernel, frames),
         out_shape=jax.ShapeDtypeStruct((REQ_DEV, rows, frames, cols, width), BF16),
-        in_specs=[sm, sm] + [vm] * 6,
+        in_specs=[vm] * 8,
         out_specs=any_,
         scratch_shapes=[pltpu.VMEM((REQ_DEV, room, width), BF16)] * 2
         + [
@@ -326,7 +346,7 @@
         compiler_params=pltpu.CompilerParams(vmem_limit_bytes=16 << 20),
         cost_estimate=cost(COST3),
         name="cross_mix",
-    )(context_slot, gate, after, query, context_pages, fetched, swapped, cross_out)
+    )(choice, live, after, query, context_pages, fetched, swapped, cross_out)
     return out.transpose(0, 1, 3, 2, 4)
 
 

time: 23.9 us -> 23.4 us (0.979)
  Pallas kernels: 11.1 us -> 10.6 us
    pallas_call x1, Pallas kernels: 2.58 us -> 2.11 us  [on_device(): pl.pallas_call(functools.partial(cross_kernel, frames), out_shape=jax.Sha...]
  transfers between devices with their start and end apart: 4 -> 4, of which waited for: 2 -> 2; matrix products, arithmetic and copies ran while one was open for 0% -> 0% of each run, Pallas kernels for 35% -> 36%
where the time goes in v9:
time: 23.4 us; the launch traced here: 23.2 us
  Pallas kernels  10.6 us (45%)
  starting transfers between devices  7.78 us (33%)
  waiting for transfers between devices  3.39 us (14%)
  local copies, waits for them, and re-layouts  1.16 us (5%)
  between operations  0.26 us (1%)
    ppermute x1, starting transfers between devices, on_device(): fetched = lax.ppermute(half, 'req', partner_pairs)  4.1 us
    pallas_call x1, Pallas kernels, on_device(): pl.pallas_call(functools.partial(time_kernel, frames), out_shape=(jax.Sha...  3.94 us
    pallas_call x1, Pallas kernels, on_device(): pl.pallas_call(conv_kernel, out_shape=(jax.ShapeDtypeStruct(grid, F32), j...  3.43 us
    ppermute x1, waiting for transfers between devices, on_device(): near = lax.ppermute(edge_act, 'strip', near_pairs)  2.85 us
    pallas_call x1, Pallas kernels, on_device(): pl.pallas_call(functools.partial(cross_kernel, frames), out_shape=jax.Sha...  2.11 us
    ppermute x1, starting transfers between devices, on_device(): near = lax.ppermute(edge_act, 'strip', near_pairs)  1.56 us
    ppermute x1, starting transfers between devices, on_device(): swapped = lax.ppermute(fetched, 'strip', near_pairs)  1.45 us
    unnamed x35, local copies, waits for them, and re-layouts  1.13 us
  transfers between devices with their start and end apart: 4, of which 2 were waited for; matrix products, arithmetic and copies ran while one was open for 0% of the time, Pallas kernels for 36%

profile of v9, /device:TPU:0, one launch (start us, length us, event | category | flops | bytes accessed | tf_op | source)
XLA Modules:
  0.0 23.2 jit_solution(2901614554789519759)
XLA Ops:
  0.0 1.0 %copy-done.2 = bf16[2,2,77,640]{3,1,2,0:T(2,128)(2,1)S(1)} copy-done((bf16[2,2,77,640]{3,1,2,0:T(2,128)(2,1)S(1)}, bf16[2,2,77,640]{3,1,2,0:T(2,128)(2,1)}, u32[]{:S(2)}) %copy-start.2) | copy-done | bytes 394264
  1.0 0.2 %pages.1 = bf16[77,2,640]{2,1,0:T(2,128)(2,1)S(1)} custom-call(bf16[2,77,2,640]{3,2,1,0:T(2,128)(2,1)S(1)} %bitcast.9), custom_call_target="tpu_custom_call" | custom-call | flops 3000000000 | tf_op jit(solution)/shard_map/pages/pallas_call | solution.py:263
  1.3 4.1 %collective-permute-start.2 = (bf16[77,2,640]{2,0,1:T(8,128)(2,1)S(1)}, bf16[77,2,640]{2,0,1:T(8,128)(2,1)S(1)}, u32[]{:S(2)}, u32[]{:S(2)}) collective-permute-start(bf16[77,2,640]{2,0,1:T(8,128)(2,1)S(1)} %copy.19), channel_id=1, source_target_pairs={{0,4},{1,5},{2,6},{3,7},{4,0},{5,1},{6,2},{7,3},{8,12},{9,13},{10,... | collective-permute-start | bytes 591368 | tf_op jit(solution)/shard_map/ppermute | solution.py:273
  5.4 0.3 %edge.1 = (bf16[4,16,1280]{2,1,0:T(8,128)(2,1)S(1)}, bf16[4,16,1280]{2,1,0:T(8,128)(2,1)S(1)}) custom-call(bf16[4,4,14,2,640]{4,3,2,1,0:T(2,128)(2,1)S(1)} %bitcast.12, f32[640]{0:T(1024)S(1)} %copy-done.11), custom_call_target="tpu_custom_call" | custom-call | flops 16000000000 | tf_op jit(solution)/shard_map/edge/pallas_call | solution.py:279
  5.8 0.0 copy-start.1
  5.8 0.0 copy-start.4
  5.8 0.0 copy-start.5
  5.8 1.6 %collective-permute-start = (bf16[4,16,1280]{2,1,0:T(8,128)(2,1)S(1)}, bf16[4,16,1280]{2,1,0:T(8,128)(2,1)S(1)}, u32[]{:S(2)}, u32[]{:S(2)}) collective-permute-start(bf16[4,16,1280]{2,1,0:T(8,128)(2,1)S(1)} %get-tuple-element.18.edge_act_ref), channel_id=1, source_target_pairs={{0,8},{8,0},{16,24},{24,16},{1,9},{9,1},{17,25},{25,17},{2,10},{10... | collective-permute-start | bytes 491528 | tf_op jit(solution)/shard_map/ppermute | solution.py:288
  7.4 0.6 %activate.1 = (bf16[4,4,16,1280]{3,2,1,0:T(8,128)(2,1)S(1)}, bf16[4,4,16,1280]{3,2,1,0:T(8,128)(2,1)S(1)}, bf16[4,16,1280]{2,1,0:T(8,128)(2,1)S(1)}) custom-call(bf16[4,4,14,2,640]{4,3,2,1,0:T(2,128)(2,1)S(1)} %bitcast.13, f32[640]{0:T(1024)S(1)} %copy-done.11, bf16[4,16,1280]{2,1,0:T(8,128)(2,1)S(1)} %get-tuple-element.17.edge_x_ref, ...), custom_call_target="tpu_custom_call" | custom-call | flops 300000000 | tf_op jit(solution)/shard_map/activate/pallas_call | solution.py:289
  7.9 0.7 %collective-permute-start.1 = (bf16[4,16,1280]{2,1,0:T(8,128)(2,1)S(1)}, bf16[4,16,1280]{2,1,0:T(8,128)(2,1)S(1)}, u32[]{:S(2)}, u32[]{:S(2)}) collective-permute-start(bf16[4,16,1280]{2,1,0:T(8,128)(2,1)S(1)} %get-tuple-element.24), channel_id=1, source_target_pairs={{8,16},{16,8},{9,17},{17,9},{10,18},{18,10},{11,19},{19,11},{12,20... | collective-permute-start | bytes 491528 | tf_op jit(solution)/shard_map/ppermute | solution.py:298
  8.7 2.9 %collective-permute-done.near_ref = bf16[4,16,1280]{2,1,0:T(8,128)(2,1)S(1)} collective-permute-done((bf16[4,16,1280]{2,1,0:T(8,128)(2,1)S(1)}, bf16[4,16,1280]{2,1,0:T(8,128)(2,1)S(1)}, u32[]{:S(2)}, u32[]{:S(2)}) %collective-permute-start) | collective-permute-done | bytes 163872 | tf_op jit(solution)/shard_map/ppermute | solution.py:288
  11.6 0.0 copy-start.6
  11.6 0.0 copy-start.7
  11.6 0.0 copy-start.8
  11.6 0.0 copy-start.9
  11.6 0.0 copy-start.12
  11.6 0.0 copy-start.13
  11.6 0.0 copy-start.14
  11.7 3.4 %conv_own.1 = (f32[2,4,4,16,640]{4,3,2,1,0:T(8,128)S(1)}, bf16[2,4,4,16,640]{4,3,2,1,0:T(8,128)(2,1)S(1)}, bf16[2,4,4,16,640]{4,3,2,1,0:T(8,128)(2,1)S(1)}) custom-call(bf16[4,4,16,1280]{3,2,1,0:T(8,128)(2,1)S(1)} %get-tuple-element.19.x_ref, bf16[4,4,16,1280]{3,2,1,0:T(8,128)(2,1)S(1)} %get-tuple-element.20.act_ref, ...), custom_call_target="tpu_custom_call" | custom-call | flops 300000000 | tf_op jit(solution)/shard_map/conv_own/pallas_call | solution.py:300
  15.1 1.5 %collective-permute-start.3 = (bf16[77,2,640]{2,0,1:T(8,128)(2,1)S(1)}, bf16[77,2,640]{2,0,1:T(8,128)(2,1)S(1)}, u32[]{:S(2)}, u32[]{:S(2)}) collective-permute-start(bf16[77,2,640]{2,0,1:T(8,128)(2,1)S(1)} %collective-permute-done.2), channel_id=1, source_target_pairs={{0,8},{8,0},{16,24},{24,16},{1,9},{9,1},{17,25},{25,17},{2,10},{10... | collective-permute-start | bytes 591368 | tf_op jit(solution)/shard_map/ppermute | solution.py:274
  16.6 0.0 copy-start
  16.6 3.9 %time_mix.1 = (f32[2,4,4,16,640]{4,3,2,1,0:T(8,128)S(1)}, bf16[2,4,4,16,640]{4,3,2,1,0:T(8,128)(2,1)S(1)}, bf16[2,4,4,16,640]{4,3,2,1,0:T(8,128)(2,1)S(1)}, bf16...) custom-call(s32[16]{0:T(128)S(1)} %copy-done.13, ...), custom_call_target="tpu_custom_call", output_to_operand_aliasing={{0}: (2, {}), {1}: (3, {}), {2}: (4, {})} | custom-call | flops 6000000000 | tf_op jit(solution)/shard_map/time_mix/pallas_call | solution.py:310
  20.6 0.5 %collective-permute-done.3 = bf16[77,2,640]{2,0,1:T(8,128)(2,1)S(1)} collective-permute-done((bf16[77,2,640]{2,0,1:T(8,128)(2,1)S(1)}, bf16[77,2,640]{2,0,1:T(8,128)(2,1)S(1)}, u32[]{:S(2)}, u32[]{:S(2)}) %collective-permute-start.3) | collective-permute-done | bytes 197152 | tf_op jit(solution)/shard_map/ppermute | solution.py:274
  21.1 2.1 %cross_mix.1 = bf16[2,4,14,2,640]{4,3,2,1,0:T(2,128)(2,1)} custom-call(bf16[2,4,16,640]{3,2,1,0:T(8,128)(2,1)S(1)} %get-tuple-element.25.choice_ref, f32[2,16,640]{2,1,0:T(8,128)S(1)} %get-tuple-element.26.live_ref, f32[2,4,4,16,640]{4,3,2,1,0:T(8,128)S(1)} %get-tuple-element.27.after_ref, bf16[2,2,4,16,640]{4,3,2,1,0:T(8,128)(2,1)S(1)} %get-tuple-element.28.query_ref, ...), custom_call_target="tpu_custom_call" | custom-call | flops 1000000000 | tf_op jit(solution)/shard_map/cross_mix/pallas_call | solution.py:333
  (27 shorter events, 0.1 us)
Async XLA Ops:
  0.0 1.0 %copy-start.2 = (bf16[2,2,77,640]{3,1,2,0:T(2,128)(2,1)S(1)}, bf16[2,2,77,640]{3,1,2,0:T(2,128)(2,1)}, u32[]{:S(2)}) copy-start(bf16[2,2,77,640]{3,1,2,0:T(2,128)(2,1)} %param.18) | copy-start | bytes 1182724
  1.0 4.4 %copy-start.10 = (bf16[2,2,4,2,14,640]{5,3,4,2,1,0:T(2,128)(2,1)S(1)}, bf16[2,2,4,2,14,640]{5,3,4,2,1,0:T(2,128)(2,1)}, u32[]{:S(2)}) copy-start(bf16[2,2,4,2,14,640]{5,3,4,2,1,0:T(2,128)(2,1)} %param.15) | copy-start | bytes 1720324
  1.0 4.4 %copy-start.11 = (f32[640]{0:T(1024)S(1)}, f32[640]{0:T(1024)}, u32[]{:S(2)}) copy-start(f32[640]{0:T(1024)} %gain_ref.3) | copy-start | bytes 7684
  1.3 13.8 %collective-permute-start.2 = (bf16[77,2,640]{2,0,1:T(8,128)(2,1)S(1)}, bf16[77,2,640]{2,0,1:T(8,128)(2,1)S(1)}, u32[]{:S(2)}, u32[]{:S(2)}) collective-permute-start(bf16[77,2,640]{2,0,1:T(8,128)(2,1)S(1)} %copy.19), channel_id=1, source_target_pairs={{0,4},{1,5},{2,6},{3,7},{4,0},{5,1},{6,2},{7,3},{8,12},{9,13},{10,... | collective-permute-start | bytes 591368 | tf_op jit(solution)/shard_map/ppermute | solution.py:273
  5.4 6.1 %slice-start = ((s8[7372800]{0:T(1024)(128)(4,1)}), s8[4194304]{0:T(1024)(128)(4,1)S(1)}, s32[]{:S(2)}) async-start(s8[7372800]{0:T(1024)(128)(4,1)} %bitcast.7), calls=%async_computation | async-start | bytes 8388608
  5.4 3.2 %copy-start.3 = (bf16[2,2,77,640]{3,1,2,0:T(2,128)(2,1)S(1)}, bf16[2,2,77,640]{3,1,2,0:T(2,128)(2,1)}, u32[]{:S(2)}) copy-start(bf16[2,2,77,640]{3,1,2,0:T(2,128)(2,1)} %param.18) | copy-start | bytes 1182724
  5.4 6.1 %slice-start.1 = ((s8[7372800]{0:T(1024)(128)(4,1)}), s8[3178496]{0:T(1024)(128)(4,1)S(1)}, s32[]{:S(2)}) async-start(s8[7372800]{0:T(1024)(128)(4,1)} %bitcast.7), calls=%async_computation.1 | async-start | bytes 6356992
  5.8 5.8 %copy-start.1 = (bf16[640,640]{1,0:T(8,128)(2,1)S(1)}, bf16[640,640]{1,0:T(8,128)(2,1)}, u32[]{:S(2)}) copy-start(bf16[640,640]{1,0:T(8,128)(2,1)} %wq_ref.3) | copy-start | bytes 2457604
  5.8 5.8 %copy-start.4 = (f32[640]{0:T(1024)S(1)}, f32[640]{0:T(1024)}, u32[]{:S(2)}) copy-start(f32[640]{0:T(1024)} %bias_ref.1) | copy-start | bytes 7684
  5.8 5.8 %copy-start.5 = (f32[640]{0:T(1024)S(1)}, f32[640]{0:T(1024)}, u32[]{:S(2)}) copy-start(f32[640]{0:T(1024)} %tgain_ref.3) | copy-start | bytes 7684
  5.8 5.7 %collective-permute-start = (bf16[4,16,1280]{2,1,0:T(8,128)(2,1)S(1)}, bf16[4,16,1280]{2,1,0:T(8,128)(2,1)S(1)}, u32[]{:S(2)}, u32[]{:S(2)}) collective-permute-start(bf16[4,16,1280]{2,1,0:T(8,128)(2,1)S(1)} %get-tuple-element.18.edge_act_ref), channel_id=1, source_target_pairs={{0,8},{8,0},{16,24},{24,16},{1,9},{9,1},{17,25},{25,17},{2,10},{10... | collective-permute-start | bytes 491528 | tf_op jit(solution)/shard_map/ppermute | solution.py:288
  7.9 8.6 %collective-permute-start.1 = (bf16[4,16,1280]{2,1,0:T(8,128)(2,1)S(1)}, bf16[4,16,1280]{2,1,0:T(8,128)(2,1)S(1)}, u32[]{:S(2)}, u32[]{:S(2)}) collective-permute-start(bf16[4,16,1280]{2,1,0:T(8,128)(2,1)S(1)} %get-tuple-element.24), channel_id=1, source_target_pairs={{8,16},{16,8},{9,17},{17,9},{10,18},{18,10},{11,19},{19,11},{12,20... | collective-permute-start | bytes 491528 | tf_op jit(solution)/shard_map/ppermute | solution.py:298
  11.6 5.0 %copy-start.6 = (bf16[640,640]{1,0:T(8,128)(2,1)S(1)}, bf16[640,640]{1,0:T(8,128)(2,1)}, u32[]{:S(2)}) copy-start(bf16[640,640]{1,0:T(8,128)(2,1)} %wk_ref.1) | copy-start | bytes 2457604
  11.6 5.0 %copy-start.7 = (bf16[640,640]{1,0:T(8,128)(2,1)S(1)}, bf16[640,640]{1,0:T(8,128)(2,1)}, u32[]{:S(2)}) copy-start(bf16[640,640]{1,0:T(8,128)(2,1)} %wv_ref.1) | copy-start | bytes 2457604
  11.6 5.0 %copy-start.8 = (bf16[640,640]{1,0:T(8,128)(2,1)S(1)}, bf16[640,640]{1,0:T(8,128)(2,1)}, u32[]{:S(2)}) copy-start(bf16[640,640]{1,0:T(8,128)(2,1)} %wo_ref.1) | copy-start | bytes 2457604
  11.6 5.0 %copy-start.9 = (bf16[640,640]{1,0:T(8,128)(2,1)S(1)}, bf16[640,640]{1,0:T(8,128)(2,1)}, u32[]{:S(2)}) copy-start(bf16[640,640]{1,0:T(8,128)(2,1)} %xq_ref.1) | copy-start | bytes 2457604
  11.6 5.0 %copy-start.12 = (f32[640]{0:T(1024)S(1)}, f32[640]{0:T(1024)}, u32[]{:S(2)}) copy-start(f32[640]{0:T(1024)} %xgain_ref.1) | copy-start | bytes 7684
  11.6 5.0 %copy-start.13 = (s32[16]{0:T(128)S(1)}, s32[16]{0:T(128)}, u32[]{:S(2)}) copy-start(s32[16]{0:T(128)} %slot_ref.1) | copy-start | bytes 196
  11.6 5.0 %copy-start.14 = (s32[2]{0:T(128)S(1)}, s32[2]{0:T(128)}, u32[]{:S(2)}) copy-start(s32[2]{0:T(128)} %gate_ref.1) | copy-start | bytes 28
  15.1 6.0 %collective-permute-start.3 = (bf16[77,2,640]{2,0,1:T(8,128)(2,1)S(1)}, bf16[77,2,640]{2,0,1:T(8,128)(2,1)S(1)}, u32[]{:S(2)}, u32[]{:S(2)}) collective-permute-start(bf16[77,2,640]{2,0,1:T(8,128)(2,1)S(1)} %collective-permute-done.2), channel_id=1, source_target_pairs={{0,8},{8,0},{16,24},{24,16},{1,9},{9,1},{17,25},{25,17},{2,10},{10... | collective-permute-start | bytes 591368 | tf_op jit(solution)/shard_map/ppermute | solution.py:274
  16.6 4.5 %copy-start = (bf16[640,640]{1,0:T(8,128)(2,1)S(1)}, bf16[640,640]{1,0:T(8,128)(2,1)}, u32[]{:S(2)}) copy-start(bf16[640,640]{1,0:T(8,128)(2,1)} %xo_ref.1) | copy-start | bytes 2457604

commit v10 on v9

--- a/solution.py
+++ b/solution.py
@@ -3,6 +3,7 @@
 import jax.numpy as jnp
 from jax import lax
 from jax.experimental import pallas as pl
+from jax.experimental.layout import Layout, with_layout_constraint
 from jax.experimental.pallas import tpu as pltpu
 from jax.sharding import PartitionSpec as P
 
@@ -79,9 +80,7 @@
         edge_ref[s] = act_ref[s, other]
 
 
-def conv_kernel(
-    x_ref, act_ref, near_ref, w_ref, bias_ref, tgain_ref, wq_ref, out_ref, normed_ref, tq_ref, ext
-):
+def conv_kernel(x_ref, act_ref, near_ref, w_ref, bias_ref, out_ref, ext):
     slots, rows, _, wide = x_ref.shape
     width = wide // 2
     side = 2 * first_row()
@@ -101,13 +100,6 @@
             x_ref[:, :, :, ls].astype(F32) + bias_ref[...].reshape(1, 1, 1, width) + mid[:, ls].reshape(slots, rows, PAD, width)
         )
         out_ref[c, :, inner_rows] += rest[:, ls].reshape(slots, rows - 1, PAD, width)
-    normalize(out_ref, tgain_ref, wq_ref, normed_ref, tq_ref, pl.ds(side // 2, rows - 1))
-
-
-def normalize(field_ref, gain_ref, wq_ref, normed_ref, tq_ref, place):
-    field = rms(field_ref[:, :, place], gain_ref[...]).astype(BF16)
-    normed_ref[:, :, place] = field
-    tq_ref[:, :, place] = dot(field.reshape(-1, field.shape[-1]), wq_ref[...]).astype(BF16).reshape(field.shape)
 
 
 def pair_taps(w_ref, dr):
@@ -122,8 +114,8 @@
 
 
 def time_kernel(
-    frames, slot_ref, gate_ref, part_ref, normed, tq, next_ref, w_ref, tgain_ref, wq_ref, wk_ref, wv_ref, wo_ref,
-    xgain_ref, xq_ref, after_ref, _normed, _tq, query_ref, choice_ref, live_ref, tk, tv, mixed, scores, chances,
+    frames, slot_ref, gate_ref, part_ref, next_ref, w_ref, tgain_ref, wq_ref, wk_ref, wv_ref, wo_ref,
+    xgain_ref, xq_ref, after_ref, query_ref, choice_ref, live_ref, normed, tq, tk, tv, mixed, scores, chances,
     slot, gate, sems
 ):
     loads = [
@@ -145,10 +137,10 @@
         for c in range(2):
             part_ref[c, :, side * (rows - 1)] += add[:, c * width : (c + 1) * width].reshape(slots, PAD, width)
 
-    normalize(part_ref, tgain_ref, wq_ref, normed, tq, pl.ds(side * (rows - 1), 1))
-    both = dot(normed[...].reshape(total, width), jnp.concatenate([wk_ref[...], wv_ref[...]], axis=1))
-    tk[...] = both[:, :width].astype(BF16)
-    tv[...] = both[:, width:].astype(BF16)
+    normed[...] = rms(part_ref[...].reshape(total, width), tgain_ref[...]).astype(BF16)
+    every = dot(normed[...], jnp.concatenate([wq_ref[...], wk_ref[...], wv_ref[...]], axis=1))
+    for i, field in enumerate((tq, tk, tv)):
+        field[...] = every[:, i * width : (i + 1) * width].astype(BF16)
     group = rows * PAD
     pair = 2 * HEAD_DIM
     row = lax.broadcasted_iota(jnp.int32, (group, 2 * group), 0)
@@ -162,8 +154,7 @@
         for j in range(width // pair)
     ]
     for g, rs, ls in tiles:
-        query = tq[g // slots, g % slots, :, :, ls].reshape(group, pair)
-        scores[rs, ls] = dot_t(query, apart(tk[rs, ls]))
+        scores[rs, ls] = dot_t(tq[rs, ls], apart(tk[rs, ls]))
     for _, rs, ls in tiles:
         s = scores[rs, ls] + mask
         top = jnp.where(
@@ -270,8 +261,9 @@
         cost_estimate=cost(COSTP),
         name="pages",
     )(stored)
-    fetched = lax.ppermute(half, "req", partner_pairs)
-    swapped = lax.ppermute(fetched, "strip", near_pairs)
+    keep = Layout(major_to_minor=(0, 1, 2))
+    fetched = with_layout_constraint(lax.ppermute(half, "req", partner_pairs), keep)
+    swapped = with_layout_constraint(lax.ppermute(fetched, "strip", near_pairs), keep)
     fetched = fetched.transpose(1, 0, 2)
     swapped = swapped.transpose(1, 0, 2)
     row = jax.ShapeDtypeStruct((slots, PAD, wide), BF16)
@@ -297,37 +289,35 @@
     )(raw, conv_gain, edge_x, edge_act)
     other = lax.ppermute(edge, "strip", next_pairs)
     grid = (cols, slots, rows, PAD, width)
-    part, normed, queries = pl.pallas_call(
+    part = pl.pallas_call(
         conv_kernel,
-        out_shape=(jax.ShapeDtypeStruct(grid, F32), jax.ShapeDtypeStruct(grid, BF16), jax.ShapeDtypeStruct(grid, BF16)),
-        in_specs=[vm] * 7,
-        out_specs=(vm,) * 3,
+        out_shape=jax.ShapeDtypeStruct(grid, F32),
+        in_specs=[vm] * 5,
+        out_specs=vm,
         scratch_shapes=[pltpu.VMEM((slots, rows + 2, PAD, wide), BF16)],
         compiler_params=pltpu.CompilerParams(vmem_limit_bytes=16 << 20),
         cost_estimate=cost(COST1),
         name="conv_own",
-    )(x, act, near, conv_weight, conv_bias, temporal_gain, temporal_query)
-    after, _, _, query, choice, live = pl.pallas_call(
+    )(x, act, near, conv_weight, conv_bias)
+    after, query, choice, live = pl.pallas_call(
         functools.partial(time_kernel, frames),
         out_shape=(
             jax.ShapeDtypeStruct(grid, F32),
-            jax.ShapeDtypeStruct(grid, BF16),
-            jax.ShapeDtypeStruct(grid, BF16),
             jax.ShapeDtypeStruct((cols, REQ_DEV, rows, PAD, width), BF16),
             jax.ShapeDtypeStruct((REQ_DEV, 2 * REQ_DEV, PAD, width), BF16),
             jax.ShapeDtypeStruct((REQ_DEV, PAD, width), F32),
         ),
-        in_specs=[any_] * 2 + [vm] * 12,
-        out_specs=(vm,) * 6,
-        scratch_shapes=[pltpu.VMEM((total, width), BF16)] * 3
+        in_specs=[any_] * 2 + [vm] * 10,
+        out_specs=(vm,) * 4,
+        scratch_shapes=[pltpu.VMEM((total, width), BF16)] * 5
         + [pltpu.VMEM((total, width // HEAD_DIM * rows * PAD), kind) for kind in (F32, BF16)]
         + [pltpu.SMEM(context_slot.shape, jnp.int32), pltpu.SMEM(gate.shape, jnp.int32), pltpu.SemaphoreType.DMA((2,))],
-        input_output_aliases={2: 0, 3: 1, 4: 2},
+        input_output_aliases={2: 0},
         compiler_params=pltpu.CompilerParams(vmem_limit_bytes=16 << 20),
         cost_estimate=cost(COST2),
         name="time_mix",
     )(
-        context_slot, gate, part, normed, queries, other, conv_weight, temporal_gain, temporal_query, temporal_key, temporal_value,
+        context_slot, gate, part, other, conv_weight, temporal_gain, temporal_query, temporal_key, temporal_value,
         temporal_out, cross_gain, cross_query,
     )
     out = pl.pallas_call(

time: 23.4 us -> 23 us (0.983)
  waiting for transfers between devices: 3.39 us -> 3 us
    pallas_call x1, Pallas kernels: 3.43 us -> 2.72 us  [on_device(): pl.pallas_call(conv_kernel, out_shape=jax.ShapeDtypeStruct(grid, F32), in...]
    pallas_call x1, Pallas kernels: 3.94 us -> 4.51 us  [on_device(): pl.pallas_call(functools.partial(time_kernel, frames), out_shape=(jax.Sha...]
    ppermute x2, waiting for transfers between devices: 0.54 us -> 0.16 us  [the longest x1 0.15 us: on_device(): lax.ppermute(half, 'req', partner_pairs)]
where the time goes in v10:
time: 23 us; the launch traced here: 22.8 us
  Pallas kernels  10.5 us (46%)
  starting transfers between devices  7.87 us (34%)
  waiting for transfers between devices  3 us (13%)
  local copies, waits for them, and re-layouts  1.18 us (5%)
  between operations  0.27 us (1%)
    pallas_call x1, Pallas kernels, on_device(): pl.pallas_call(functools.partial(time_kernel, frames), out_shape=(jax.Sha...  4.51 us
    ppermute x1, starting transfers between devices, on_device(): lax.ppermute(half, 'req', partner_pairs)  4.1 us
    ppermute x1, waiting for transfers between devices, on_device(): near = lax.ppermute(edge_act, 'strip', near_pairs)  2.84 us
    pallas_call x1, Pallas kernels, on_device(): pl.pallas_call(conv_kernel, out_shape=jax.ShapeDtypeStruct(grid, F32), in...  2.72 us
    pallas_call x1, Pallas kernels, on_device(): pl.pallas_call(functools.partial(cross_kernel, frames), out_shape=jax.Sha...  2.11 us
    ppermute x1, starting transfers between devices, on_device(): near = lax.ppermute(edge_act, 'strip', near_pairs)  1.56 us
    ppermute x1, starting transfers between devices, on_device(): lax.ppermute(fetched, 'strip', near_pairs)  1.54 us
    unnamed x35, local copies, waits for them, and re-layouts  1.13 us
  transfers between devices with their start and end apart: 4, of which 2 were waited for; matrix products, arithmetic and copies ran while one was open for 0% of the time, Pallas kernels for 36%

profile of v10, /device:TPU:0, one launch (start us, length us, event | category | flops | bytes accessed | tf_op | source)
XLA Modules:
  0.0 22.8 jit_solution(13734123990824937999)
XLA Ops:
  0.0 1.0 %copy-done.1 = bf16[2,2,77,640]{3,1,2,0:T(2,128)(2,1)S(1)} copy-done((bf16[2,2,77,640]{3,1,2,0:T(2,128)(2,1)S(1)}, bf16[2,2,77,640]{3,1,2,0:T(2,128)(2,1)}, u32[]{:S(2)}) %copy-start.1) | copy-done | bytes 394264
  1.0 0.2 %pages.1 = bf16[77,2,640]{2,1,0:T(2,128)(2,1)S(1)} custom-call(bf16[2,77,2,640]{3,2,1,0:T(2,128)(2,1)S(1)} %bitcast.15), custom_call_target="tpu_custom_call" | custom-call | flops 3000000000 | tf_op jit(solution)/shard_map/pages/pallas_call | solution.py:254
  1.3 4.1 %collective-permute-start.2 = (bf16[77,2,640]{2,1,0:T(2,128)(2,1)S(1)}, bf16[77,2,640]{2,1,0:T(2,128)(2,1)S(1)}, u32[]{:S(2)}, u32[]{:S(2)}) collective-permute-start(bf16[77,2,640]{2,1,0:T(2,128)(2,1)S(1)} %pages.1), channel_id=1, source_target_pairs={{0,4},{1,5},{2,6},{3,7},{4,0},{5,1},{6,2},{7,3},{8,12},{9,13},{10,... | collective-permute-start | bytes 591368 | tf_op jit(solution)/shard_map/ppermute | solution.py:265
  5.4 0.3 %edge.1 = (bf16[4,16,1280]{2,1,0:T(8,128)(2,1)S(1)}, bf16[4,16,1280]{2,1,0:T(8,128)(2,1)S(1)}) custom-call(bf16[4,4,14,2,640]{4,3,2,1,0:T(2,128)(2,1)S(1)} %bitcast.16, f32[640]{0:T(1024)S(1)} %copy-done.10), custom_call_target="tpu_custom_call" | custom-call | flops 16000000000 | tf_op jit(solution)/shard_map/edge/pallas_call | solution.py:271
  5.7 0.0 copy-start.2
  5.7 0.0 copy-start.3
  5.7 1.6 %collective-permute-start = (bf16[4,16,1280]{2,1,0:T(8,128)(2,1)S(1)}, bf16[4,16,1280]{2,1,0:T(8,128)(2,1)S(1)}, u32[]{:S(2)}, u32[]{:S(2)}) collective-permute-start(bf16[4,16,1280]{2,1,0:T(8,128)(2,1)S(1)} %get-tuple-element.15.edge_act_ref), channel_id=1, source_target_pairs={{0,8},{8,0},{16,24},{24,16},{1,9},{9,1},{17,25},{25,17},{2,10},{10... | collective-permute-start | bytes 491528 | tf_op jit(solution)/shard_map/ppermute | solution.py:280
  7.3 0.6 %activate.1 = (bf16[4,4,16,1280]{3,2,1,0:T(8,128)(2,1)S(1)}, bf16[4,4,16,1280]{3,2,1,0:T(8,128)(2,1)S(1)}, bf16[4,16,1280]{2,1,0:T(8,128)(2,1)S(1)}) custom-call(bf16[4,4,14,2,640]{4,3,2,1,0:T(2,128)(2,1)S(1)} %bitcast.17, f32[640]{0:T(1024)S(1)} %copy-done.10, bf16[4,16,1280]{2,1,0:T(8,128)(2,1)S(1)} %get-tuple-element.14.edge_x_ref, ...), custom_call_target="tpu_custom_call" | custom-call | flops 300000000 | tf_op jit(solution)/shard_map/activate/pallas_call | solution.py:281
  7.9 0.7 %collective-permute-start.1 = (bf16[4,16,1280]{2,1,0:T(8,128)(2,1)S(1)}, bf16[4,16,1280]{2,1,0:T(8,128)(2,1)S(1)}, u32[]{:S(2)}, u32[]{:S(2)}) collective-permute-start(bf16[4,16,1280]{2,1,0:T(8,128)(2,1)S(1)} %get-tuple-element.18), channel_id=1, source_target_pairs={{8,16},{16,8},{9,17},{17,9},{10,18},{18,10},{11,19},{19,11},{12,20... | collective-permute-start | bytes 491528 | tf_op jit(solution)/shard_map/ppermute | solution.py:290
  8.6 2.8 %collective-permute-done.near_ref = bf16[4,16,1280]{2,1,0:T(8,128)(2,1)S(1)} collective-permute-done((bf16[4,16,1280]{2,1,0:T(8,128)(2,1)S(1)}, bf16[4,16,1280]{2,1,0:T(8,128)(2,1)S(1)}, u32[]{:S(2)}, u32[]{:S(2)}) %collective-permute-start) | collective-permute-done | bytes 163872 | tf_op jit(solution)/shard_map/ppermute | solution.py:280
  11.5 0.0 copy-start.4
  11.5 0.0 copy-start.5
  11.5 0.0 copy-start.6
  11.5 0.0 copy-start.7
  11.5 0.0 copy-start.8
  11.6 0.0 copy-start.11
  11.6 0.0 copy-start.12
  11.6 0.0 copy-start.13
  11.6 2.7 %conv_own.1.part_ref = f32[2,4,4,16,640]{4,3,2,1,0:T(8,128)S(1)} custom-call(bf16[4,4,16,1280]{3,2,1,0:T(8,128)(2,1)S(1)} %get-tuple-element.16.x_ref, bf16[4,4,16,1280]{3,2,1,0:T(8,128)(2,1)S(1)} %get-tuple-element.17.act_ref, bf16[4,16,1280]{2,1,0:T(8,128)(2,1)S(1)} %collective-permute-done.near_ref, bf16[3,3,640,640]{3,2,1,0:T(8,128)(2,1)S(1)} %bitcast.12, ...), custom_call_target="tpu_custom_call" | custom-call | flops 300000000 | tf_op jit(solution)/shard_map/conv_own/pallas_call | solution.py:292
  14.3 0.0 copy-start
  14.3 0.2 collective-permute-done.2
  14.5 1.5 %collective-permute-start.3 = (bf16[77,2,640]{2,1,0:T(2,128)(2,1)S(1)}, bf16[77,2,640]{2,1,0:T(2,128)(2,1)S(1)}, u32[]{:S(2)}, u32[]{:S(2)}) collective-permute-start(bf16[77,2,640]{2,1,0:T(2,128)(2,1)S(1)} %collective-permute-done.2), channel_id=1, source_target_pairs={{0,8},{8,0},{16,24},{24,16},{1,9},{9,1},{17,25},{25,17},{2,10},{10... | collective-permute-start | bytes 591368 | tf_op jit(solution)/shard_map/ppermute | solution.py:266
  16.1 4.5 %time_mix.1 = (f32[2,4,4,16,640]{4,3,2,1,0:T(8,128)S(1)}, bf16[2,2,4,16,640]{4,3,2,1,0:T(8,128)(2,1)S(1)}, bf16[2,4,16,640]{3,2,1,0:T(8,128)(2,1)S(1)}, f32[2,16,640]{2,1,0:T(8,128)S(1)}) custom-call(s32[16]{0:T(128)S(1)} %copy-done.13, s32[2]{0:T(128)S(1)} %copy-done.14, ...), custom_call_target="tpu_custom_call", output_to_operand_aliasing={{0}: (2, {})} | custom-call | flops 6000000000 | tf_op jit(solution)/shard_map/time_mix/pallas_call | solution.py:302
  20.7 2.1 %cross_mix.1 = bf16[2,4,14,2,640]{4,3,2,1,0:T(2,128)(2,1)} custom-call(bf16[2,4,16,640]{3,2,1,0:T(8,128)(2,1)S(1)} %get-tuple-element.19.choice_ref, f32[2,16,640]{2,1,0:T(8,128)S(1)} %get-tuple-element.20.live_ref, f32[2,4,4,16,640]{4,3,2,1,0:T(8,128)S(1)} %get-tuple-element.21.after_ref, bf16[2,2,4,16,640]{4,3,2,1,0:T(8,128)(2,1)S(1)} %get-tuple-element.22.query_ref, ...), custom_call_target="tpu_custom_call" | custom-call | flops 1000000000 | tf_op jit(solution)/shard_map/cross_mix/pallas_call | solution.py:323
  (28 shorter events, 0.1 us)
Async XLA Ops:
  0.0 1.0 %copy-start.1 = (bf16[2,2,77,640]{3,1,2,0:T(2,128)(2,1)S(1)}, bf16[2,2,77,640]{3,1,2,0:T(2,128)(2,1)}, u32[]{:S(2)}) copy-start(bf16[2,2,77,640]{3,1,2,0:T(2,128)(2,1)} %param.18) | copy-start | bytes 1182724
  1.0 4.4 %copy-start.9 = (bf16[2,2,4,2,14,640]{5,3,4,2,1,0:T(2,128)(2,1)S(1)}, bf16[2,2,4,2,14,640]{5,3,4,2,1,0:T(2,128)(2,1)}, u32[]{:S(2)}) copy-start(bf16[2,2,4,2,14,640]{5,3,4,2,1,0:T(2,128)(2,1)} %param.15) | copy-start | bytes 1720324
  1.0 4.4 %copy-start.10 = (f32[640]{0:T(1024)S(1)}, f32[640]{0:T(1024)}, u32[]{:S(2)}) copy-start(f32[640]{0:T(1024)} %gain_ref.3) | copy-start | bytes 7684
  1.3 13.2 %collective-permute-start.2 = (bf16[77,2,640]{2,1,0:T(2,128)(2,1)S(1)}, bf16[77,2,640]{2,1,0:T(2,128)(2,1)S(1)}, u32[]{:S(2)}, u32[]{:S(2)}) collective-permute-start(bf16[77,2,640]{2,1,0:T(2,128)(2,1)S(1)} %pages.1), channel_id=1, source_target_pairs={{0,4},{1,5},{2,6},{3,7},{4,0},{5,1},{6,2},{7,3},{8,12},{9,13},{10,... | collective-permute-start | bytes 591368 | tf_op jit(solution)/shard_map/ppermute | solution.py:265
  5.4 6.1 %slice-start = ((s8[7372800]{0:T(1024)(128)(4,1)}), s8[4194304]{0:T(1024)(128)(4,1)S(1)}, s32[]{:S(2)}) async-start(s8[7372800]{0:T(1024)(128)(4,1)} %bitcast.11), calls=%async_computation | async-start | bytes 8388608
  5.4 6.1 %slice-start.1 = ((s8[7372800]{0:T(1024)(128)(4,1)}), s8[3178496]{0:T(1024)(128)(4,1)S(1)}, s32[]{:S(2)}) async-start(s8[7372800]{0:T(1024)(128)(4,1)} %bitcast.11), calls=%async_computation.1 | async-start | bytes 6356992
  5.7 2.8 %copy-start.2 = (bf16[2,2,77,640]{3,1,2,0:T(2,128)(2,1)S(1)}, bf16[2,2,77,640]{3,1,2,0:T(2,128)(2,1)}, u32[]{:S(2)}) copy-start(bf16[2,2,77,640]{3,1,2,0:T(2,128)(2,1)} %param.18) | copy-start | bytes 1182724
  5.7 5.7 %copy-start.3 = (f32[640]{0:T(1024)S(1)}, f32[640]{0:T(1024)}, u32[]{:S(2)}) copy-start(f32[640]{0:T(1024)} %bias_ref.1) | copy-start | bytes 7684
  5.7 5.7 %collective-permute-start = (bf16[4,16,1280]{2,1,0:T(8,128)(2,1)S(1)}, bf16[4,16,1280]{2,1,0:T(8,128)(2,1)S(1)}, u32[]{:S(2)}, u32[]{:S(2)}) collective-permute-start(bf16[4,16,1280]{2,1,0:T(8,128)(2,1)S(1)} %get-tuple-element.15.edge_act_ref), channel_id=1, source_target_pairs={{0,8},{8,0},{16,24},{24,16},{1,9},{9,1},{17,25},{25,17},{2,10},{10... | collective-permute-start | bytes 491528 | tf_op jit(solution)/shard_map/ppermute | solution.py:280
  7.9 8.2 %collective-permute-start.1 = (bf16[4,16,1280]{2,1,0:T(8,128)(2,1)S(1)}, bf16[4,16,1280]{2,1,0:T(8,128)(2,1)S(1)}, u32[]{:S(2)}, u32[]{:S(2)}) collective-permute-start(bf16[4,16,1280]{2,1,0:T(8,128)(2,1)S(1)} %get-tuple-element.18), channel_id=1, source_target_pairs={{8,16},{16,8},{9,17},{17,9},{10,18},{18,10},{11,19},{19,11},{12,20... | collective-permute-start | bytes 491528 | tf_op jit(solution)/shard_map/ppermute | solution.py:290
  11.5 4.5 %copy-start.4 = (bf16[640,640]{1,0:T(8,128)(2,1)S(1)}, bf16[640,640]{1,0:T(8,128)(2,1)}, u32[]{:S(2)}) copy-start(bf16[640,640]{1,0:T(8,128)(2,1)} %wq_ref.1) | copy-start | bytes 2457604
  11.5 4.5 %copy-start.5 = (bf16[640,640]{1,0:T(8,128)(2,1)S(1)}, bf16[640,640]{1,0:T(8,128)(2,1)}, u32[]{:S(2)}) copy-start(bf16[640,640]{1,0:T(8,128)(2,1)} %wk_ref.1) | copy-start | bytes 2457604
  11.5 4.5 %copy-start.6 = (bf16[640,640]{1,0:T(8,128)(2,1)S(1)}, bf16[640,640]{1,0:T(8,128)(2,1)}, u32[]{:S(2)}) copy-start(bf16[640,640]{1,0:T(8,128)(2,1)} %wv_ref.1) | copy-start | bytes 2457604
  11.5 4.5 %copy-start.7 = (bf16[640,640]{1,0:T(8,128)(2,1)S(1)}, bf16[640,640]{1,0:T(8,128)(2,1)}, u32[]{:S(2)}) copy-start(bf16[640,640]{1,0:T(8,128)(2,1)} %wo_ref.1) | copy-start | bytes 2457604
  11.5 4.5 %copy-start.8 = (bf16[640,640]{1,0:T(8,128)(2,1)S(1)}, bf16[640,640]{1,0:T(8,128)(2,1)}, u32[]{:S(2)}) copy-start(bf16[640,640]{1,0:T(8,128)(2,1)} %xq_ref.1) | copy-start | bytes 2457604
  11.6 4.5 %copy-start.11 = (f32[640]{0:T(1024)S(1)}, f32[640]{0:T(1024)}, u32[]{:S(2)}) copy-start(f32[640]{0:T(1024)} %tgain_ref.1) | copy-start | bytes 7684
  11.6 4.5 %copy-start.12 = (f32[640]{0:T(1024)S(1)}, f32[640]{0:T(1024)}, u32[]{:S(2)}) copy-start(f32[640]{0:T(1024)} %xgain_ref.1) | copy-start | bytes 7684
  11.6 4.5 %copy-start.13 = (s32[16]{0:T(128)S(1)}, s32[16]{0:T(128)}, u32[]{:S(2)}) copy-start(s32[16]{0:T(128)} %slot_ref.1) | copy-start | bytes 196
  11.6 4.5 %copy-start.14 = (s32[2]{0:T(128)S(1)}, s32[2]{0:T(128)}, u32[]{:S(2)}) copy-start(s32[2]{0:T(128)} %gate_ref.1) | copy-start | bytes 28
  14.3 6.4 %copy-start = (bf16[640,640]{1,0:T(8,128)(2,1)S(1)}, bf16[640,640]{1,0:T(8,128)(2,1)}, u32[]{:S(2)}) copy-start(bf16[640,640]{1,0:T(8,128)(2,1)} %xo_ref.1) | copy-start | bytes 2457604
  14.5 6.2 %collective-permute-start.3 = (bf16[77,2,640]{2,1,0:T(2,128)(2,1)S(1)}, bf16[77,2,640]{2,1,0:T(2,128)(2,1)S(1)}, u32[]{:S(2)}, u32[]{:S(2)}) collective-permute-start(bf16[77,2,640]{2,1,0:T(2,128)(2,1)S(1)} %collective-permute-done.2), channel_id=1, source_target_pairs={{0,8},{8,0},{16,24},{24,16},{1,9},{9,1},{17,25},{25,17},{2,10},{10... | collective-permute-start | bytes 591368 | tf_op jit(solution)/shard_map/ppermute | solution.py:266

commit v11 on v10

--- a/solution.py
+++ b/solution.py
@@ -38,10 +38,8 @@
     return lax.dot_general(a, b, (((1,), (1,)), ((), ())), preferred_element_type=F32)
 
 
-def pages_kernel(pages_ref, half_ref, sem):
-    copy = pltpu.make_async_copy(pages_ref.at[1 - first_row()], half_ref, sem)
-    copy.start()
-    copy.wait()
+def pages_kernel(pages_ref, half_ref):
+    half_ref[...] = pages_ref[1 - first_row()]
 
 
 def first_row():
@@ -219,14 +217,14 @@
     add = dot(mixed[...].reshape(-1, width), xo_ref[...]).reshape(cols, half, rows, PAD, width)
     copies = []
     for r in range(half):
-        for c in range(cols):
-            cond = (after_ref[c, r] + add[c, r]).astype(BF16).astype(F32)
-            uncond = after_ref[c, half + r].astype(BF16).astype(F32)
-            guided = jnp.where(live_ref[r] == 1.0, uncond + scale * (cond - uncond), cond)
-            for w in range(rows):
-                made[r, w, :, c, :] = guided[w, :frames].astype(BF16)
-        copies.append(pltpu.make_async_copy(made.at[r], out_ref.at[r], sems.at[r]))
-        copies[r].start()
+        for w in range(rows):
+            for c in range(cols):
+                cond = (after_ref[c, r, w] + add[c, r, w]).astype(BF16).astype(F32)
+                uncond = after_ref[c, half + r, w].astype(BF16).astype(F32)
+                guided = jnp.where(live_ref[r] == 1.0, uncond + scale * (cond - uncond), cond)
+                made[r, w, :, c, :] = guided[:frames].astype(BF16)
+            copies.append(pltpu.make_async_copy(made.at[r, w], out_ref.at[r, w], sems.at[r, w]))
+            copies[-1].start()
     for copy in copies:
         copy.wait()
 
@@ -254,9 +252,8 @@
     half = pl.pallas_call(
         pages_kernel,
         out_shape=jax.ShapeDtypeStruct(stored.shape[1:], BF16),
-        in_specs=[any_],
+        in_specs=[vm],
         out_specs=vm,
-        scratch_shapes=[pltpu.SemaphoreType.DMA],
         compiler_params=pltpu.CompilerParams(vmem_limit_bytes=8 << 20),
         cost_estimate=cost(COSTP),
         name="pages",
@@ -331,7 +328,7 @@
             pltpu.VMEM((REQ_DEV, cols * rows * PAD, width // HEAD_DIM * room), BF16),
             pltpu.VMEM((cols, REQ_DEV, rows, PAD, width), BF16),
             pltpu.VMEM((REQ_DEV, rows, frames, cols, width), BF16),
-            pltpu.SemaphoreType.DMA((REQ_DEV,)),
+            pltpu.SemaphoreType.DMA((REQ_DEV, rows)),
         ],
         compiler_params=pltpu.CompilerParams(vmem_limit_bytes=16 << 20),
         cost_estimate=cost(COST3),

time: 23 us -> 22.8 us (level)
  no operation moved by 1% of the time
where the time goes in v11:
time: 22.8 us; the launch traced here: 22.6 us
  Pallas kernels  10.3 us (45%)
  starting transfers between devices  7.87 us (35%)
  waiting for transfers between devices  3 us (13%)
  local copies, waits for them, and re-layouts  1.18 us (5%)
  between operations  0.27 us (1%)
    pallas_call x1, Pallas kernels, on_device(): pl.pallas_call(functools.partial(time_kernel, frames), out_shape=(jax.Sha...  4.5 us
    ppermute x1, starting transfers between devices, on_device(): lax.ppermute(half, 'req', partner_pairs)  4.1 us
    ppermute x1, waiting for transfers between devices, on_device(): near = lax.ppermute(edge_act, 'strip', near_pairs)  2.84 us
    pallas_call x1, Pallas kernels, on_device(): pl.pallas_call(conv_kernel, out_shape=jax.ShapeDtypeStruct(grid, F32), in...  2.72 us
    pallas_call x1, Pallas kernels, on_device(): pl.pallas_call(functools.partial(cross_kernel, frames), out_shape=jax.Sha...  2.13 us
    ppermute x1, starting transfers between devices, on_device(): near = lax.ppermute(edge_act, 'strip', near_pairs)  1.56 us
    ppermute x1, starting transfers between devices, on_device(): lax.ppermute(fetched, 'strip', near_pairs)  1.54 us
    unnamed x35, local copies, waits for them, and re-layouts  1.13 us
  transfers between devices with their start and end apart: 4, of which 2 were waited for; matrix products, arithmetic and copies ran while one was open for 0% of the time, Pallas kernels for 36%

profile of v11, /device:TPU:0, one launch (start us, length us, event | category | flops | bytes accessed | tf_op | source)
XLA Modules:
  0.0 22.6 jit_solution(601286347803791938)
XLA Ops:
  0.0 1.0 %copy-done.1 = bf16[2,2,77,640]{3,1,2,0:T(2,128)(2,1)S(1)} copy-done((bf16[2,2,77,640]{3,1,2,0:T(2,128)(2,1)S(1)}, bf16[2,2,77,640]{3,1,2,0:T(2,128)(2,1)}, u32[]{:S(2)}) %copy-start.1) | copy-done | bytes 394264
  1.0 4.1 %collective-permute-start.2 = (bf16[77,2,640]{2,1,0:T(2,128)(2,1)S(1)}, bf16[77,2,640]{2,1,0:T(2,128)(2,1)S(1)}, u32[]{:S(2)}, u32[]{:S(2)}) collective-permute-start(bf16[77,2,640]{2,1,0:T(2,128)(2,1)S(1)} %pages.1), channel_id=1, source_target_pairs={{0,4},{1,5},{2,6},{3,7},{4,0},{5,1},{6,2},{7,3},{8,12},{9,13},{10,... | collective-permute-start | bytes 591368 | tf_op jit(solution)/shard_map/ppermute | solution.py:262
  5.1 0.3 %edge.1 = (bf16[4,16,1280]{2,1,0:T(8,128)(2,1)S(1)}, bf16[4,16,1280]{2,1,0:T(8,128)(2,1)S(1)}) custom-call(bf16[4,4,14,2,640]{4,3,2,1,0:T(2,128)(2,1)S(1)} %bitcast.16, f32[640]{0:T(1024)S(1)} %copy-done.10), custom_call_target="tpu_custom_call" | custom-call | flops 16000000000 | tf_op jit(solution)/shard_map/edge/pallas_call | solution.py:268
  5.5 0.0 copy-start.2
  5.5 0.0 copy-start.3
  5.5 1.6 %collective-permute-start = (bf16[4,16,1280]{2,1,0:T(8,128)(2,1)S(1)}, bf16[4,16,1280]{2,1,0:T(8,128)(2,1)S(1)}, u32[]{:S(2)}, u32[]{:S(2)}) collective-permute-start(bf16[4,16,1280]{2,1,0:T(8,128)(2,1)S(1)} %get-tuple-element.15.edge_act_ref), channel_id=1, source_target_pairs={{0,8},{8,0},{16,24},{24,16},{1,9},{9,1},{17,25},{25,17},{2,10},{10... | collective-permute-start | bytes 491528 | tf_op jit(solution)/shard_map/ppermute | solution.py:277
  7.1 0.6 %activate.1 = (bf16[4,4,16,1280]{3,2,1,0:T(8,128)(2,1)S(1)}, bf16[4,4,16,1280]{3,2,1,0:T(8,128)(2,1)S(1)}, bf16[4,16,1280]{2,1,0:T(8,128)(2,1)S(1)}) custom-call(bf16[4,4,14,2,640]{4,3,2,1,0:T(2,128)(2,1)S(1)} %bitcast.17, f32[640]{0:T(1024)S(1)} %copy-done.10, bf16[4,16,1280]{2,1,0:T(8,128)(2,1)S(1)} %get-tuple-element.14.edge_x_ref, ...), custom_call_target="tpu_custom_call" | custom-call | flops 300000000 | tf_op jit(solution)/shard_map/activate/pallas_call | solution.py:278
  7.7 0.7 %collective-permute-start.1 = (bf16[4,16,1280]{2,1,0:T(8,128)(2,1)S(1)}, bf16[4,16,1280]{2,1,0:T(8,128)(2,1)S(1)}, u32[]{:S(2)}, u32[]{:S(2)}) collective-permute-start(bf16[4,16,1280]{2,1,0:T(8,128)(2,1)S(1)} %get-tuple-element.18), channel_id=1, source_target_pairs={{8,16},{16,8},{9,17},{17,9},{10,18},{18,10},{11,19},{19,11},{12,20... | collective-permute-start | bytes 491528 | tf_op jit(solution)/shard_map/ppermute | solution.py:287
  8.4 2.8 %collective-permute-done.near_ref = bf16[4,16,1280]{2,1,0:T(8,128)(2,1)S(1)} collective-permute-done((bf16[4,16,1280]{2,1,0:T(8,128)(2,1)S(1)}, bf16[4,16,1280]{2,1,0:T(8,128)(2,1)S(1)}, u32[]{:S(2)}, u32[]{:S(2)}) %collective-permute-start) | collective-permute-done | bytes 163872 | tf_op jit(solution)/shard_map/ppermute | solution.py:277
  11.3 0.0 copy-start.4
  11.3 0.0 copy-start.5
  11.3 0.0 copy-start.6
  11.3 0.0 copy-start.7
  11.3 0.0 copy-start.8
  11.3 0.0 copy-start.11
  11.3 0.0 copy-start.12
  11.4 0.0 copy-start.13
  11.4 0.0 copy-start.14
  11.4 2.7 %conv_own.1.part_ref = f32[2,4,4,16,640]{4,3,2,1,0:T(8,128)S(1)} custom-call(bf16[4,4,16,1280]{3,2,1,0:T(8,128)(2,1)S(1)} %get-tuple-element.16.x_ref, bf16[4,4,16,1280]{3,2,1,0:T(8,128)(2,1)S(1)} %get-tuple-element.17.act_ref, bf16[4,16,1280]{2,1,0:T(8,128)(2,1)S(1)} %collective-permute-done.near_ref, bf16[3,3,640,640]{3,2,1,0:T(8,128)(2,1)S(1)} %bitcast.12, ...), custom_call_target="tpu_custom_call" | custom-call | flops 300000000 | tf_op jit(solution)/shard_map/conv_own/pallas_call | solution.py:289
  14.1 0.0 copy-start
  14.1 0.1 collective-permute-done.2
  14.3 1.5 %collective-permute-start.3 = (bf16[77,2,640]{2,1,0:T(2,128)(2,1)S(1)}, bf16[77,2,640]{2,1,0:T(2,128)(2,1)S(1)}, u32[]{:S(2)}, u32[]{:S(2)}) collective-permute-start(bf16[77,2,640]{2,1,0:T(2,128)(2,1)S(1)} %collective-permute-done.2), channel_id=1, source_target_pairs={{0,8},{8,0},{16,24},{24,16},{1,9},{9,1},{17,25},{25,17},{2,10},{10... | collective-permute-start | bytes 591368 | tf_op jit(solution)/shard_map/ppermute | solution.py:263
  15.9 4.5 %time_mix.1 = (f32[2,4,4,16,640]{4,3,2,1,0:T(8,128)S(1)}, bf16[2,2,4,16,640]{4,3,2,1,0:T(8,128)(2,1)S(1)}, bf16[2,4,16,640]{3,2,1,0:T(8,128)(2,1)S(1)}, f32[2,16,640]{2,1,0:T(8,128)S(1)}) custom-call(s32[16]{0:T(128)S(1)} %copy-done.13, s32[2]{0:T(128)S(1)} %copy-done.14, ...), custom_call_target="tpu_custom_call", output_to_operand_aliasing={{0}: (2, {})} | custom-call | flops 6000000000 | tf_op jit(solution)/shard_map/time_mix/pallas_call | solution.py:299
  20.5 2.1 %cross_mix.1 = bf16[2,4,14,2,640]{4,3,2,1,0:T(2,128)(2,1)} custom-call(bf16[2,4,16,640]{3,2,1,0:T(8,128)(2,1)S(1)} %get-tuple-element.19.choice_ref, f32[2,16,640]{2,1,0:T(8,128)S(1)} %get-tuple-element.20.live_ref, f32[2,4,4,16,640]{4,3,2,1,0:T(8,128)S(1)} %get-tuple-element.21.after_ref, bf16[2,2,4,16,640]{4,3,2,1,0:T(8,128)(2,1)S(1)} %get-tuple-element.22.query_ref, ...), custom_call_target="tpu_custom_call" | custom-call | flops 1000000000 | tf_op jit(solution)/shard_map/cross_mix/pallas_call | solution.py:320
  (28 shorter events, 0.2 us)
Async XLA Ops:
  0.0 1.0 %copy-start.1 = (bf16[2,2,77,640]{3,1,2,0:T(2,128)(2,1)S(1)}, bf16[2,2,77,640]{3,1,2,0:T(2,128)(2,1)}, u32[]{:S(2)}) copy-start(bf16[2,2,77,640]{3,1,2,0:T(2,128)(2,1)} %param.18) | copy-start | bytes 1182724
  1.0 4.1 %copy-start.9 = (bf16[2,2,4,2,14,640]{5,3,4,2,1,0:T(2,128)(2,1)S(1)}, bf16[2,2,4,2,14,640]{5,3,4,2,1,0:T(2,128)(2,1)}, u32[]{:S(2)}) copy-start(bf16[2,2,4,2,14,640]{5,3,4,2,1,0:T(2,128)(2,1)} %param.15) | copy-start | bytes 1720324
  1.0 4.1 %copy-start.10 = (f32[640]{0:T(1024)S(1)}, f32[640]{0:T(1024)}, u32[]{:S(2)}) copy-start(f32[640]{0:T(1024)} %gain_ref.3) | copy-start | bytes 7684
  1.0 13.2 %collective-permute-start.2 = (bf16[77,2,640]{2,1,0:T(2,128)(2,1)S(1)}, bf16[77,2,640]{2,1,0:T(2,128)(2,1)S(1)}, u32[]{:S(2)}, u32[]{:S(2)}) collective-permute-start(bf16[77,2,640]{2,1,0:T(2,128)(2,1)S(1)} %pages.1), channel_id=1, source_target_pairs={{0,4},{1,5},{2,6},{3,7},{4,0},{5,1},{6,2},{7,3},{8,12},{9,13},{10,... | collective-permute-start | bytes 591368 | tf_op jit(solution)/shard_map/ppermute | solution.py:262
  5.1 6.1 %slice-start = ((s8[7372800]{0:T(1024)(128)(4,1)}), s8[4194304]{0:T(1024)(128)(4,1)S(1)}, s32[]{:S(2)}) async-start(s8[7372800]{0:T(1024)(128)(4,1)} %bitcast.11), calls=%async_computation | async-start | bytes 8388608
  5.1 6.1 %slice-start.1 = ((s8[7372800]{0:T(1024)(128)(4,1)}), s8[3178496]{0:T(1024)(128)(4,1)S(1)}, s32[]{:S(2)}) async-start(s8[7372800]{0:T(1024)(128)(4,1)} %bitcast.11), calls=%async_computation.1 | async-start | bytes 6356992
  5.5 2.8 %copy-start.2 = (bf16[2,2,77,640]{3,1,2,0:T(2,128)(2,1)S(1)}, bf16[2,2,77,640]{3,1,2,0:T(2,128)(2,1)}, u32[]{:S(2)}) copy-start(bf16[2,2,77,640]{3,1,2,0:T(2,128)(2,1)} %param.18) | copy-start | bytes 1182724
  5.5 5.7 %copy-start.3 = (f32[640]{0:T(1024)S(1)}, f32[640]{0:T(1024)}, u32[]{:S(2)}) copy-start(f32[640]{0:T(1024)} %bias_ref.1) | copy-start | bytes 7684
  5.5 5.7 %collective-permute-start = (bf16[4,16,1280]{2,1,0:T(8,128)(2,1)S(1)}, bf16[4,16,1280]{2,1,0:T(8,128)(2,1)S(1)}, u32[]{:S(2)}, u32[]{:S(2)}) collective-permute-start(bf16[4,16,1280]{2,1,0:T(8,128)(2,1)S(1)} %get-tuple-element.15.edge_act_ref), channel_id=1, source_target_pairs={{0,8},{8,0},{16,24},{24,16},{1,9},{9,1},{17,25},{25,17},{2,10},{10... | collective-permute-start | bytes 491528 | tf_op jit(solution)/shard_map/ppermute | solution.py:277
  7.7 8.2 %collective-permute-start.1 = (bf16[4,16,1280]{2,1,0:T(8,128)(2,1)S(1)}, bf16[4,16,1280]{2,1,0:T(8,128)(2,1)S(1)}, u32[]{:S(2)}, u32[]{:S(2)}) collective-permute-start(bf16[4,16,1280]{2,1,0:T(8,128)(2,1)S(1)} %get-tuple-element.18), channel_id=1, source_target_pairs={{8,16},{16,8},{9,17},{17,9},{10,18},{18,10},{11,19},{19,11},{12,20... | collective-permute-start | bytes 491528 | tf_op jit(solution)/shard_map/ppermute | solution.py:287
  11.3 4.5 %copy-start.4 = (bf16[640,640]{1,0:T(8,128)(2,1)S(1)}, bf16[640,640]{1,0:T(8,128)(2,1)}, u32[]{:S(2)}) copy-start(bf16[640,640]{1,0:T(8,128)(2,1)} %wq_ref.1) | copy-start | bytes 2457604
  11.3 4.5 %copy-start.5 = (bf16[640,640]{1,0:T(8,128)(2,1)S(1)}, bf16[640,640]{1,0:T(8,128)(2,1)}, u32[]{:S(2)}) copy-start(bf16[640,640]{1,0:T(8,128)(2,1)} %wk_ref.1) | copy-start | bytes 2457604
  11.3 4.5 %copy-start.6 = (bf16[640,640]{1,0:T(8,128)(2,1)S(1)}, bf16[640,640]{1,0:T(8,128)(2,1)}, u32[]{:S(2)}) copy-start(bf16[640,640]{1,0:T(8,128)(2,1)} %wv_ref.1) | copy-start | bytes 2457604
  11.3 4.5 %copy-start.7 = (bf16[640,640]{1,0:T(8,128)(2,1)S(1)}, bf16[640,640]{1,0:T(8,128)(2,1)}, u32[]{:S(2)}) copy-start(bf16[640,640]{1,0:T(8,128)(2,1)} %wo_ref.1) | copy-start | bytes 2457604
  11.3 4.5 %copy-start.8 = (bf16[640,640]{1,0:T(8,128)(2,1)S(1)}, bf16[640,640]{1,0:T(8,128)(2,1)}, u32[]{:S(2)}) copy-start(bf16[640,640]{1,0:T(8,128)(2,1)} %xq_ref.1) | copy-start | bytes 2457604
  11.3 4.5 %copy-start.11 = (f32[640]{0:T(1024)S(1)}, f32[640]{0:T(1024)}, u32[]{:S(2)}) copy-start(f32[640]{0:T(1024)} %tgain_ref.1) | copy-start | bytes 7684
  11.3 4.5 %copy-start.12 = (f32[640]{0:T(1024)S(1)}, f32[640]{0:T(1024)}, u32[]{:S(2)}) copy-start(f32[640]{0:T(1024)} %xgain_ref.1) | copy-start | bytes 7684
  11.4 4.5 %copy-start.13 = (s32[16]{0:T(128)S(1)}, s32[16]{0:T(128)}, u32[]{:S(2)}) copy-start(s32[16]{0:T(128)} %slot_ref.1) | copy-start | bytes 196
  11.4 4.5 %copy-start.14 = (s32[2]{0:T(128)S(1)}, s32[2]{0:T(128)}, u32[]{:S(2)}) copy-start(s32[2]{0:T(128)} %gate_ref.1) | copy-start | bytes 28
  14.1 6.4 %copy-start = (bf16[640,640]{1,0:T(8,128)(2,1)S(1)}, bf16[640,640]{1,0:T(8,128)(2,1)}, u32[]{:S(2)}) copy-start(bf16[640,640]{1,0:T(8,128)(2,1)} %xo_ref.1) | copy-start | bytes 2457604
  14.3 6.2 %collective-permute-start.3 = (bf16[77,2,640]{2,1,0:T(2,128)(2,1)S(1)}, bf16[77,2,640]{2,1,0:T(2,128)(2,1)S(1)}, u32[]{:S(2)}, u32[]{:S(2)}) collective-permute-start(bf16[77,2,640]{2,1,0:T(2,128)(2,1)S(1)} %collective-permute-done.2), channel_id=1, source_target_pairs={{0,8},{8,0},{16,24},{24,16},{1,9},{9,1},{17,25},{25,17},{2,10},{10... | collective-permute-start | bytes 591368 | tf_op jit(solution)/shard_map/ppermute | solution.py:263

commit v12 on v11

--- a/solution.py
+++ b/solution.py
@@ -113,7 +113,7 @@
 
 def time_kernel(
     frames, slot_ref, gate_ref, part_ref, next_ref, w_ref, tgain_ref, wq_ref, wk_ref, wv_ref, wo_ref,
-    xgain_ref, xq_ref, after_ref, query_ref, choice_ref, live_ref, normed, tq, tk, tv, mixed, scores, chances,
+    xgain_ref, xq_ref, _part, after_ref, query_ref, choice_ref, live_ref, normed, tq, tk, tv, mixed, scores, chances,
     slot, gate, sems
 ):
     loads = [
@@ -164,8 +164,9 @@
     for _, rs, ls in tiles:
         out = dot(chances[rs, ls], jnp.concatenate([apart(tv[rs, ls]), ones], axis=1))
         mixed[rs, ls] = (out[:, :pair] / out[:, pair:]).astype(BF16)
-    after_ref[...] = part_ref[...] + dot(mixed[...], wo_ref[...]).reshape(after_ref.shape)
-    nc = rms(after_ref[:, :half], xgain_ref[...]).astype(BF16).reshape(-1, width)
+    add = dot(mixed[...], wo_ref[...]).reshape(part_ref.shape)
+    cond = part_ref[:, :half] + add[:, :half]
+    nc = rms(cond, xgain_ref[...]).astype(BF16).reshape(-1, width)
     query_ref[...] = dot(nc, xq_ref[...]).astype(BF16).reshape(query_ref.shape)
     for load in loads:
         load.wait()
@@ -176,14 +177,18 @@
         place = i + jnp.where(page - i == first_page, 0, REQ_DEV)
         for j in range(2 * REQ_DEV):
             choice_ref[r, j] = jnp.full(choice_ref.shape[2:], jnp.where(place == j, 1.0, 0.0), F32).astype(BF16)
-        live_ref[r] = jnp.full(live_ref.shape[1:], jnp.where(gate[r] == 1, 1.0, 0.0), F32)
+        frame = lax.broadcasted_iota(jnp.int32, (PAD, width), 0).astype(F32)
+        guide = 1.0 + 2.0 * frame / (frames - 1)
+        live_ref[r] = jnp.where(gate[r] == 1, guide, 1.0)
+        for c in range(2):
+            uncond = part_ref[c, half + r] + add[c, half + r]
+            after_ref[c, r] = jnp.where(gate[r] == 1, uncond + guide * (cond[c, r] - uncond), cond[c, r])
 
 
 def cross_kernel(
     frames, choice_ref, live_ref, after_ref, query_ref, own_ref, fetched_ref, swapped_ref, xo_ref, out_ref, keys, values, scores, chances, mixed, made, sems
 ):
-    cols, slots, rows, _, width = after_ref.shape
-    half = slots // 2
+    cols, half, rows, _, width = after_ref.shape
     even = first_row() == 1
     tokens = own_ref.shape[2]
     room = -(-tokens // 128) * 128
@@ -212,16 +217,12 @@
     for r, ls, ks in tiles:
         out = dot(chances[r, :, ks], jnp.concatenate([apart(values[r, :, ls]), ones], axis=1))
         mixed[:, r, :, :, ls] = (out[:, :pair] / out[:, pair:]).astype(BF16).reshape(cols, rows, PAD, pair)
-    frame = lax.broadcasted_iota(jnp.int32, (PAD, width), 0).astype(F32)
-    scale = 1.0 + 2.0 * frame / (frames - 1)
     add = dot(mixed[...].reshape(-1, width), xo_ref[...]).reshape(cols, half, rows, PAD, width)
     copies = []
     for r in range(half):
         for w in range(rows):
             for c in range(cols):
-                cond = (after_ref[c, r, w] + add[c, r, w]).astype(BF16).astype(F32)
-                uncond = after_ref[c, half + r, w].astype(BF16).astype(F32)
-                guided = jnp.where(live_ref[r] == 1.0, uncond + scale * (cond - uncond), cond)
+                guided = after_ref[c, r, w] + live_ref[r] * add[c, r, w]
                 made[r, w, :, c, :] = guided[:frames].astype(BF16)
             copies.append(pltpu.make_async_copy(made.at[r, w], out_ref.at[r, w], sems.at[r, w]))
             copies[-1].start()
@@ -296,16 +297,17 @@
         cost_estimate=cost(COST1),
         name="conv_own",
     )(x, act, near, conv_weight, conv_bias)
-    after, query, choice, live = pl.pallas_call(
+    _, after, query, choice, live = pl.pallas_call(
         functools.partial(time_kernel, frames),
         out_shape=(
             jax.ShapeDtypeStruct(grid, F32),
+            jax.ShapeDtypeStruct((cols, REQ_DEV, rows, PAD, width), F32),
             jax.ShapeDtypeStruct((cols, REQ_DEV, rows, PAD, width), BF16),
             jax.ShapeDtypeStruct((REQ_DEV, 2 * REQ_DEV, PAD, width), BF16),
             jax.ShapeDtypeStruct((REQ_DEV, PAD, width), F32),
         ),
         in_specs=[any_] * 2 + [vm] * 10,
-        out_specs=(vm,) * 4,
+        out_specs=(vm,) * 5,
         scratch_shapes=[pltpu.VMEM((total, width), BF16)] * 5
         + [pltpu.VMEM((total, width // HEAD_DIM * rows * PAD), kind) for kind in (F32, BF16)]
         + [pltpu.SMEM(context_slot.shape, jnp.int32), pltpu.SMEM(gate.shape, jnp.int32), pltpu.SemaphoreType.DMA((2,))],

time: 22.8 us -> 22.7 us (level)
  no operation moved by 1% of the time
where the time goes in v12:
time: 22.7 us; the launch traced here: 22.5 us
  Pallas kernels  10.2 us (45%)
  starting transfers between devices  7.87 us (35%)
  waiting for transfers between devices  3.02 us (13%)
  local copies, waits for them, and re-layouts  1.18 us (5%)
  between operations  0.27 us (1%)
    pallas_call x1, Pallas kernels, on_device(): pl.pallas_call(functools.partial(time_kernel, frames), out_shape=(jax.Sha...  4.49 us
    ppermute x1, starting transfers between devices, on_device(): lax.ppermute(half, 'req', partner_pairs)  4.1 us
    ppermute x1, waiting for transfers between devices, on_device(): near = lax.ppermute(edge_act, 'strip', near_pairs)  2.85 us
    pallas_call x1, Pallas kernels, on_device(): pl.pallas_call(conv_kernel, out_shape=jax.ShapeDtypeStruct(grid, F32), in...  2.72 us
    pallas_call x1, Pallas kernels, on_device(): pl.pallas_call(functools.partial(cross_kernel, frames), out_shape=jax.Sha...  2.03 us
    ppermute x1, starting transfers between devices, on_device(): near = lax.ppermute(edge_act, 'strip', near_pairs)  1.56 us
    ppermute x1, starting transfers between devices, on_device(): lax.ppermute(fetched, 'strip', near_pairs)  1.54 us
    unnamed x35, local copies, waits for them, and re-layouts  1.13 us
  transfers between devices with their start and end apart: 4, of which 2 were waited for; matrix products, arithmetic and copies ran while one was open for 0% of the time, Pallas kernels for 36%

profile of v12, /device:TPU:0, one launch (start us, length us, event | category | flops | bytes accessed | tf_op | source)
XLA Modules:
  0.0 22.5 jit_solution(1731328872018253941)
XLA Ops:
  0.0 1.0 %copy-done = bf16[2,2,77,640]{3,1,2,0:T(2,128)(2,1)S(1)} copy-done((bf16[2,2,77,640]{3,1,2,0:T(2,128)(2,1)S(1)}, bf16[2,2,77,640]{3,1,2,0:T(2,128)(2,1)}, u32[]{:S(2)}) %copy-start) | copy-done | bytes 394264
  1.0 4.1 %collective-permute-start.2 = (bf16[77,2,640]{2,1,0:T(2,128)(2,1)S(1)}, bf16[77,2,640]{2,1,0:T(2,128)(2,1)S(1)}, u32[]{:S(2)}, u32[]{:S(2)}) collective-permute-start(bf16[77,2,640]{2,1,0:T(2,128)(2,1)S(1)} %pages.1), channel_id=1, source_target_pairs={{0,4},{1,5},{2,6},{3,7},{4,0},{5,1},{6,2},{7,3},{8,12},{9,13},{10,... | collective-permute-start | bytes 591368 | tf_op jit(solution)/shard_map/ppermute | solution.py:263
  5.1 0.3 %edge.1 = (bf16[4,16,1280]{2,1,0:T(8,128)(2,1)S(1)}, bf16[4,16,1280]{2,1,0:T(8,128)(2,1)S(1)}) custom-call(bf16[4,4,14,2,640]{4,3,2,1,0:T(2,128)(2,1)S(1)} %bitcast.16, f32[640]{0:T(1024)S(1)} %copy-done.10), custom_call_target="tpu_custom_call" | custom-call | flops 16000000000 | tf_op jit(solution)/shard_map/edge/pallas_call | solution.py:269
  5.5 0.0 copy-start.1
  5.5 0.0 copy-start.2
  5.5 1.6 %collective-permute-start = (bf16[4,16,1280]{2,1,0:T(8,128)(2,1)S(1)}, bf16[4,16,1280]{2,1,0:T(8,128)(2,1)S(1)}, u32[]{:S(2)}, u32[]{:S(2)}) collective-permute-start(bf16[4,16,1280]{2,1,0:T(8,128)(2,1)S(1)} %get-tuple-element.15.edge_act_ref), channel_id=1, source_target_pairs={{0,8},{8,0},{16,24},{24,16},{1,9},{9,1},{17,25},{25,17},{2,10},{10... | collective-permute-start | bytes 491528 | tf_op jit(solution)/shard_map/ppermute | solution.py:278
  7.1 0.6 %activate.1 = (bf16[4,4,16,1280]{3,2,1,0:T(8,128)(2,1)S(1)}, bf16[4,4,16,1280]{3,2,1,0:T(8,128)(2,1)S(1)}, bf16[4,16,1280]{2,1,0:T(8,128)(2,1)S(1)}) custom-call(bf16[4,4,14,2,640]{4,3,2,1,0:T(2,128)(2,1)S(1)} %bitcast.17, f32[640]{0:T(1024)S(1)} %copy-done.10, bf16[4,16,1280]{2,1,0:T(8,128)(2,1)S(1)} %get-tuple-element.14.edge_x_ref, ...), custom_call_target="tpu_custom_call" | custom-call | flops 300000000 | tf_op jit(solution)/shard_map/activate/pallas_call | solution.py:279
  7.7 0.7 %collective-permute-start.1 = (bf16[4,16,1280]{2,1,0:T(8,128)(2,1)S(1)}, bf16[4,16,1280]{2,1,0:T(8,128)(2,1)S(1)}, u32[]{:S(2)}, u32[]{:S(2)}) collective-permute-start(bf16[4,16,1280]{2,1,0:T(8,128)(2,1)S(1)} %get-tuple-element.18), channel_id=1, source_target_pairs={{8,16},{16,8},{9,17},{17,9},{10,18},{18,10},{11,19},{19,11},{12,20... | collective-permute-start | bytes 491528 | tf_op jit(solution)/shard_map/ppermute | solution.py:288
  8.4 2.9 %collective-permute-done.near_ref = bf16[4,16,1280]{2,1,0:T(8,128)(2,1)S(1)} collective-permute-done((bf16[4,16,1280]{2,1,0:T(8,128)(2,1)S(1)}, bf16[4,16,1280]{2,1,0:T(8,128)(2,1)S(1)}, u32[]{:S(2)}, u32[]{:S(2)}) %collective-permute-start) | collective-permute-done | bytes 163872 | tf_op jit(solution)/shard_map/ppermute | solution.py:278
  11.3 0.0 copy-start.3
  11.3 0.0 copy-start.4
  11.3 0.0 copy-start.5
  11.3 0.0 copy-start.6
  11.3 0.0 copy-start.7
  11.3 0.0 copy-start.11
  11.3 0.0 copy-start.12
  11.4 0.0 copy-start.13
  11.4 0.0 copy-start.14
  11.4 2.7 %conv_own.1.part_ref = f32[2,4,4,16,640]{4,3,2,1,0:T(8,128)S(1)} custom-call(bf16[4,4,16,1280]{3,2,1,0:T(8,128)(2,1)S(1)} %get-tuple-element.16.x_ref, bf16[4,4,16,1280]{3,2,1,0:T(8,128)(2,1)S(1)} %get-tuple-element.17.act_ref, bf16[4,16,1280]{2,1,0:T(8,128)(2,1)S(1)} %collective-permute-done.near_ref, bf16[3,3,640,640]{3,2,1,0:T(8,128)(2,1)S(1)} %bitcast.12, ...), custom_call_target="tpu_custom_call" | custom-call | flops 300000000 | tf_op jit(solution)/shard_map/conv_own/pallas_call | solution.py:290
  14.1 0.0 copy-start.8
  14.1 0.2 collective-permute-done.2
  14.3 1.5 %collective-permute-start.3 = (bf16[77,2,640]{2,1,0:T(2,128)(2,1)S(1)}, bf16[77,2,640]{2,1,0:T(2,128)(2,1)S(1)}, u32[]{:S(2)}, u32[]{:S(2)}) collective-permute-start(bf16[77,2,640]{2,1,0:T(2,128)(2,1)S(1)} %collective-permute-done.2), channel_id=1, source_target_pairs={{0,8},{8,0},{16,24},{24,16},{1,9},{9,1},{17,25},{25,17},{2,10},{10... | collective-permute-start | bytes 591368 | tf_op jit(solution)/shard_map/ppermute | solution.py:264
  15.9 4.5 %time_mix.1 = (f32[2,4,4,16,640]{4,3,2,1,0:T(8,128)S(1)}, f32[2,2,4,16,640]{4,3,2,1,0:T(8,128)S(1)}, bf16[2,2,4,16,640]{4,3,2,1,0:T(8,128)(2,1)S(1)}, bf16[2,4,1...) custom-call(s32[16]{0:T(128)S(1)} %copy-done.13, s32[2]{0:T(128)S(1)} %copy-done.14, ...), custom_call_target="tpu_custom_call", output_to_operand_aliasing={{0}: (2, {})} | custom-call | flops 6000000000 | tf_op jit(solution)/shard_map/time_mix/pallas_call | solution.py:300
  20.5 2.0 %cross_mix.1 = bf16[2,4,14,2,640]{4,3,2,1,0:T(2,128)(2,1)} custom-call(bf16[2,4,16,640]{3,2,1,0:T(8,128)(2,1)S(1)} %get-tuple-element.19.choice_ref, f32[2,16,640]{2,1,0:T(8,128)S(1)} %get-tuple-element.20.live_ref, f32[2,2,4,16,640]{4,3,2,1,0:T(8,128)S(1)} %get-tuple-element.21.after_ref, bf16[2,2,4,16,640]{4,3,2,1,0:T(8,128)(2,1)S(1)} %get-tuple-element.22.query_ref, ...), custom_call_target="tpu_custom_call" | custom-call | flops 1000000000 | tf_op jit(solution)/shard_map/cross_mix/pallas_call | solution.py:322
  (28 shorter events, 0.2 us)
Async XLA Ops:
  0.0 1.0 %copy-start = (bf16[2,2,77,640]{3,1,2,0:T(2,128)(2,1)S(1)}, bf16[2,2,77,640]{3,1,2,0:T(2,128)(2,1)}, u32[]{:S(2)}) copy-start(bf16[2,2,77,640]{3,1,2,0:T(2,128)(2,1)} %param.18) | copy-start | bytes 1182724
  1.0 4.1 %copy-start.9 = (bf16[2,2,4,2,14,640]{5,3,4,2,1,0:T(2,128)(2,1)S(1)}, bf16[2,2,4,2,14,640]{5,3,4,2,1,0:T(2,128)(2,1)}, u32[]{:S(2)}) copy-start(bf16[2,2,4,2,14,640]{5,3,4,2,1,0:T(2,128)(2,1)} %param.15) | copy-start | bytes 1720324
  1.0 4.1 %copy-start.10 = (f32[640]{0:T(1024)S(1)}, f32[640]{0:T(1024)}, u32[]{:S(2)}) copy-start(f32[640]{0:T(1024)} %gain_ref.3) | copy-start | bytes 7684
  1.0 13.2 %collective-permute-start.2 = (bf16[77,2,640]{2,1,0:T(2,128)(2,1)S(1)}, bf16[77,2,640]{2,1,0:T(2,128)(2,1)S(1)}, u32[]{:S(2)}, u32[]{:S(2)}) collective-permute-start(bf16[77,2,640]{2,1,0:T(2,128)(2,1)S(1)} %pages.1), channel_id=1, source_target_pairs={{0,4},{1,5},{2,6},{3,7},{4,0},{5,1},{6,2},{7,3},{8,12},{9,13},{10,... | collective-permute-start | bytes 591368 | tf_op jit(solution)/shard_map/ppermute | solution.py:263
  5.1 6.1 %slice-start = ((s8[7372800]{0:T(1024)(128)(4,1)}), s8[4194304]{0:T(1024)(128)(4,1)S(1)}, s32[]{:S(2)}) async-start(s8[7372800]{0:T(1024)(128)(4,1)} %bitcast.11), calls=%async_computation | async-start | bytes 8388608
  5.1 6.1 %slice-start.1 = ((s8[7372800]{0:T(1024)(128)(4,1)}), s8[3178496]{0:T(1024)(128)(4,1)S(1)}, s32[]{:S(2)}) async-start(s8[7372800]{0:T(1024)(128)(4,1)} %bitcast.11), calls=%async_computation.1 | async-start | bytes 6356992
  5.5 2.8 %copy-start.1 = (bf16[2,2,77,640]{3,1,2,0:T(2,128)(2,1)S(1)}, bf16[2,2,77,640]{3,1,2,0:T(2,128)(2,1)}, u32[]{:S(2)}) copy-start(bf16[2,2,77,640]{3,1,2,0:T(2,128)(2,1)} %param.18) | copy-start | bytes 1182724
  5.5 5.7 %copy-start.2 = (f32[640]{0:T(1024)S(1)}, f32[640]{0:T(1024)}, u32[]{:S(2)}) copy-start(f32[640]{0:T(1024)} %bias_ref.1) | copy-start | bytes 7684
  5.5 5.7 %collective-permute-start = (bf16[4,16,1280]{2,1,0:T(8,128)(2,1)S(1)}, bf16[4,16,1280]{2,1,0:T(8,128)(2,1)S(1)}, u32[]{:S(2)}, u32[]{:S(2)}) collective-permute-start(bf16[4,16,1280]{2,1,0:T(8,128)(2,1)S(1)} %get-tuple-element.15.edge_act_ref), channel_id=1, source_target_pairs={{0,8},{8,0},{16,24},{24,16},{1,9},{9,1},{17,25},{25,17},{2,10},{10... | collective-permute-start | bytes 491528 | tf_op jit(solution)/shard_map/ppermute | solution.py:278
  7.7 8.2 %collective-permute-start.1 = (bf16[4,16,1280]{2,1,0:T(8,128)(2,1)S(1)}, bf16[4,16,1280]{2,1,0:T(8,128)(2,1)S(1)}, u32[]{:S(2)}, u32[]{:S(2)}) collective-permute-start(bf16[4,16,1280]{2,1,0:T(8,128)(2,1)S(1)} %get-tuple-element.18), channel_id=1, source_target_pairs={{8,16},{16,8},{9,17},{17,9},{10,18},{18,10},{11,19},{19,11},{12,20... | collective-permute-start | bytes 491528 | tf_op jit(solution)/shard_map/ppermute | solution.py:288
  11.3 4.5 %copy-start.3 = (bf16[640,640]{1,0:T(8,128)(2,1)S(1)}, bf16[640,640]{1,0:T(8,128)(2,1)}, u32[]{:S(2)}) copy-start(bf16[640,640]{1,0:T(8,128)(2,1)} %wq_ref.1) | copy-start | bytes 2457604
  11.3 4.5 %copy-start.4 = (bf16[640,640]{1,0:T(8,128)(2,1)S(1)}, bf16[640,640]{1,0:T(8,128)(2,1)}, u32[]{:S(2)}) copy-start(bf16[640,640]{1,0:T(8,128)(2,1)} %wk_ref.1) | copy-start | bytes 2457604
  11.3 4.5 %copy-start.5 = (bf16[640,640]{1,0:T(8,128)(2,1)S(1)}, bf16[640,640]{1,0:T(8,128)(2,1)}, u32[]{:S(2)}) copy-start(bf16[640,640]{1,0:T(8,128)(2,1)} %wv_ref.1) | copy-start | bytes 2457604
  11.3 4.5 %copy-start.6 = (bf16[640,640]{1,0:T(8,128)(2,1)S(1)}, bf16[640,640]{1,0:T(8,128)(2,1)}, u32[]{:S(2)}) copy-start(bf16[640,640]{1,0:T(8,128)(2,1)} %wo_ref.1) | copy-start | bytes 2457604
  11.3 4.5 %copy-start.7 = (bf16[640,640]{1,0:T(8,128)(2,1)S(1)}, bf16[640,640]{1,0:T(8,128)(2,1)}, u32[]{:S(2)}) copy-start(bf16[640,640]{1,0:T(8,128)(2,1)} %xq_ref.1) | copy-start | bytes 2457604
  11.3 4.5 %copy-start.11 = (f32[640]{0:T(1024)S(1)}, f32[640]{0:T(1024)}, u32[]{:S(2)}) copy-start(f32[640]{0:T(1024)} %tgain_ref.1) | copy-start | bytes 7684
  11.3 4.5 %copy-start.12 = (f32[640]{0:T(1024)S(1)}, f32[640]{0:T(1024)}, u32[]{:S(2)}) copy-start(f32[640]{0:T(1024)} %xgain_ref.1) | copy-start | bytes 7684
  11.4 4.5 %copy-start.13 = (s32[16]{0:T(128)S(1)}, s32[16]{0:T(128)}, u32[]{:S(2)}) copy-start(s32[16]{0:T(128)} %slot_ref.1) | copy-start | bytes 196
  11.4 4.5 %copy-start.14 = (s32[2]{0:T(128)S(1)}, s32[2]{0:T(128)}, u32[]{:S(2)}) copy-start(s32[2]{0:T(128)} %gate_ref.1) | copy-start | bytes 28
  14.1 6.4 %copy-start.8 = (bf16[640,640]{1,0:T(8,128)(2,1)S(1)}, bf16[640,640]{1,0:T(8,128)(2,1)}, u32[]{:S(2)}) copy-start(bf16[640,640]{1,0:T(8,128)(2,1)} %xo_ref.1) | copy-start | bytes 2457604
  14.3 6.2 %collective-permute-start.3 = (bf16[77,2,640]{2,1,0:T(2,128)(2,1)S(1)}, bf16[77,2,640]{2,1,0:T(2,128)(2,1)S(1)}, u32[]{:S(2)}, u32[]{:S(2)}) collective-permute-start(bf16[77,2,640]{2,1,0:T(2,128)(2,1)S(1)} %collective-permute-done.2), channel_id=1, source_target_pairs={{0,8},{8,0},{16,24},{24,16},{1,9},{9,1},{17,25},{25,17},{2,10},{10... | collective-permute-start | bytes 591368 | tf_op jit(solution)/shard_map/ppermute | solution.py:264
